TPU v7x, 256 devices: a whole 4x4x8 slice. The times are simulated.
256 devices in a mesh: ctx: 32 (over z_hi, y, core), ch: 8 (over x, z_lo).
Axes of the slice: x: 4, y: 4, z: 8 (z_hi: 4, z_lo: 2; z = z_hi * 2 + z_lo), core: 2. Of those that a mesh axis runs over, the one named last changes fastest.
Arguments:
- inputs: float32 [24576, 2048], P('ctx', 'ch'), may hold values from -6 to 6
- cotangent: float32 [24576, 2048], P('ctx', 'ch'), may hold values from -6 to 6
- filter_rows: float32 [1536, 2048], P('ctx', 'ch'), may hold values from -0.15625 to 0.15625
- skip_gain: float32 [2048], P('ch'), may hold values from -1 to 1
- band_blocks: int32 [2048], P('ch'), may hold values from 1 to 2
Outputs:
- outputs: float32 [24576, 2048], P('ctx', 'ch')
- input_grad: float32 [2048, 24576], P(('ch', 'ctx'))
All inputs are finite; a program needn't handle non-finite values.
Results may differ from a plain program's by a relative error of at most 0.00007.
Values sent between devices are 32-bit elements; how exact they have to be, the bound alone decides.
No kernel may reach another device: no remote copies, remote signals or barrier semaphores. Data moves between devices by JAX's collectives and lax.ppermute only.
A program may use at most 128 MiB of HBM per device.

v0:
```python
import jax
import jax.numpy as jnp
from jax import lax
from jax.experimental import pallas as pl
from jax.experimental.pallas import tpu as pltpu
from jax.sharding import PartitionSpec as P

LANES = 128
SUBS = 8


def tap_tile(taps_ref, gain_ref, band_ref, block_len):
    rows, chans = taps_ref.shape
    lag = lax.axis_index("ctx") * rows + lax.broadcasted_iota(jnp.int32, (rows, chans), 0)
    kept = jnp.where(lag < band_ref[...] * block_len, taps_ref[...], 0.0)
    kept = kept + jnp.where(lag == 0, gain_ref[...], 0.0)
    return jnp.concatenate([kept, jnp.zeros((LANES - rows, chans), jnp.float32)], axis=0).T


def pack_with_taps(x_ref, taps_ref, gain_ref, band_ref, out_ref):
    tiles = x_ref.shape[0] // LANES
    for k in range(tiles):
        part = x_ref[k * LANES:(k + 1) * LANES, :].T
        out_ref[:, k, :, :] = part.reshape(-1, SUBS, LANES)
    part = tap_tile(taps_ref, gain_ref, band_ref, x_ref.shape[0])
    out_ref[:, tiles, :, :] = part.reshape(-1, SUBS, LANES)


def pack_plain(x_ref, out_ref):
    for k in range(x_ref.shape[0] // LANES):
        part = x_ref[k * LANES:(k + 1) * LANES, :].T
        out_ref[:, k, :, :] = part.reshape(-1, SUBS, LANES)


def unpack(y_ref, out_ref):
    for k in range(out_ref.shape[0] // LANES):
        part = y_ref[:, k, :, :].reshape(-1, LANES)
        out_ref[k * LANES:(k + 1) * LANES, :] = part.T


def split(value):
    high = value.astype(jnp.bfloat16)
    return high, (value - high.astype(jnp.float32)).astype(jnp.bfloat16)


def lay_taps(read_piece, pieces, rows, lag_tiles, row_ref):
    lane = lax.broadcasted_iota(jnp.int32, (SUBS, LANES), 1)
    held = [jnp.zeros((SUBS, LANES), jnp.float32) for _ in range(lag_tiles + 2)]
    for piece in range(pieces):
        tile, offset = divmod(LANES + rows * piece, LANES)
        value = read_piece(piece)
        turned = pltpu.roll(value, offset, axis=1) if offset else value
        if offset + rows <= LANES:
            held[tile] = held[tile] + turned
        else:
            held[tile] = held[tile] + jnp.where(lane >= offset, turned, 0.0)
            held[tile + 1] = held[tile + 1] + jnp.where(lane < offset, turned, 0.0)
    for tile in range(lag_tiles + 2):
        row_ref[:, tile * LANES:(tile + 1) * LANES] = held[tile]


def toeplitz(row_ref, chan):
    row = row_ref[pl.ds(chan, 1), :]
    wide = jnp.broadcast_to(row, (LANES, row.shape[1]))
    return pltpu.roll(wide, 0, axis=1, stride=1, stride_axis=0)[:, LANES:]


def shifted(value, steps):
    if steps == 0:
        return value
    blank = jnp.zeros((abs(steps), value.shape[1]), value.dtype)
    if steps > 0:
        return jnp.concatenate([blank, value[:-steps]], axis=0)
    return jnp.concatenate([value[-steps:], blank], axis=0)


def convolve(signal_ref, signal_tiles, taps_ref, taps_tiles, put, row_ref, blocks, tiles, rows, lag_tiles, backward):
    chunk = signal_tiles * SUBS
    tap_chunk = taps_tiles * SUBS

    def read_piece(piece):
        base = piece * tap_chunk + (taps_tiles - 1) * SUBS
        return taps_ref[base:base + SUBS, :]

    lay_taps(read_piece, blocks, rows, lag_tiles, row_ref)
    depth = lag_tiles + 1
    sign = -1 if backward else 1

    def one(chan, carry):
        high_t, low_t = split(toeplitz(row_ref, chan))
        moved = {}
        for k in range(tiles):
            value = signal_ref[pl.ds(k * SUBS + chan, blocks, stride=chunk), :]
            for steps in range(3):
                high, low = split(shifted(value, sign * steps))
                moved[k, steps] = jnp.concatenate([high, low], axis=0)
        columns = []
        for d in range(depth):
            parts = []
            for k in range(tiles):
                turns, at = divmod(k - sign * d, tiles)
                parts.append(moved[at, abs(turns)])
            columns.append(jnp.concatenate(parts, axis=0))
        left = jnp.concatenate(columns, axis=1)
        if backward:
            right = jnp.concatenate([high_t, low_t], axis=0)
            total = lax.dot_general(left, right, (((1,), (1,)), ((), ())), preferred_element_type=jnp.float32)
        else:
            right = jnp.concatenate(
                [jnp.concatenate([t[:, d * LANES:(d + 1) * LANES] for t in (high_t, low_t)], axis=1) for d in range(depth)],
                axis=0,
            )
            total = jnp.dot(left, right, preferred_element_type=jnp.float32)
        total = total[:, :LANES] + total[:, LANES:]
        for k in range(tiles):
            base = 2 * blocks * k
            put(k, chan, total[base:base + blocks] + total[base + blocks:base + 2 * blocks])
        return carry

    lax.fori_loop(0, SUBS, one, 0)


def forward(blocks, tiles, rows, lag_tiles, x_ref, y_ref, row_ref):
    def put(k, chan, value):
        y_ref[pl.ds(k * SUBS + chan, blocks, stride=tiles * SUBS), :] = value

    convolve(x_ref, tiles + 1, x_ref, tiles + 1, put, row_ref, blocks, tiles, rows, lag_tiles, False)


def gradient(blocks, tiles, rows, lag_tiles, g_ref, x_ref, out_ref, row_ref, held_ref):
    def put(k, chan, value):
        held_ref[pl.ds(k * SUBS + chan, blocks, stride=tiles * SUBS), :] = value

    convolve(g_ref, tiles, x_ref, tiles + 1, put, row_ref, blocks, tiles, rows, lag_tiles, True)
    for tile in range(blocks * tiles):
        out_ref[:, tile * LANES:(tile + 1) * LANES] = held_ref[tile * SUBS:(tile + 1) * SUBS, :]


def call(body, shape, scratch=(), flops=0, moved=0):
    return pl.pallas_call(
        body,
        out_shape=jax.ShapeDtypeStruct(shape, jnp.float32),
        scratch_shapes=list(scratch),
        compiler_params=pltpu.CompilerParams(vmem_limit_bytes=40 * 1024 * 1024),
        cost_estimate=pl.CostEstimate(flops=flops, bytes_accessed=moved, transcendentals=0),
    )


def local(inputs, cotangent, filter_rows, skip_gain, band_blocks):
    count = lax.axis_size("ctx")
    block_len, chans = inputs.shape
    rows = filter_rows.shape[0]
    tiles = block_len // LANES
    lag_tiles = rows * count // LANES
    size = block_len * chans * 4

    def exchanged(value):
        return lax.all_to_all(value, "ctx", split_axis=0, concat_axis=0, tiled=True)

    sent_x = call(pack_with_taps, (count, tiles + 1, SUBS, LANES), moved=2 * size)(
        inputs, filter_rows, skip_gain[None, :], band_blocks[None, :])
    got_x = exchanged(sent_x).reshape(-1, LANES)
    sent_g = call(pack_plain, (count, tiles, SUBS, LANES), moved=2 * size)(cotangent)
    got_g = exchanged(sent_g).reshape(-1, LANES)
    row = pltpu.VMEM((SUBS, (lag_tiles + 2) * LANES), jnp.float32)
    flops = 2 * SUBS * 2 * count * tiles * (lag_tiles + 1) * LANES * 2 * LANES
    sizes = (count, tiles, rows, lag_tiles)
    sent_y = call(lambda *refs: forward(*sizes, *refs), (count * tiles * SUBS, LANES), [row], flops, 2 * size)(got_x)
    got_y = exchanged(sent_y.reshape(count, tiles, SUBS, LANES))
    held = pltpu.VMEM((count * tiles * SUBS, LANES), jnp.float32)
    input_grad = call(lambda *refs: gradient(*sizes, *refs), (SUBS, count * block_len), [row, held], flops, 3 * size)(
        got_g, got_x)
    outputs = call(unpack, (block_len, chans), moved=2 * size)(got_y)
    return outputs, input_grad


def solution(mesh):
    return jax.shard_map(
        local,
        mesh=mesh,
        in_specs=(P("ctx", "ch"), P("ctx", "ch"), P("ctx", "ch"), P("ch"), P("ch")),
        out_specs=(P("ctx", "ch"), P(("ch", "ctx"), None)),
        check_vma=False,
    )
```

profile of v0, /device:TPU:1, one launch (start us, length us, event | category | flops | bytes accessed | tf_op | source)
XLA Modules:
  0.0 101.6 jit_solution(13074287640246144971)
XLA Ops:
  0.6 0.0 copy-start.4
  0.6 0.0 copy-start.3
  0.7 0.7 copy-done.4
  1.3 0.0 copy-done.3
  1.3 0.0 copy-start
  1.3 1.1 %copy-done = f32[768,256]{1,0:T(8,128)S(1)} copy-done((f32[768,256]{1,0:T(8,128)S(1)}, f32[768,256]{1,0:T(8,128)}, u32[]{:S(2)}) %copy-start) | copy-done | bytes 786456
  2.5 0.0 copy-start.2
  2.5 0.8 copy-done.2
  3.3 1.2 %shard_map.68 = f32[32,7,8,128]{3,2,1,0:T(8,128)} custom-call(f32[768,256]{1,0:T(8,128)S(1)} %copy-done, f32[48,256]{1,0:T(8,128)S(1)} %copy-done.2, f32[1,256]{1,0:T(1,128)S(1)} %bitcast.8, s32[1,256]{1,0:T(1,128)S(1)} %bitcast.9), custom_call_target="tpu_custom_call" | custom-call | bytes 1572864 | tf_op jit(solution)/shard_map/pallas_call | solution.py:160
  4.5 0.0 copy-start.1
  4.5 12.9 %all-to-all-start = ((f32[32,7,8,128]{3,2,1,0:T(8,128)}), f32[32,7,8,128]{3,2,1,0:T(8,128)S(1)}, u32[]{:S(2)}, u32[]{:S(2)}) async-start(f32[32,7,8,128]{3,2,1,0:T(8,128)} %shard_map.68), calls=%async_computation | async-start | bytes 1835008 | tf_op jit(solution)/shard_map/all_to_all | solution.py:158
  17.4 0.0 copy-done.1
  17.4 1.1 %shard_map.71 = f32[32,6,8,128]{3,2,1,0:T(8,128)} custom-call(f32[768,256]{1,0:T(8,128)S(1)} %copy-done.1), custom_call_target="tpu_custom_call" | custom-call | bytes 1572864 | tf_op jit(solution)/shard_map/pallas_call | solution.py:163
  18.5 23.8 %all-to-all-done = f32[32,7,8,128]{3,2,1,0:T(8,128)S(1)} async-done(((f32[32,7,8,128]{3,2,1,0:T(8,128)}), f32[32,7,8,128]{3,2,1,0:T(8,128)S(1)}, u32[]{:S(2)}, u32[]{:S(2)}) %all-to-all-start) | async-done | bytes 917536 | tf_op jit(solution)/shard_map/all_to_all | solution.py:158
  42.3 6.4 %all-to-all-start.2 = ((f32[32,6,8,128]{3,2,1,0:T(8,128)}), f32[32,6,8,128]{3,2,1,0:T(8,128)S(1)}, u32[]{:S(2)}, u32[]{:S(2)}) async-start(f32[32,6,8,128]{3,2,1,0:T(8,128)} %shard_map.71), calls=%async_computation.2 | async-start | bytes 1572864 | tf_op jit(solution)/shard_map/all_to_all | solution.py:158
  48.8 6.5 %shard_map.69 = f32[1536,128]{1,0:T(8,128)} custom-call(f32[1792,128]{1,0:T(8,128)S(1)} %bitcast.5), custom_call_target="tpu_custom_call" | custom-call | flops 2617245696 | bytes 1572864 | tf_op jit(solution)/shard_map/pallas_call | solution.py:168
  55.2 16.7 %all-to-all-done.2 = f32[32,6,8,128]{3,2,1,0:T(8,128)S(1)} async-done(((f32[32,6,8,128]{3,2,1,0:T(8,128)}), f32[32,6,8,128]{3,2,1,0:T(8,128)S(1)}, u32[]{:S(2)}, u32[]{:S(2)}) %all-to-all-start.2) | async-done | bytes 786464 | tf_op jit(solution)/shard_map/all_to_all | solution.py:158
  72.0 5.5 %all-to-all-start.1 = ((f32[32,6,8,128]{3,2,1,0:T(8,128)}), f32[32,6,8,128]{3,2,1,0:T(8,128)S(1)}, u32[]{:S(2)}, u32[]{:S(2)}) async-start(f32[32,6,8,128]{3,2,1,0:T(8,128)} %bitcast.3), calls=%async_computation.1 | async-start | bytes 1572864 | tf_op jit(solution)/shard_map/all_to_all | solution.py:158
  77.4 6.8 %shard_map.72 = f32[8,24576]{1,0:T(8,128)} custom-call(f32[1536,128]{1,0:T(8,128)S(1)} %bitcast.7, f32[1792,128]{1,0:T(8,128)S(1)} %bitcast.6), custom_call_target="tpu_custom_call" | custom-call | flops 2617245696 | bytes 2359296 | tf_op jit(solution)/shard_map/pallas_call | solution.py:171
  84.2 16.2 %all-to-all-done.1.y_ref = f32[32,6,8,128]{3,2,1,0:T(8,128)S(1)} async-done(((f32[32,6,8,128]{3,2,1,0:T(8,128)}), f32[32,6,8,128]{3,2,1,0:T(8,128)S(1)}, u32[]{:S(2)}, u32[]{:S(2)}) %all-to-all-start.1) | async-done | bytes 786464 | tf_op jit(solution)/shard_map/all_to_all | solution.py:158
  100.4 1.1 %shard_map.70 = f32[768,256]{1,0:T(8,128)} custom-call(f32[32,6,8,128]{3,2,1,0:T(8,128)S(1)} %all-to-all-done.1.y_ref), custom_call_target="tpu_custom_call" | custom-call | bytes 1572864 | tf_op jit(solution)/shard_map/pallas_call | solution.py:173
Async XLA Ops:
  0.6 0.7 copy-start.4
  0.6 0.7 copy-start.3
  1.3 1.1 %copy-start = (f32[768,256]{1,0:T(8,128)S(1)}, f32[768,256]{1,0:T(8,128)}, u32[]{:S(2)}) copy-start(f32[768,256]{1,0:T(8,128)} %x_ref.2) | copy-start | bytes 2359300
  2.5 0.8 copy-start.2
  4.5 12.9 %copy-start.1 = (f32[768,256]{1,0:T(8,128)S(1)}, f32[768,256]{1,0:T(8,128)}, u32[]{:S(2)}) copy-start(f32[768,256]{1,0:T(8,128)} %x_ref.3) | copy-start | bytes 2359300
  4.5 37.8 %all-to-all-start = ((f32[32,7,8,128]{3,2,1,0:T(8,128)}), f32[32,7,8,128]{3,2,1,0:T(8,128)S(1)}, u32[]{:S(2)}, u32[]{:S(2)}) async-start(f32[32,7,8,128]{3,2,1,0:T(8,128)} %shard_map.68), calls=%async_computation | async-start | bytes 1835008 | tf_op jit(solution)/shard_map/all_to_all | solution.py:158
  42.3 29.6 %all-to-all-start.2 = ((f32[32,6,8,128]{3,2,1,0:T(8,128)}), f32[32,6,8,128]{3,2,1,0:T(8,128)S(1)}, u32[]{:S(2)}, u32[]{:S(2)}) async-start(f32[32,6,8,128]{3,2,1,0:T(8,128)} %shard_map.71), calls=%async_computation.2 | async-start | bytes 1572864 | tf_op jit(solution)/shard_map/all_to_all | solution.py:158
  72.0 28.5 %all-to-all-start.1 = ((f32[32,6,8,128]{3,2,1,0:T(8,128)}), f32[32,6,8,128]{3,2,1,0:T(8,128)S(1)}, u32[]{:S(2)}, u32[]{:S(2)}) async-start(f32[32,6,8,128]{3,2,1,0:T(8,128)} %bitcast.3), calls=%async_computation.1 | async-start | bytes 1572864 | tf_op jit(solution)/shard_map/all_to_all | solution.py:158
where the time goes:
time: 102 us
  waiting for transfers between devices  56.7 us (56%)
  starting transfers between devices  24.8 us (24%)
  Pallas kernels  16.8 us (16%)
  local copies, waits for them, and re-layouts  2.61 us (3%)
    all_to_all x3, waiting for transfers between devices, exchanged(): return lax.all_to_all(value, 'ctx', split_axis=0, concat_axis=0, tiled=True)  56.7 us
    all_to_all x3, starting transfers between devices, exchanged(): return lax.all_to_all(value, 'ctx', split_axis=0, concat_axis=0, tiled=True)  24.8 us
    pallas_call x1, Pallas kernels, local(): call(lambda *refs: gradient(*sizes, *refs), (SUBS, count * block_len), [r...  6.78 us
    pallas_call x1, Pallas kernels, local(): call(lambda *refs: forward(*sizes, *refs), (count * tiles * SUBS, LANES),...  6.47 us
    unnamed x10, local copies, waits for them, and re-layouts  2.61 us
  transfers between devices with their start and end apart: 3, of which 3 were waited for; matrix products, arithmetic and copies ran while one was open for 0% of the time, Pallas kernels for 14%

commit v1 on v0

v1 whole, which is shorter than its diff:
```python
import jax
import jax.numpy as jnp
from jax import lax
from jax.experimental import pallas as pl
from jax.experimental.pallas import tpu as pltpu
from jax.sharding import Mesh, PartitionSpec as P

LANES = 128
SUBS = 8
NEAR = 8


def store_parts(out_ref, k, part):
    far = out_ref.shape[1]
    step = part.shape[0] // far
    for z in range(far):
        out_ref[:, z, k, :, :] = part[z * step:(z + 1) * step].reshape(-1, SUBS, LANES)


def pack_with_taps(x_ref, taps_ref, gain_ref, band_ref, out_ref):
    block_len = x_ref.shape[0]
    tiles = block_len // LANES
    for k in range(tiles):
        store_parts(out_ref, k, x_ref[k * LANES:(k + 1) * LANES, :].T)
    rows, chans = taps_ref.shape
    place = lax.axis_index("far") * NEAR + lax.axis_index("near")
    lag = place * rows + lax.broadcasted_iota(jnp.int32, (rows, chans), 0)
    kept = jnp.where(lag < band_ref[...] * block_len, taps_ref[...], 0.0)
    kept = kept + jnp.where(lag == 0, gain_ref[...], 0.0)
    kept = jnp.concatenate([kept, jnp.zeros((LANES - rows, chans), jnp.float32)], axis=0)
    store_parts(out_ref, tiles, kept.T)


def pack_plain(x_ref, out_ref):
    for k in range(x_ref.shape[0] // LANES):
        part = x_ref[k * LANES:(k + 1) * LANES, :].T
        out_ref[:, k, :, :] = part.reshape(-1, SUBS, LANES)


def unpack(y_ref, out_ref):
    for k in range(out_ref.shape[0] // LANES):
        part = jnp.concatenate([y_ref[:, z, k, :, :].reshape(-1, LANES) for z in range(y_ref.shape[1])], axis=0)
        out_ref[k * LANES:(k + 1) * LANES, :] = part.T


def split(value):
    high = value.astype(jnp.bfloat16)
    return high, (value - high.astype(jnp.float32)).astype(jnp.bfloat16)


def collect(rows, halo_blocks, x_ref, halo_ref, taps_ref):
    near, far, tiles = x_ref.shape[:3]
    tiles = tiles - 1
    lane = lax.broadcasted_iota(jnp.int32, (far * SUBS, LANES), 1)
    own_tiles = rows * near // LANES
    held = [jnp.zeros((far * SUBS, LANES), jnp.float32) for _ in range(own_tiles)]
    for piece in range(near):
        tile, offset = divmod(rows * piece, LANES)
        value = x_ref[piece, :, tiles, :, :].reshape(far * SUBS, LANES)
        turned = pltpu.roll(value, offset, axis=1) if offset else value
        if offset + rows <= LANES:
            held[tile] = held[tile] + turned
        else:
            held[tile] = held[tile] + jnp.where(lane >= offset, turned, 0.0)
            held[tile + 1] = held[tile + 1] + jnp.where(lane < offset, turned, 0.0)
    height = far * SUBS
    halo_rows = halo_blocks * far * tiles * SUBS
    for tile in range(own_tiles):
        taps_ref[tile * height:(tile + 1) * height, :] = held[tile]
        halo_ref[halo_rows + tile * height:halo_rows + (tile + 1) * height, :] = held[tile]
    for block in range(halo_blocks):
        for z in range(far):
            base = (block * far + z) * tiles * SUBS
            halo_ref[base:base + tiles * SUBS, :] = x_ref[near - halo_blocks + block, z, :tiles, :, :].reshape(-1, LANES)


def toeplitz(row):
    wide = jnp.broadcast_to(row, (LANES, row.shape[1]))
    return pltpu.roll(wide, 0, axis=1, stride=1, stride_axis=0)[:, LANES:]


def shifted(value, steps):
    if steps == 0:
        return value
    blank = jnp.zeros((steps, value.shape[1]), value.dtype)
    return jnp.concatenate([value[steps:], blank], axis=0)


def lay_rows(row_ref, pieces, count, height, rows_of):
    per = (row_ref.shape[0] - 2) // count
    row_ref[0] = jnp.zeros(row_ref.shape[1:], jnp.float32)
    row_ref[row_ref.shape[0] - 1] = jnp.zeros(row_ref.shape[1:], jnp.float32)
    me = lax.axis_index("far")
    for back, (ref, base) in enumerate(pieces):
        source = lax.rem(me + count - back, count)
        for tile in range(per):
            row_ref[1 + source * per + tile] = rows_of(ref, base + tile * height)


def row_of(row_ref, chan):
    return jnp.concatenate([row_ref[t, pl.ds(chan, 1), :] for t in range(row_ref.shape[0])], axis=1)


def forward(halo_blocks, tiles, x_ref, halo_ref, *refs):
    others, (y_ref, row_ref, held_ref) = refs[:-3], refs[-3:]
    far = len(others) + 1
    chans = far * SUBS
    near = y_ref.shape[0] // (far * tiles * SUBS)
    chunk = far * (tiles + 1) * SUBS
    halo_rows = halo_blocks * far * tiles * SUBS
    pieces = [(others[0], 0), (halo_ref, halo_rows)] + [(ref, 0) for ref in others[1:]]
    lay_rows(row_ref, pieces, far, chans, lambda ref, base: ref[base:base + chans, :])
    first = lax.axis_index("far") == 0
    for block in range(halo_blocks):
        for z in range(far):
            source = (block * far + z) * tiles * SUBS
            target = block * chunk + z * (tiles + 1) * SUBS
            value = halo_ref[source:source + tiles * SUBS, :]
            held_ref[target:target + tiles * SUBS, :] = jnp.where(first, 0.0, value)
    held_ref[halo_blocks * chunk:, :] = x_ref[...]
    depth = row_ref.shape[0] - 1

    def one(chan, carry):
        z, i = lax.div(chan, SUBS), lax.rem(chan, SUBS)
        high_t, low_t = split(toeplitz(row_of(row_ref, chan)))
        moved = {}
        for k in range(tiles):
            for steps in range(halo_blocks + 1):
                start = (halo_blocks - steps) * chunk + z * (tiles + 1) * SUBS + k * SUBS + i
                moved[k, steps] = jnp.concatenate(split(held_ref[pl.ds(start, near, stride=chunk), :]), axis=0)
        columns = []
        for d in range(depth):
            parts = []
            for k in range(tiles):
                turns, at = divmod(k - d, tiles)
                parts.append(moved[at, -turns])
            columns.append(jnp.concatenate(parts, axis=0))
        left = jnp.concatenate(columns, axis=1)
        right = jnp.concatenate(
            [jnp.concatenate([t[:, d * LANES:(d + 1) * LANES] for t in (high_t, low_t)], axis=1) for d in range(depth)],
            axis=0,
        )
        total = jnp.dot(left, right, preferred_element_type=jnp.float32)
        total = total[:, :LANES] + total[:, LANES:]
        for k in range(tiles):
            base = 2 * near * k
            value = total[base:base + near] + total[base + near:base + 2 * near]
            y_ref[pl.ds((z * tiles + k) * SUBS + i, near, stride=far * tiles * SUBS), :] = value
        return carry

    lax.fori_loop(0, chans, one, 0)


def gradient(blocks, tiles, halo_rows, g_ref, halo_ref, *refs):
    others, (out_ref, row_ref, held_ref) = refs[:-3], refs[-3:]
    far = len(others) + 1
    me = lax.axis_index("far")
    pieces = [(others[0], 0), (halo_ref, halo_rows)] + [(ref, 0) for ref in others[1:]]
    lay_rows(row_ref, pieces, far, far * SUBS,
             lambda ref, base: ref[pl.ds(pl.multiple_of(base + me * SUBS, SUBS), SUBS), :])
    depth = row_ref.shape[0] - 1
    chunk = tiles * SUBS

    def one(chan, carry):
        high_t, low_t = split(toeplitz(row_of(row_ref, chan)))
        moved = {}
        for k in range(tiles):
            value = g_ref[pl.ds(k * SUBS + chan, blocks, stride=chunk), :]
            for steps in range((depth + tiles - 2) // tiles + 1):
                moved[k, steps] = jnp.concatenate(split(shifted(value, steps)), axis=0)
        columns = []
        for d in range(depth):
            parts = []
            for k in range(tiles):
                turns, at = divmod(k + d, tiles)
                parts.append(moved[at, turns])
            columns.append(jnp.concatenate(parts, axis=0))
        left = jnp.concatenate(columns, axis=1)
        right = jnp.concatenate([high_t, low_t], axis=0)
        total = lax.dot_general(left, right, (((1,), (1,)), ((), ())), preferred_element_type=jnp.float32)
        total = total[:, :LANES] + total[:, LANES:]
        for k in range(tiles):
            base = 2 * blocks * k
            value = total[base:base + blocks] + total[base + blocks:base + 2 * blocks]
            held_ref[pl.ds(k * SUBS + chan, blocks, stride=chunk), :] = value
        return carry

    lax.fori_loop(0, SUBS, one, 0)
    for tile in range(blocks * tiles):
        out_ref[:, tile * LANES:(tile + 1) * LANES] = held_ref[tile * SUBS:(tile + 1) * SUBS, :]


def call(body, shapes, scratch=(), flops=0, moved=0):
    shapes = [jax.ShapeDtypeStruct(shape, jnp.float32) for shape in shapes]
    return pl.pallas_call(
        body,
        out_shape=shapes if len(shapes) > 1 else shapes[0],
        scratch_shapes=list(scratch),
        compiler_params=pltpu.CompilerParams(vmem_limit_bytes=40 * 1024 * 1024),
        cost_estimate=pl.CostEstimate(flops=flops, bytes_accessed=moved, transcendentals=0),
    )


def local(inputs, cotangent, filter_rows, skip_gain, band_blocks):
    far = lax.axis_size("far")
    near = lax.axis_size("near")
    count = far * near
    block_len, chans = inputs.shape
    rows = filter_rows.shape[0]
    tiles = block_len // LANES
    lag_tiles = rows * count // LANES
    halo_blocks = rows * count // block_len
    size = block_len * chans * 4

    def exchanged(value, axes):
        return lax.all_to_all(value, axes, split_axis=0, concat_axis=0, tiled=True)

    def ahead(value, steps):
        return lax.ppermute(value, "far", [(z, (z + steps) % far) for z in range(far)])

    sent_x = call(pack_with_taps, [(near, far, tiles + 1, SUBS, LANES)], moved=2 * size)(
        inputs, filter_rows, skip_gain[None, :], band_blocks[None, :])
    got_x = exchanged(sent_x, "near")
    halo_rows = halo_blocks * far * tiles * SUBS
    own_taps = lag_tiles // far * far * SUBS
    halo, taps = call(lambda *refs: collect(rows, halo_blocks, *refs),
                      [(halo_rows + own_taps, LANES), (own_taps, LANES)], moved=size)(got_x)
    got_halo = ahead(halo, 1)
    pieces = [taps] + [ahead(taps, steps) for steps in range(2, far)]
    sent_g = call(pack_plain, [(count, tiles, SUBS, LANES)], moved=2 * size)(cotangent)
    got_g = exchanged(sent_g, ("far", "near")).reshape(-1, LANES)

    def row(height):
        return pltpu.VMEM((lag_tiles + 2, height, LANES), jnp.float32)

    got_x = got_x.reshape(-1, LANES)
    held_rows = (near + halo_blocks) * far * (tiles + 1) * SUBS
    flops = 2 * far * SUBS * 2 * near * tiles * (lag_tiles + 1) * LANES * 2 * LANES
    sent_y = call(lambda *refs: forward(halo_blocks, tiles, *refs), [(count * tiles * SUBS, LANES)],
                  [row(far * SUBS), pltpu.VMEM((held_rows, LANES), jnp.float32)], 4 * flops, 2 * size)(
        got_x, got_halo, *pieces)
    got_y = exchanged(sent_y.reshape(near, far, tiles, SUBS, LANES), "near")
    input_grad = call(lambda *refs: gradient(count, tiles, halo_rows, *refs), [(SUBS, count * block_len)],
                      [row(SUBS), pltpu.VMEM((count * tiles * SUBS, LANES), jnp.float32)], flops, 3 * size)(
        got_g, got_halo, *pieces)
    outputs = call(unpack, [(block_len, chans)], moved=2 * size)(got_y)
    return outputs, input_grad


def solution(mesh):
    count, width = mesh.devices.shape
    fine = Mesh(mesh.devices.reshape(count // NEAR, NEAR, width), ("far", "near", "ch"))
    tokens = ("far", "near")
    return jax.shard_map(
        local,
        mesh=fine,
        in_specs=(P(tokens, "ch"), P(tokens, "ch"), P(tokens, "ch"), P("ch"), P("ch")),
        out_specs=(P(tokens, "ch"), P(("ch", "far", "near"), None)),
        check_vma=False,
    )
```

time: 102 us -> 105 us (1.029)
  waiting for transfers between devices: 56.7 us -> 39.3 us
  Pallas kernels: 16.8 us -> 27.2 us
  starting transfers between devices: 24.8 us -> 35.1 us
    all_to_all x3, waiting for transfers between devices: 56.7 us -> 18.2 us  [exchanged(): return lax.all_to_all(value, axes, split_axis=0, concat_axis=0, tiled=True)]
    ppermute x0 -> x3, waiting for transfers between devices: none -> 21.1 us  [ahead(): lax.ppermute(value, 'far', [(z, (z + steps) % far) for z in range(far)])]
    pallas_call x5 -> x6, Pallas kernels: 16.8 us -> 27.2 us  [the longest x1 16.9 us: local(): call(lambda *refs: forward(halo_blocks, tiles, *refs), [(count * tiles *...]
    ppermute x0 -> x3, starting transfers between devices: none -> 8.95 us  [ahead(): lax.ppermute(value, 'far', [(z, (z + steps) % far) for z in range(far)])]
    all_to_all x3, starting transfers between devices: 24.8 us -> 26.2 us  [exchanged(): return lax.all_to_all(value, axes, split_axis=0, concat_axis=0, tiled=True)]
  transfers between devices with their start and end apart: 3 -> 6, of which waited for: 3 -> 3; matrix products, arithmetic and copies ran while one was open for 0% -> 0% of each run, Pallas kernels for 14% -> 24%
where the time goes in v1:
time: 105 us
  waiting for transfers between devices  39.3 us (37%)
  starting transfers between devices  35.1 us (33%)
  Pallas kernels  27.2 us (26%)
  local copies, waits for them, and re-layouts  2.61 us (2%)
    all_to_all x3, starting transfers between devices, exchanged(): return lax.all_to_all(value, axes, split_axis=0, concat_axis=0, tiled=True)  26.2 us
    ppermute x3, waiting for transfers between devices, ahead(): lax.ppermute(value, 'far', [(z, (z + steps) % far) for z in range(far)])  21.1 us
    all_to_all x3, waiting for transfers between devices, exchanged(): return lax.all_to_all(value, axes, split_axis=0, concat_axis=0, tiled=True)  18.2 us
    pallas_call x1, Pallas kernels, local(): call(lambda *refs: forward(halo_blocks, tiles, *refs), [(count * tiles *...  16.9 us
    ppermute x3, starting transfers between devices, ahead(): lax.ppermute(value, 'far', [(z, (z + steps) % far) for z in range(far)])  8.95 us
    pallas_call x1, Pallas kernels, local(): call(lambda *refs: gradient(count, tiles, halo_rows, *refs), [(SUBS, coun...  6.63 us
    unnamed x10, local copies, waits for them, and re-layouts  2.61 us
  transfers between devices with their start and end apart: 6, of which 3 were waited for; matrix products, arithmetic and copies ran while one was open for 0% of the time, Pallas kernels for 24%

profile of v1, /device:TPU:1, one launch (start us, length us, event | category | flops | bytes accessed | tf_op | source)
XLA Modules:
  0.0 104.9 jit_solution(14817909185036356637)
XLA Ops:
  0.6 0.0 copy-start.4
  0.6 0.0 copy-start.3
  0.7 0.7 copy-done.4
  1.3 0.0 copy-done.3
  1.3 0.0 copy-start
  1.3 1.1 %copy-done = f32[768,256]{1,0:T(8,128)S(1)} copy-done((f32[768,256]{1,0:T(8,128)S(1)}, f32[768,256]{1,0:T(8,128)}, u32[]{:S(2)}) %copy-start) | copy-done | bytes 786456
  2.5 0.0 copy-start.2
  2.5 0.8 copy-done.2
  3.3 1.2 %shard_map.68 = f32[8,4,7,8,128]{4,3,2,1,0:T(8,128)} custom-call(f32[768,256]{1,0:T(8,128)S(1)} %copy-done, f32[48,256]{1,0:T(8,128)S(1)} %copy-done.2, f32[1,256]{1,0:T(1,128)S(1)} %bitcast.7, s32[1,256]{1,0:T(1,128)S(1)} %bitcast.8), custom_call_target="tpu_custom_call" | custom-call | bytes 1572864 | tf_op jit(solution)/shard_map/pallas_call | solution.py:221
  4.5 0.0 copy-start.1
  4.5 6.8 %all-to-all-start = ((f32[8,4,7,8,128]{4,3,2,1,0:T(8,128)}), f32[8,4,7,8,128]{4,3,2,1,0:T(8,128)S(1)}, u32[]{:S(2)}, u32[]{:S(2)}) async-start(f32[8,4,7,8,128]{4,3,2,1,0:T(8,128)} %shard_map.68), calls=%async_computation | async-start | bytes 1835008 | tf_op jit(solution)/shard_map/all_to_all | solution.py:216
  11.3 0.0 copy-done.1
  11.3 1.1 %shard_map.72 = f32[32,6,8,128]{3,2,1,0:T(8,128)} custom-call(f32[768,256]{1,0:T(8,128)S(1)} %copy-done.1), custom_call_target="tpu_custom_call" | custom-call | bytes 1572864 | tf_op jit(solution)/shard_map/pallas_call | solution.py:230
  12.5 12.6 %all-to-all-done.refs_0_ = f32[8,4,7,8,128]{4,3,2,1,0:T(8,128)S(1)} async-done(((f32[8,4,7,8,128]{4,3,2,1,0:T(8,128)}), f32[8,4,7,8,128]{4,3,2,1,0:T(8,128)S(1)}, u32[]{:S(2)}, u32[]{:S(2)}) %all-to-all-start) | async-done | bytes 917536 | tf_op jit(solution)/shard_map/all_to_all | solution.py:216
  25.0 9.4 %all-to-all-start.2 = ((f32[32,6,8,128]{3,2,1,0:T(8,128)}), f32[32,6,8,128]{3,2,1,0:T(8,128)S(1)}, u32[]{:S(2)}, u32[]{:S(2)}) async-start(f32[32,6,8,128]{3,2,1,0:T(8,128)} %shard_map.72), calls=%async_computation.2 | async-start | bytes 1572864 | tf_op jit(solution)/shard_map/all_to_all | solution.py:216
  34.4 0.1 shard_map.69
  34.5 2.4 %collective-permute-start = (f32[480,128]{1,0:T(8,128)S(1)}, f32[480,128]{1,0:T(8,128)S(1)}, u32[]{:S(2)}, u32[]{:S(2)}) collective-permute-start(f32[480,128]{1,0:T(8,128)S(1)} %get-tuple-element.4), channel_id=1, source_target_pairs={{0,64},{64,128},{128,192},{192,0},{1,65},{65,129},{129,193},{193,1... | collective-permute-start | bytes 737288 | tf_op jit(solution)/shard_map/ppermute | solution.py:219
  36.9 3.3 %collective-permute-start.1 = (f32[96,128]{1,0:T(8,128)S(1)}, f32[96,128]{1,0:T(8,128)S(1)}, u32[]{:S(2)}, u32[]{:S(2)}) collective-permute-start(f32[96,128]{1,0:T(8,128)S(1)} %get-tuple-element.5.refs_2_), channel_id=1, source_target_pairs={{0,128},{64,192},{128,0},{192,64},{1,129},{65,193},{129,1},{193,65... | collective-permute-start | bytes 147464 | tf_op jit(solution)/shard_map/ppermute | solution.py:219
  40.2 3.3 %collective-permute-start.2 = (f32[96,128]{1,0:T(8,128)S(1)}, f32[96,128]{1,0:T(8,128)S(1)}, u32[]{:S(2)}, u32[]{:S(2)}) collective-permute-start(f32[96,128]{1,0:T(8,128)S(1)} %get-tuple-element.5.refs_2_), channel_id=1, source_target_pairs={{0,192},{64,0},{128,64},{192,128},{1,193},{65,1},{129,65},{193,129... | collective-permute-start | bytes 147464 | tf_op jit(solution)/shard_map/ppermute | solution.py:219
  43.5 21.1 %collective-permute-done.1.refs_3_ = f32[96,128]{1,0:T(8,128)S(1)} collective-permute-done((f32[96,128]{1,0:T(8,128)S(1)}, f32[96,128]{1,0:T(8,128)S(1)}, u32[]{:S(2)}, u32[]{:S(2)}) %collective-permute-start.1) | collective-permute-done | bytes 49184 | tf_op jit(solution)/shard_map/ppermute | solution.py:219
  64.5 0.0 collective-permute-done.2.refs_4_
  64.5 0.0 collective-permute-done.refs_1_
  64.5 16.9 %shard_map.70 = f32[1536,128]{1,0:T(8,128)} custom-call(f32[1792,128]{1,0:T(8,128)S(1)} %bitcast.5, f32[480,128]{1,0:T(8,128)S(1)} %collective-permute-done.refs_1_, f32[96,128]{1,0:T(8,128)S(1)} %get-tuple-element.5.refs_2_, f32[96,128]{1,0:T(8,128)S(1)} %collective-permute-done.1.refs_3_, f32[96,128]{1,0:T(8,128)S(1)} %collective-permute-done.2.refs_4_), custom_call_target="tpu_custom_call" | custom-call | flops 10468982784 | bytes 1572864 | tf_op jit(solution)/shard_map/pallas_call | solution.py:239
  81.5 0.0 all-to-all-done.2
  81.5 10.0 %all-to-all-start.1 = ((f32[8,4,6,8,128]{4,3,2,1,0:T(8,128)}), f32[8,4,6,8,128]{4,3,2,1,0:T(8,128)S(1)}, u32[]{:S(2)}, u32[]{:S(2)}) async-start(f32[8,4,6,8,128]{4,3,2,1,0:T(8,128)} %bitcast.3), calls=%async_computation.1 | async-start | bytes 1572864 | tf_op jit(solution)/shard_map/all_to_all | solution.py:216
  91.5 6.6 %shard_map.73 = f32[8,24576]{1,0:T(8,128)} custom-call(f32[1536,128]{1,0:T(8,128)S(1)} %bitcast.6, f32[480,128]{1,0:T(8,128)S(1)} %collective-permute-done.refs_1_, f32[96,128]{1,0:T(8,128)S(1)} %get-tuple-element.5.refs_2_, f32[96,128]{1,0:T(8,128)S(1)} %collective-permute-done.1.refs_3_, f32[96,128]{1,0:T(8,128)S(1)} %collective-permute-done.2.refs_4_), custom_call_target="tpu_custom_call" | custom-call | flops 2617245696 | bytes 2359296 | tf_op jit(solution)/shard_map/pallas_call | solution.py:243
  98.1 5.7 %all-to-all-done.1.y_ref = f32[8,4,6,8,128]{4,3,2,1,0:T(8,128)S(1)} async-done(((f32[8,4,6,8,128]{4,3,2,1,0:T(8,128)}), f32[8,4,6,8,128]{4,3,2,1,0:T(8,128)S(1)}, u32[]{:S(2)}, u32[]{:S(2)}) %all-to-all-start.1) | async-done | bytes 786464 | tf_op jit(solution)/shard_map/all_to_all | solution.py:216
  103.7 1.1 %shard_map.71 = f32[768,256]{1,0:T(8,128)} custom-call(f32[8,4,6,8,128]{4,3,2,1,0:T(8,128)S(1)} %all-to-all-done.1.y_ref), custom_call_target="tpu_custom_call" | custom-call | bytes 1572864 | tf_op jit(solution)/shard_map/pallas_call | solution.py:246
Async XLA Ops:
  0.6 0.7 copy-start.4
  0.6 0.7 copy-start.3
  1.3 1.1 %copy-start = (f32[768,256]{1,0:T(8,128)S(1)}, f32[768,256]{1,0:T(8,128)}, u32[]{:S(2)}) copy-start(f32[768,256]{1,0:T(8,128)} %x_ref.2) | copy-start | bytes 2359300
  2.5 0.8 copy-start.2
  4.5 6.8 %copy-start.1 = (f32[768,256]{1,0:T(8,128)S(1)}, f32[768,256]{1,0:T(8,128)}, u32[]{:S(2)}) copy-start(f32[768,256]{1,0:T(8,128)} %x_ref.3) | copy-start | bytes 2359300
  4.5 20.5 %all-to-all-start = ((f32[8,4,7,8,128]{4,3,2,1,0:T(8,128)}), f32[8,4,7,8,128]{4,3,2,1,0:T(8,128)S(1)}, u32[]{:S(2)}, u32[]{:S(2)}) async-start(f32[8,4,7,8,128]{4,3,2,1,0:T(8,128)} %shard_map.68), calls=%async_computation | async-start | bytes 1835008 | tf_op jit(solution)/shard_map/all_to_all | solution.py:216
  25.0 56.4 %all-to-all-start.2 = ((f32[32,6,8,128]{3,2,1,0:T(8,128)}), f32[32,6,8,128]{3,2,1,0:T(8,128)S(1)}, u32[]{:S(2)}, u32[]{:S(2)}) async-start(f32[32,6,8,128]{3,2,1,0:T(8,128)} %shard_map.72), calls=%async_computation.2 | async-start | bytes 1572864 | tf_op jit(solution)/shard_map/all_to_all | solution.py:216
  34.5 30.1 %collective-permute-start = (f32[480,128]{1,0:T(8,128)S(1)}, f32[480,128]{1,0:T(8,128)S(1)}, u32[]{:S(2)}, u32[]{:S(2)}) collective-permute-start(f32[480,128]{1,0:T(8,128)S(1)} %get-tuple-element.4), channel_id=1, source_target_pairs={{0,64},{64,128},{128,192},{192,0},{1,65},{65,129},{129,193},{193,1... | collective-permute-start | bytes 737288 | tf_op jit(solution)/shard_map/ppermute | solution.py:219
  36.9 27.7 %collective-permute-start.1 = (f32[96,128]{1,0:T(8,128)S(1)}, f32[96,128]{1,0:T(8,128)S(1)}, u32[]{:S(2)}, u32[]{:S(2)}) collective-permute-start(f32[96,128]{1,0:T(8,128)S(1)} %get-tuple-element.5.refs_2_), channel_id=1, source_target_pairs={{0,128},{64,192},{128,0},{192,64},{1,129},{65,193},{129,1},{193,65... | collective-permute-start | bytes 147464 | tf_op jit(solution)/shard_map/ppermute | solution.py:219
  40.2 24.4 %collective-permute-start.2 = (f32[96,128]{1,0:T(8,128)S(1)}, f32[96,128]{1,0:T(8,128)S(1)}, u32[]{:S(2)}, u32[]{:S(2)}) collective-permute-start(f32[96,128]{1,0:T(8,128)S(1)} %get-tuple-element.5.refs_2_), channel_id=1, source_target_pairs={{0,192},{64,0},{128,64},{192,128},{1,193},{65,1},{129,65},{193,129... | collective-permute-start | bytes 147464 | tf_op jit(solution)/shard_map/ppermute | solution.py:219
  81.5 22.3 %all-to-all-start.1 = ((f32[8,4,6,8,128]{4,3,2,1,0:T(8,128)}), f32[8,4,6,8,128]{4,3,2,1,0:T(8,128)S(1)}, u32[]{:S(2)}, u32[]{:S(2)}) async-start(f32[8,4,6,8,128]{4,3,2,1,0:T(8,128)} %bitcast.3), calls=%async_computation.1 | async-start | bytes 1572864 | tf_op jit(solution)/shard_map/all_to_all | solution.py:216

commit v2 on v1

v2 whole, which is shorter than its diff:
```python
import jax
import jax.numpy as jnp
from jax import lax
from jax.experimental import pallas as pl
from jax.experimental.pallas import tpu as pltpu
from jax.sharding import Mesh, PartitionSpec as P

LANES = 128
SUBS = 8
NEAR = 8


def store_parts(out_ref, k, part):
    far = out_ref.shape[1]
    step = part.shape[0] // far
    for z in range(far):
        out_ref[:, z, k, :, :] = part[z * step:(z + 1) * step].reshape(-1, SUBS, LANES)


def pack_with_taps(x_ref, gain_ref, band_ref, *refs):
    taps_refs, out_ref = refs[:-1], refs[-1]
    block_len = x_ref.shape[0]
    tiles = block_len // LANES
    for k in range(tiles):
        store_parts(out_ref, k, x_ref[k * LANES:(k + 1) * LANES, :].T)
    rows, chans = taps_refs[0].shape
    far = len(taps_refs)
    room = LANES // 2
    blank = jnp.zeros((room - rows, chans), jnp.float32)
    columns = []
    for back, taps_ref in enumerate(taps_refs):
        place = lax.rem(lax.axis_index("far") + far - back, far) * NEAR + lax.axis_index("near")
        lag = place * rows + lax.broadcasted_iota(jnp.int32, (rows, chans), 0)
        kept = jnp.where(lag < band_ref[...] * block_len, taps_ref[...], 0.0)
        columns += [kept + jnp.where(lag == 0, gain_ref[...], 0.0), blank]
    for tile in range(far // 2):
        store_parts(out_ref, tiles + tile, jnp.concatenate(columns[4 * tile:4 * tile + 4], axis=0).T)


def pack_plain(x_ref, after_ref, out_ref):
    for k in range(x_ref.shape[0] // LANES):
        part = x_ref[k * LANES:(k + 1) * LANES, :].T
        out_ref[:, k, :, :] = part.reshape(-1, SUBS, LANES)


def unpack(y_ref, after_ref, out_ref):
    for k in range(out_ref.shape[0] // LANES):
        part = jnp.concatenate([y_ref[:, z, k, :, :].reshape(-1, LANES) for z in range(y_ref.shape[1])], axis=0)
        out_ref[k * LANES:(k + 1) * LANES, :] = part.T


def split(value):
    high = value.astype(jnp.bfloat16)
    return high, (value - high.astype(jnp.float32)).astype(jnp.bfloat16)


def toeplitz(row):
    wide = jnp.broadcast_to(row, (LANES, row.shape[1]))
    return pltpu.roll(wide, 0, axis=1, stride=1, stride_axis=0)[:, LANES:]


def shifted(value, steps):
    if steps == 0:
        return value
    blank = jnp.zeros((steps, value.shape[1]), value.dtype)
    return jnp.concatenate([value[steps:], blank], axis=0)


def lay_rows(row_ref, taps_tiles, rows, near, far, piece_of):
    lane = lax.broadcasted_iota(jnp.int32, row_ref.shape[1:], 1)
    row_ref[...] = jnp.zeros(row_ref.shape, jnp.float32)
    room = LANES // 2
    per = rows * near // LANES
    for back in range(far):
        source = lax.rem(lax.axis_index("far") + far - back, far)
        for piece in range(near):
            tile, offset = divmod(rows * piece, LANES)
            value = piece_of(piece, back // 2)
            turn = (offset - room * (back % 2)) % LANES
            value = pltpu.roll(value, turn, axis=1) if turn else value
            at = 1 + source * per + tile
            row_ref[at] = row_ref[at] + jnp.where((lane >= offset) & (lane < offset + rows), value, 0.0)
            if offset + rows > LANES:
                row_ref[at + 1] = row_ref[at + 1] + jnp.where(lane < offset + rows - LANES, value, 0.0)


def row_of(row_ref, chan):
    return jnp.concatenate([row_ref[t, pl.ds(chan, 1), :] for t in range(row_ref.shape[0])], axis=1)


def forward(halo_blocks, tiles, rows, x_ref, halo_ref, y_ref, row_ref, held_ref):
    near, far, depth = x_ref.shape[:3]
    taps_tiles = depth - tiles
    chans = far * SUBS
    chunk = far * depth * SUBS
    lay_rows(row_ref, taps_tiles, rows, near, far,
             lambda piece, tile: x_ref[piece, :, tiles + tile, :, :].reshape(chans, LANES))
    first = lax.axis_index("far") == 0
    for block in range(halo_blocks):
        for z in range(far):
            at = block * chunk + z * depth * SUBS
            held_ref[at:at + tiles * SUBS, :] = jnp.where(first, 0.0, halo_ref[block, z].reshape(-1, LANES))
    held_ref[halo_blocks * chunk:, :] = x_ref[...].reshape(-1, LANES)
    each = depth * SUBS
    depth = row_ref.shape[0] - 1

    def one(chan, carry):
        z, i = lax.div(chan, SUBS), lax.rem(chan, SUBS)
        high_t, low_t = split(toeplitz(row_of(row_ref, chan)))
        moved = {}
        for k in range(tiles):
            for steps in range(halo_blocks + 1):
                start = (halo_blocks - steps) * chunk + z * each + k * SUBS + i
                moved[k, steps] = jnp.concatenate(split(held_ref[pl.ds(start, near, stride=chunk), :]), axis=0)
        columns = []
        for d in range(depth):
            parts = []
            for k in range(tiles):
                turns, at = divmod(k - d, tiles)
                parts.append(moved[at, -turns])
            columns.append(jnp.concatenate(parts, axis=0))
        left = jnp.concatenate(columns, axis=1)
        right = jnp.concatenate(
            [jnp.concatenate([t[:, d * LANES:(d + 1) * LANES] for t in (high_t, low_t)], axis=1) for d in range(depth)],
            axis=0,
        )
        total = jnp.dot(left, right, preferred_element_type=jnp.float32)
        total = total[:, :LANES] + total[:, LANES:]
        for k in range(tiles):
            base = 2 * near * k
            value = total[base:base + near] + total[base + near:base + 2 * near]
            y_ref[pl.ds((z * tiles + k) * SUBS + i, near, stride=far * tiles * SUBS), :] = value
        return carry

    lax.fori_loop(0, chans, one, 0)


def gradient(blocks, tiles, rows, g_ref, x_ref, out_ref, token_ref, row_ref, held_ref):
    token_ref[...] = jnp.zeros(token_ref.shape, jnp.float32)
    near, far = x_ref.shape[:2]
    me = lax.axis_index("far")
    lay_rows(row_ref, x_ref.shape[2] - tiles, rows, near, far,
             lambda piece, tile: x_ref[piece, me, tiles + tile, :, :])
    depth = row_ref.shape[0] - 1
    chunk = tiles * SUBS

    def one(chan, carry):
        high_t, low_t = split(toeplitz(row_of(row_ref, chan)))
        moved = {}
        for k in range(tiles):
            value = g_ref[pl.ds(k * SUBS + chan, blocks, stride=chunk), :]
            for steps in range((depth + tiles - 2) // tiles + 1):
                moved[k, steps] = jnp.concatenate(split(shifted(value, steps)), axis=0)
        columns = []
        for d in range(depth):
            parts = []
            for k in range(tiles):
                turns, at = divmod(k + d, tiles)
                parts.append(moved[at, turns])
            columns.append(jnp.concatenate(parts, axis=0))
        left = jnp.concatenate(columns, axis=1)
        right = jnp.concatenate([high_t, low_t], axis=0)
        total = lax.dot_general(left, right, (((1,), (1,)), ((), ())), preferred_element_type=jnp.float32)
        total = total[:, :LANES] + total[:, LANES:]
        for k in range(tiles):
            base = 2 * blocks * k
            value = total[base:base + blocks] + total[base + blocks:base + 2 * blocks]
            held_ref[pl.ds(k * SUBS + chan, blocks, stride=chunk), :] = value
        return carry

    lax.fori_loop(0, SUBS, one, 0)
    for tile in range(blocks * tiles):
        out_ref[:, tile * LANES:(tile + 1) * LANES] = held_ref[tile * SUBS:(tile + 1) * SUBS, :]


def call(body, shapes, scratch=(), flops=0, moved=0, operands=0, after=0):
    specs = [pl.BlockSpec(memory_space=pltpu.VMEM)] * operands + [pl.BlockSpec(memory_space=pl.ANY)] * after
    shapes = [jax.ShapeDtypeStruct(shape, jnp.float32) for shape in shapes]
    return pl.pallas_call(
        body,
        out_shape=shapes if len(shapes) > 1 else shapes[0],
        **({"in_specs": specs} if specs else {}),
        scratch_shapes=list(scratch),
        compiler_params=pltpu.CompilerParams(vmem_limit_bytes=40 * 1024 * 1024),
        cost_estimate=pl.CostEstimate(flops=flops, bytes_accessed=moved, transcendentals=0),
    )


def local(inputs, cotangent, filter_rows, skip_gain, band_blocks):
    far = lax.axis_size("far")
    near = lax.axis_size("near")
    count = far * near
    block_len, chans = inputs.shape
    rows = filter_rows.shape[0]
    tiles = block_len // LANES
    lag_tiles = rows * count // LANES
    halo_blocks = rows * count // block_len
    size = block_len * chans * 4

    def exchanged(value, axes):
        return lax.all_to_all(value, axes, split_axis=0, concat_axis=0, tiled=True)

    def ahead(value, steps):
        return lax.ppermute(value, "far", [(z, (z + steps) % far) for z in range(far)])

    taps = [filter_rows] + [ahead(filter_rows, steps) for steps in range(1, far)]
    depth = tiles + far // 2
    sent_x = call(pack_with_taps, [(near, far, depth, SUBS, LANES)], moved=2 * size)(
        inputs, skip_gain[None, :], band_blocks[None, :], *taps)
    got_x = exchanged(sent_x, "near")
    halo = got_x[near - halo_blocks:, :, :tiles]
    got_halo = ahead(halo, 1)
    sent_g = call(pack_plain, [(count, tiles, SUBS, LANES)], moved=2 * size, operands=1, after=1)(cotangent, halo)
    got_g = exchanged(sent_g, ("far", "near")).reshape(-1, LANES)

    def row(height):
        return pltpu.VMEM((lag_tiles + 2, height, LANES), jnp.float32)

    held_rows = (near + halo_blocks) * far * depth * SUBS
    flops = 2 * far * SUBS * 2 * near * tiles * (lag_tiles + 1) * LANES * 2 * LANES
    sent_y = call(lambda *refs: forward(halo_blocks, tiles, rows, *refs), [(count * tiles * SUBS, LANES)],
                  [row(far * SUBS), pltpu.VMEM((held_rows, LANES), jnp.float32)], 40 * flops, 2 * size)(
        got_x, got_halo)
    got_y = exchanged(sent_y.reshape(near, far, tiles, SUBS, LANES), "near")
    input_grad, token = call(lambda *refs: gradient(count, tiles, rows, *refs), [(SUBS, count * block_len), (SUBS, LANES)],
                      [row(SUBS), pltpu.VMEM((count * tiles * SUBS, LANES), jnp.float32)], flops, 3 * size)(
        got_g, got_x)
    outputs = call(unpack, [(block_len, chans)], moved=2 * size, operands=1, after=1)(got_y, token)
    return outputs, input_grad


def solution(mesh):
    count, width = mesh.devices.shape
    fine = Mesh(mesh.devices.reshape(count // NEAR, NEAR, width), ("far", "near", "ch"))
    tokens = ("far", "near")
    return jax.shard_map(
        local,
        mesh=fine,
        in_specs=(P(tokens, "ch"), P(tokens, "ch"), P(tokens, "ch"), P("ch"), P("ch")),
        out_specs=(P(tokens, "ch"), P(("ch", "far", "near"), None)),
        check_vma=False,
    )
```

time: 105 us -> 90.8 us (0.86)
  waiting for transfers between devices: 39.3 us -> 14.8 us
  blocking collectives: 0 us -> 20.9 us
  starting transfers between devices: 35.1 us -> 25.1 us
    all_to_all x0 -> x1, blocking collectives: none -> 20.9 us  [exchanged(): return lax.all_to_all(value, axes, split_axis=0, concat_axis=0, tiled=True)]
    ppermute x3 -> x4, waiting for transfers between devices: 21.1 us -> 4.15 us  [ahead(): lax.ppermute(value, 'far', [(z, (z + steps) % far) for z in range(far)])]
    all_to_all x3 -> x2, starting transfers between devices: 26.2 us -> 11.7 us  [exchanged(): return lax.all_to_all(value, axes, split_axis=0, concat_axis=0, tiled=True)]
    all_to_all x3 -> x2, waiting for transfers between devices: 18.2 us -> 10.6 us  [exchanged(): return lax.all_to_all(value, axes, split_axis=0, concat_axis=0, tiled=True)]
    ppermute x3 -> x4, starting transfers between devices: 8.95 us -> 13.4 us  [ahead(): lax.ppermute(value, 'far', [(z, (z + steps) % far) for z in range(far)])]
    pallas_call x6 -> x5, Pallas kernels: 27.2 us -> 26.4 us  [the longest x1 17 us: local(): call(lambda *refs: forward(halo_blocks, tiles, rows, *refs), [(count * ti...]
  transfers between devices with their start and end apart: 6 -> 6, of which waited for: 3 -> 4; matrix products, arithmetic and copies ran while one was open for 0% -> 0% of each run, Pallas kernels for 24% -> 28%
where the time goes in v2:
time: 90.8 us; the launch traced here: 90.4 us
  Pallas kernels  26.4 us (29%)
  starting transfers between devices  25.1 us (28%)
  blocking collectives  20.9 us (23%)
  waiting for transfers between devices  14.8 us (16%)
  local copies, waits for them, and re-layouts  2.64 us (3%)
    all_to_all x1, blocking collectives, exchanged(): return lax.all_to_all(value, axes, split_axis=0, concat_axis=0, tiled=True)  20.9 us
    pallas_call x1, Pallas kernels, local(): call(lambda *refs: forward(halo_blocks, tiles, rows, *refs), [(count * ti...  17 us
    ppermute x4, starting transfers between devices, ahead(): lax.ppermute(value, 'far', [(z, (z + steps) % far) for z in range(far)])  13.4 us
    all_to_all x2, starting transfers between devices, exchanged(): return lax.all_to_all(value, axes, split_axis=0, concat_axis=0, tiled=True)  11.7 us
    all_to_all x2, waiting for transfers between devices, exchanged(): return lax.all_to_all(value, axes, split_axis=0, concat_axis=0, tiled=True)  10.6 us
    pallas_call x1, Pallas kernels, local(): call(lambda *refs: gradient(count, tiles, rows, *refs), [(SUBS, count * b...  6.7 us
    ppermute x4, waiting for transfers between devices, ahead(): lax.ppermute(value, 'far', [(z, (z + steps) % far) for z in range(far)])  4.15 us
    unnamed x10, local copies, waits for them, and re-layouts  2.63 us
  transfers between devices with their start and end apart: 6, of which 4 were waited for; matrix products, arithmetic and copies ran while one was open for 0% of the time, Pallas kernels for 28%

profile of v2, /device:TPU:1, one launch (start us, length us, event | category | flops | bytes accessed | tf_op | source)
XLA Modules:
  0.0 90.4 jit_solution(16832777765271248026)
XLA Ops:
  0.6 3.9 %collective-permute-start = (f32[48,256]{1,0:T(8,128)}, f32[48,256]{1,0:T(8,128)S(1)}, u32[]{:S(2)}, u32[]{:S(2)}) collective-permute-start(f32[48,256]{1,0:T(8,128)} %refs_0_.1), channel_id=1, source_target_pairs={{0,64},{64,128},{128,192},{192,0},{1,65},{65,129},{129,193},{193,1... | collective-permute-start | bytes 147464 | tf_op jit(solution)/shard_map/ppermute | solution.py:204
  4.5 5.1 %collective-permute-start.1 = (f32[48,256]{1,0:T(8,128)}, f32[48,256]{1,0:T(8,128)S(1)}, u32[]{:S(2)}, u32[]{:S(2)}) collective-permute-start(f32[48,256]{1,0:T(8,128)} %refs_0_.1), channel_id=1, source_target_pairs={{0,128},{64,192},{128,0},{192,64},{1,129},{65,193},{129,1},{193,65... | collective-permute-start | bytes 147464 | tf_op jit(solution)/shard_map/ppermute | solution.py:204
  9.6 2.4 %collective-permute-start.2 = (f32[48,256]{1,0:T(8,128)}, f32[48,256]{1,0:T(8,128)S(1)}, u32[]{:S(2)}, u32[]{:S(2)}) collective-permute-start(f32[48,256]{1,0:T(8,128)} %refs_0_.1), channel_id=1, source_target_pairs={{0,192},{64,0},{128,64},{192,128},{1,193},{65,1},{129,65},{193,129... | collective-permute-start | bytes 147464 | tf_op jit(solution)/shard_map/ppermute | solution.py:204
  12.0 0.0 collective-permute-done.refs_1_
  12.0 0.0 collective-permute-done.1.refs_2_
  12.0 3.3 %collective-permute-done.2.refs_3_ = f32[48,256]{1,0:T(8,128)S(1)} collective-permute-done((f32[48,256]{1,0:T(8,128)}, f32[48,256]{1,0:T(8,128)S(1)}, u32[]{:S(2)}, u32[]{:S(2)}) %collective-permute-start.2) | collective-permute-done | bytes 49184 | tf_op jit(solution)/shard_map/ppermute | solution.py:204
  15.4 0.0 copy-start.4
  15.4 0.0 copy-start.3
  15.4 0.7 copy-done.4
  16.0 0.0 copy-done.3
  16.1 0.0 copy-start.1
  16.1 1.1 %copy-done.1 = f32[768,256]{1,0:T(8,128)S(1)} copy-done((f32[768,256]{1,0:T(8,128)S(1)}, f32[768,256]{1,0:T(8,128)}, u32[]{:S(2)}) %copy-start.1) | copy-done | bytes 786456
  17.2 0.0 copy-start.2
  17.2 0.8 copy-done.2
  18.0 0.3 shard_map.68
  18.3 0.0 copy-start
  18.3 20.9 %all_to_all.15.refs_0_.refs_1_ = f32[8,4,8,8,128]{4,3,2,1,0:T(8,128)S(1)} all-to-all(f32[8,4,8,8,128]{4,3,2,1,0:T(8,128)S(1)} %shard_map.68), channel_id=1, replica_groups=mesh['far'=4,'near'=8,'ch'=8] {'near'}, dimensions={0} | all-to-all | bytes 2097152 | tf_op jit(solution)/shard_map/all_to_all | solution.py:201
  39.2 2.0 %collective-permute-start.3 = (f32[2,4,6,8,128]{4,3,2,1,0:T(8,128)S(1)}, f32[2,4,6,8,128]{4,3,2,1,0:T(8,128)S(1)}, u32[]{:S(2)}, u32[]{:S(2)}) collective-permute-start(f32[2,4,6,8,128]{4,3,2,1,0:T(8,128)S(1)} %slice.4.after_ref), channel_id=1, source_target_pairs={{0,64},{64,128},{128,192},{192,0},{1,65},{65,129},{129,193},{193,1... | collective-permute-start | bytes 589832 | tf_op jit(solution)/shard_map/ppermute | solution.py:204
  41.3 0.0 copy-done
  41.3 1.1 %shard_map.70 = f32[32,6,8,128]{3,2,1,0:T(8,128)} custom-call(f32[768,256]{1,0:T(8,128)S(1)} %copy-done, f32[2,4,6,8,128]{4,3,2,1,0:T(8,128)S(1)} %slice.4.after_ref), custom_call_target="tpu_custom_call" | custom-call | bytes 1572864 | tf_op jit(solution)/shard_map/pallas_call | solution.py:213
  42.4 6.9 %all-to-all-start.2 = ((f32[32,6,8,128]{3,2,1,0:T(8,128)}), f32[32,6,8,128]{3,2,1,0:T(8,128)S(1)}, u32[]{:S(2)}, u32[]{:S(2)}) async-start(f32[32,6,8,128]{3,2,1,0:T(8,128)} %shard_map.70), calls=%async_computation.2 | async-start | bytes 1572864 | tf_op jit(solution)/shard_map/all_to_all | solution.py:201
  49.3 0.8 collective-permute-done.3.refs_1_
  50.2 17.0 %shard_map.69 = f32[1536,128]{1,0:T(8,128)} custom-call(f32[8,4,8,8,128]{4,3,2,1,0:T(8,128)S(1)} %all_to_all.15.refs_0_.refs_1_, f32[2,4,6,8,128]{4,3,2,1,0:T(8,128)S(1)} %collective-permute-done.3.refs_1_), custom_call_target="tpu_custom_call" | custom-call | flops 104689827840 | bytes 1572864 | tf_op jit(solution)/shard_map/pallas_call | solution.py:221
  67.2 5.0 %all-to-all-done.2 = f32[32,6,8,128]{3,2,1,0:T(8,128)S(1)} async-done(((f32[32,6,8,128]{3,2,1,0:T(8,128)}), f32[32,6,8,128]{3,2,1,0:T(8,128)S(1)}, u32[]{:S(2)}, u32[]{:S(2)}) %all-to-all-start.2) | async-done | bytes 786464 | tf_op jit(solution)/shard_map/all_to_all | solution.py:201
  72.2 4.8 %all-to-all-start.1 = ((f32[8,4,6,8,128]{4,3,2,1,0:T(8,128)}), f32[8,4,6,8,128]{4,3,2,1,0:T(8,128)S(1)}, u32[]{:S(2)}, u32[]{:S(2)}) async-start(f32[8,4,6,8,128]{4,3,2,1,0:T(8,128)} %bitcast.2), calls=%async_computation.1 | async-start | bytes 1572864 | tf_op jit(solution)/shard_map/all_to_all | solution.py:201
  77.0 6.7 %shard_map.71 = (f32[8,24576]{1,0:T(8,128)}, f32[8,128]{1,0:T(8,128)S(1)}) custom-call(f32[1536,128]{1,0:T(8,128)S(1)} %bitcast.4, f32[8,4,8,8,128]{4,3,2,1,0:T(8,128)S(1)} %all_to_all.15.refs_0_.refs_1_), custom_call_target="tpu_custom_call" | custom-call | flops 2617245696 | bytes 2359296 | tf_op jit(solution)/shard_map/pallas_call | solution.py:225
  83.7 5.6 %all-to-all-done.1.y_ref = f32[8,4,6,8,128]{4,3,2,1,0:T(8,128)S(1)} async-done(((f32[8,4,6,8,128]{4,3,2,1,0:T(8,128)}), f32[8,4,6,8,128]{4,3,2,1,0:T(8,128)S(1)}, u32[]{:S(2)}, u32[]{:S(2)}) %all-to-all-start.1) | async-done | bytes 786464 | tf_op jit(solution)/shard_map/all_to_all | solution.py:201
  89.3 1.1 %shard_map.72 = f32[768,256]{1,0:T(8,128)} custom-call(f32[8,4,6,8,128]{4,3,2,1,0:T(8,128)S(1)} %all-to-all-done.1.y_ref, f32[8,128]{1,0:T(8,128)S(1)} %get-tuple-element.4.after_ref), custom_call_target="tpu_custom_call" | custom-call | bytes 1572864 | tf_op jit(solution)/shard_map/pallas_call | solution.py:228
  (1 shorter events, 0.0 us)
Async XLA Ops:
  0.6 11.4 %collective-permute-start = (f32[48,256]{1,0:T(8,128)}, f32[48,256]{1,0:T(8,128)S(1)}, u32[]{:S(2)}, u32[]{:S(2)}) collective-permute-start(f32[48,256]{1,0:T(8,128)} %refs_0_.1), channel_id=1, source_target_pairs={{0,64},{64,128},{128,192},{192,0},{1,65},{65,129},{129,193},{193,1... | collective-permute-start | bytes 147464 | tf_op jit(solution)/shard_map/ppermute | solution.py:204
  4.5 7.5 %collective-permute-start.1 = (f32[48,256]{1,0:T(8,128)}, f32[48,256]{1,0:T(8,128)S(1)}, u32[]{:S(2)}, u32[]{:S(2)}) collective-permute-start(f32[48,256]{1,0:T(8,128)} %refs_0_.1), channel_id=1, source_target_pairs={{0,128},{64,192},{128,0},{192,64},{1,129},{65,193},{129,1},{193,65... | collective-permute-start | bytes 147464 | tf_op jit(solution)/shard_map/ppermute | solution.py:204
  9.6 5.7 %collective-permute-start.2 = (f32[48,256]{1,0:T(8,128)}, f32[48,256]{1,0:T(8,128)S(1)}, u32[]{:S(2)}, u32[]{:S(2)}) collective-permute-start(f32[48,256]{1,0:T(8,128)} %refs_0_.1), channel_id=1, source_target_pairs={{0,192},{64,0},{128,64},{192,128},{1,193},{65,1},{129,65},{193,129... | collective-permute-start | bytes 147464 | tf_op jit(solution)/shard_map/ppermute | solution.py:204
  15.4 0.7 copy-start.4
  15.4 0.7 copy-start.3
  16.1 1.1 %copy-start.1 = (f32[768,256]{1,0:T(8,128)S(1)}, f32[768,256]{1,0:T(8,128)}, u32[]{:S(2)}) copy-start(f32[768,256]{1,0:T(8,128)} %x_ref.2) | copy-start | bytes 2359300
  17.2 0.8 copy-start.2
  18.3 22.9 %copy-start = (f32[768,256]{1,0:T(8,128)S(1)}, f32[768,256]{1,0:T(8,128)}, u32[]{:S(2)}) copy-start(f32[768,256]{1,0:T(8,128)} %x_ref.3) | copy-start | bytes 2359300
  39.2 10.9 %collective-permute-start.3 = (f32[2,4,6,8,128]{4,3,2,1,0:T(8,128)S(1)}, f32[2,4,6,8,128]{4,3,2,1,0:T(8,128)S(1)}, u32[]{:S(2)}, u32[]{:S(2)}) collective-permute-start(f32[2,4,6,8,128]{4,3,2,1,0:T(8,128)S(1)} %slice.4.after_ref), channel_id=1, source_target_pairs={{0,64},{64,128},{128,192},{192,0},{1,65},{65,129},{129,193},{193,1... | collective-permute-start | bytes 589832 | tf_op jit(solution)/shard_map/ppermute | solution.py:204
  42.4 29.8 %all-to-all-start.2 = ((f32[32,6,8,128]{3,2,1,0:T(8,128)}), f32[32,6,8,128]{3,2,1,0:T(8,128)S(1)}, u32[]{:S(2)}, u32[]{:S(2)}) async-start(f32[32,6,8,128]{3,2,1,0:T(8,128)} %shard_map.70), calls=%async_computation.2 | async-start | bytes 1572864 | tf_op jit(solution)/shard_map/all_to_all | solution.py:201
  72.2 17.1 %all-to-all-start.1 = ((f32[8,4,6,8,128]{4,3,2,1,0:T(8,128)}), f32[8,4,6,8,128]{4,3,2,1,0:T(8,128)S(1)}, u32[]{:S(2)}, u32[]{:S(2)}) async-start(f32[8,4,6,8,128]{4,3,2,1,0:T(8,128)} %bitcast.2), calls=%async_computation.1 | async-start | bytes 1572864 | tf_op jit(solution)/shard_map/all_to_all | solution.py:201

commit v3 on v1

--- a/solution.py
+++ b/solution.py
@@ -31,13 +31,26 @@
     store_parts(out_ref, tiles, kept.T)
 
 
-def pack_plain(x_ref, out_ref):
-    for k in range(x_ref.shape[0] // LANES):
-        part = x_ref[k * LANES:(k + 1) * LANES, :].T
-        out_ref[:, k, :, :] = part.reshape(-1, SUBS, LANES)
-
-
-def unpack(y_ref, out_ref):
+def pack_by_far(g_ref, *refs):
+    outs, held_ref = refs[:-1], refs[-1]
+    far = len(outs)
+    for k in range(g_ref.shape[0] // LANES):
+        part = g_ref[k * LANES:(k + 1) * LANES, :].T
+        step = part.shape[0] // far
+        for z in range(far):
+            held_ref[z, :, k, :, :] = part[z * step:(z + 1) * step].reshape(-1, SUBS, LANES)
+    for steps, out_ref in enumerate(outs):
+        out_ref[...] = held_ref[lax.rem(lax.axis_index("far") + steps, far)]
+
+
+def stack(*refs):
+    parts, out_ref = refs[:-1], refs[-1]
+    far = len(parts)
+    for back, ref in enumerate(parts):
+        out_ref[:, lax.rem(lax.axis_index("far") + far - back, far)] = ref[...]
+
+
+def unpack(y_ref, after_ref, out_ref):
     for k in range(out_ref.shape[0] // LANES):
         part = jnp.concatenate([y_ref[:, z, k, :, :].reshape(-1, LANES) for z in range(y_ref.shape[1])], axis=0)
         out_ref[k * LANES:(k + 1) * LANES, :] = part.T
@@ -48,7 +61,8 @@
     return high, (value - high.astype(jnp.float32)).astype(jnp.bfloat16)
 
 
-def collect(rows, halo_blocks, x_ref, halo_ref, taps_ref):
+def collect(rows, halo_blocks, x_ref, *refs):
+    halo_ref, taps_ref = refs[-2:]
     near, far, tiles = x_ref.shape[:3]
     tiles = tiles - 1
     lane = lax.broadcasted_iota(jnp.int32, (far * SUBS, LANES), 1)
@@ -148,11 +162,12 @@
             y_ref[pl.ds((z * tiles + k) * SUBS + i, near, stride=far * tiles * SUBS), :] = value
         return carry
 
-    lax.fori_loop(0, chans, one, 0)
-
-
-def gradient(blocks, tiles, halo_rows, g_ref, halo_ref, *refs):
-    others, (out_ref, row_ref, held_ref) = refs[:-3], refs[-3:]
+    lax.fori_loop(0, chans, one, 0, unroll=8)
+
+
+def gradient(near, tiles, halo_rows, g_ref, halo_ref, *refs):
+    others, (out_ref, token_ref, row_ref, held_ref) = refs[:-4], refs[-4:]
+    token_ref[...] = jnp.zeros(token_ref.shape, jnp.float32)
     far = len(others) + 1
     me = lax.axis_index("far")
     pieces = [(others[0], 0), (halo_ref, halo_rows)] + [(ref, 0) for ref in others[1:]]
@@ -160,12 +175,14 @@
              lambda ref, base: ref[pl.ds(pl.multiple_of(base + me * SUBS, SUBS), SUBS), :])
     depth = row_ref.shape[0] - 1
     chunk = tiles * SUBS
+    blocks = near * far
 
     def one(chan, carry):
         high_t, low_t = split(toeplitz(row_of(row_ref, chan)))
         moved = {}
         for k in range(tiles):
-            value = g_ref[pl.ds(k * SUBS + chan, blocks, stride=chunk), :]
+            value = jnp.concatenate(
+                [g_ref[pl.ds((z * tiles + k) * SUBS + chan, near, stride=far * chunk), :] for z in range(far)], axis=0)
             for steps in range((depth + tiles - 2) // tiles + 1):
                 moved[k, steps] = jnp.concatenate(split(shifted(value, steps)), axis=0)
         columns = []
@@ -185,18 +202,20 @@
             held_ref[pl.ds(k * SUBS + chan, blocks, stride=chunk), :] = value
         return carry
 
-    lax.fori_loop(0, SUBS, one, 0)
+    lax.fori_loop(0, SUBS, one, 0, unroll=2)
     for tile in range(blocks * tiles):
         out_ref[:, tile * LANES:(tile + 1) * LANES] = held_ref[tile * SUBS:(tile + 1) * SUBS, :]
 
 
-def call(body, shapes, scratch=(), flops=0, moved=0):
+def call(body, shapes, scratch=(), flops=0, moved=0, operands=0, after=0, room=40):
+    specs = [pl.BlockSpec(memory_space=pltpu.VMEM)] * operands + [pl.BlockSpec(memory_space=pl.ANY)] * after
     shapes = [jax.ShapeDtypeStruct(shape, jnp.float32) for shape in shapes]
     return pl.pallas_call(
         body,
         out_shape=shapes if len(shapes) > 1 else shapes[0],
+        **({"in_specs": specs} if specs else {}),
         scratch_shapes=list(scratch),
-        compiler_params=pltpu.CompilerParams(vmem_limit_bytes=40 * 1024 * 1024),
+        compiler_params=pltpu.CompilerParams(vmem_limit_bytes=room * 1024 * 1024),
         cost_estimate=pl.CostEstimate(flops=flops, bytes_accessed=moved, transcendentals=0),
     )
 
@@ -218,18 +237,20 @@
     def ahead(value, steps):
         return lax.ppermute(value, "far", [(z, (z + steps) % far) for z in range(far)])
 
-    sent_x = call(pack_with_taps, [(near, far, tiles + 1, SUBS, LANES)], moved=2 * size)(
+    sent_g = call(pack_by_far, [(near, tiles, SUBS, LANES)] * far,
+                  [pltpu.VMEM((far, near, tiles, SUBS, LANES), jnp.float32)], moved=2 * size)(cotangent)
+    parts = [ahead(part, steps) if steps else part for steps, part in enumerate(sent_g)]
+    stacked = call(stack, [(near, far, tiles, SUBS, LANES)], flops=1 * 10 ** 10, moved=2 * size)(*parts)
+    got_g = exchanged(stacked, "near").reshape(-1, LANES)
+    sent_x = call(pack_with_taps, [(near, far, tiles + 1, SUBS, LANES)], moved=2 * size, room=60)(
         inputs, filter_rows, skip_gain[None, :], band_blocks[None, :])
     got_x = exchanged(sent_x, "near")
     halo_rows = halo_blocks * far * tiles * SUBS
     own_taps = lag_tiles // far * far * SUBS
     halo, taps = call(lambda *refs: collect(rows, halo_blocks, *refs),
-                      [(halo_rows + own_taps, LANES), (own_taps, LANES)], moved=size)(got_x)
+                      [(halo_rows + own_taps, LANES), (own_taps, LANES)], moved=size, operands=1, after=1)(got_x, stacked)
     got_halo = ahead(halo, 1)
     pieces = [taps] + [ahead(taps, steps) for steps in range(2, far)]
-    sent_g = call(pack_plain, [(count, tiles, SUBS, LANES)], moved=2 * size)(cotangent)
-    got_g = exchanged(sent_g, ("far", "near")).reshape(-1, LANES)
-
     def row(height):
         return pltpu.VMEM((lag_tiles + 2, height, LANES), jnp.float32)
 
@@ -237,13 +258,13 @@
     held_rows = (near + halo_blocks) * far * (tiles + 1) * SUBS
     flops = 2 * far * SUBS * 2 * near * tiles * (lag_tiles + 1) * LANES * 2 * LANES
     sent_y = call(lambda *refs: forward(halo_blocks, tiles, *refs), [(count * tiles * SUBS, LANES)],
-                  [row(far * SUBS), pltpu.VMEM((held_rows, LANES), jnp.float32)], 4 * flops, 2 * size)(
+                  [row(far * SUBS), pltpu.VMEM((held_rows, LANES), jnp.float32)], 40 * flops, 2 * size)(
         got_x, got_halo, *pieces)
     got_y = exchanged(sent_y.reshape(near, far, tiles, SUBS, LANES), "near")
-    input_grad = call(lambda *refs: gradient(count, tiles, halo_rows, *refs), [(SUBS, count * block_len)],
+    input_grad, token = call(lambda *refs: gradient(near, tiles, halo_rows, *refs), [(SUBS, count * block_len), (SUBS, LANES)],
                       [row(SUBS), pltpu.VMEM((count * tiles * SUBS, LANES), jnp.float32)], flops, 3 * size)(
         got_g, got_halo, *pieces)
-    outputs = call(unpack, [(block_len, chans)], moved=2 * size)(got_y)
+    outputs = call(unpack, [(block_len, chans)], moved=2 * size, operands=1, after=1)(got_y, token)
     return outputs, input_grad
 
 

time: 105 us -> 80.3 us (0.76)
  waiting for transfers between devices: 39.3 us -> 25.4 us
  Pallas kernels: 27.2 us -> 20.6 us
  starting transfers between devices: 35.1 us -> 32.2 us
  local copies, waits for them, and re-layouts: 2.61 us -> 1.13 us
    all_to_all x3, starting transfers between devices: 26.2 us -> 16.4 us  [exchanged(): return lax.all_to_all(value, axes, split_axis=0, concat_axis=0, tiled=True)]
    ppermute x3 -> x6, waiting for transfers between devices: 21.1 us -> 13.4 us  [ahead(): lax.ppermute(value, 'far', [(z, (z + steps) % far) for z in range(far)])]
    ppermute x3 -> x6, starting transfers between devices: 8.95 us -> 15.8 us  [ahead(): lax.ppermute(value, 'far', [(z, (z + steps) % far) for z in range(far)])]
    pallas_call x1, Pallas kernels: 16.9 us -> 10.4 us  [local(): call(lambda *refs: forward(halo_blocks, tiles, *refs), [(count * tiles *...]
    all_to_all x3, waiting for transfers between devices: 18.2 us -> 11.9 us  [exchanged(): return lax.all_to_all(value, axes, split_axis=0, concat_axis=0, tiled=True)]
    unnamed x10 -> x2, local copies, waits for them, and re-layouts: 2.61 us -> 1.13 us
    pallas_call x4 -> x5, Pallas kernels: 10.2 us -> 10.1 us  [the longest x1 5.29 us: local(): call(lambda *refs: gradient(near, tiles, halo_rows, *refs), [(SUBS, count...]
  transfers between devices with their start and end apart: 6 -> 9, of which waited for: 3 -> 6; matrix products, arithmetic and copies ran while one was open for 0% -> 0% of each run, Pallas kernels for 24% -> 24%
where the time goes in v3:
time: 80.3 us; the launch traced here: 79.9 us
  starting transfers between devices  32.2 us (40%)
  waiting for transfers between devices  25.4 us (32%)
  Pallas kernels  20.6 us (26%)
  local copies, waits for them, and re-layouts  1.13 us (1%)
    all_to_all x3, starting transfers between devices, exchanged(): return lax.all_to_all(value, axes, split_axis=0, concat_axis=0, tiled=True)  16.4 us
    ppermute x6, starting transfers between devices, ahead(): lax.ppermute(value, 'far', [(z, (z + steps) % far) for z in range(far)])  15.8 us
    ppermute x6, waiting for transfers between devices, ahead(): lax.ppermute(value, 'far', [(z, (z + steps) % far) for z in range(far)])  13.4 us
    all_to_all x3, waiting for transfers between devices, exchanged(): return lax.all_to_all(value, axes, split_axis=0, concat_axis=0, tiled=True)  11.9 us
    pallas_call x1, Pallas kernels, local(): call(lambda *refs: forward(halo_blocks, tiles, *refs), [(count * tiles *...  10.4 us
    pallas_call x1, Pallas kernels, local(): call(lambda *refs: gradient(near, tiles, halo_rows, *refs), [(SUBS, count...  5.29 us
    pallas_call x1, Pallas kernels, local(): call(pack_with_taps, [(near, far, tiles + 1, SUBS, LANES)], moved=2 * siz...  2.39 us
  transfers between devices with their start and end apart: 9, of which 6 were waited for; matrix products, arithmetic and copies ran while one was open for 0% of the time, Pallas kernels for 24%

profile of v3, /device:TPU:1, one launch (start us, length us, event | category | flops | bytes accessed | tf_op | source)
XLA Modules:
  0.0 79.9 jit_solution(1750134849384715484)
XLA Ops:
  0.6 0.0 copy-start
  0.6 1.1 %copy-done = f32[768,256]{1,0:T(8,128)S(1)} copy-done((f32[768,256]{1,0:T(8,128)S(1)}, f32[768,256]{1,0:T(8,128)}, u32[]{:S(2)}) %copy-start) | copy-done | bytes 786456
  1.8 0.3 shard_map.69
  2.1 3.9 %collective-permute-start = (f32[8,6,8,128]{3,2,1,0:T(8,128)S(1)}, f32[8,6,8,128]{3,2,1,0:T(8,128)S(1)}, u32[]{:S(2)}, u32[]{:S(2)}) collective-permute-start(f32[8,6,8,128]{3,2,1,0:T(8,128)S(1)} %get-tuple-element.11), channel_id=1, source_target_pairs={{0,64},{64,128},{128,192},{192,0},{1,65},{65,129},{129,193},{193,1... | collective-permute-start | bytes 589832 | tf_op jit(solution)/shard_map/ppermute | solution.py:238
  6.0 5.1 %collective-permute-start.1 = (f32[8,6,8,128]{3,2,1,0:T(8,128)S(1)}, f32[8,6,8,128]{3,2,1,0:T(8,128)S(1)}, u32[]{:S(2)}, u32[]{:S(2)}) collective-permute-start(f32[8,6,8,128]{3,2,1,0:T(8,128)S(1)} %get-tuple-element.12), channel_id=1, source_target_pairs={{0,128},{64,192},{128,0},{192,64},{1,129},{65,193},{129,1},{193,65... | collective-permute-start | bytes 589832 | tf_op jit(solution)/shard_map/ppermute | solution.py:238
  11.1 2.4 %collective-permute-start.2 = (f32[8,6,8,128]{3,2,1,0:T(8,128)S(1)}, f32[8,6,8,128]{3,2,1,0:T(8,128)S(1)}, u32[]{:S(2)}, u32[]{:S(2)}) collective-permute-start(f32[8,6,8,128]{3,2,1,0:T(8,128)S(1)} %get-tuple-element.13), channel_id=1, source_target_pairs={{0,192},{64,0},{128,64},{192,128},{1,193},{65,1},{129,65},{193,129... | collective-permute-start | bytes 589832 | tf_op jit(solution)/shard_map/ppermute | solution.py:238
  13.5 2.4 %shard_map.68 = f32[8,4,7,8,128]{4,3,2,1,0:T(8,128)} custom-call(f32[768,256]{1,0:T(8,128)} %x_ref.1, f32[48,256]{1,0:T(8,128)} %taps_ref.1, f32[1,256]{1,0:T(1,128)} %bitcast.7, s32[1,256]{1,0:T(1,128)} %bitcast.8), custom_call_target="tpu_custom_call" | custom-call | bytes 1572864 | tf_op jit(solution)/shard_map/pallas_call | solution.py:245
  15.9 6.0 %all-to-all-start = ((f32[8,4,7,8,128]{4,3,2,1,0:T(8,128)}), f32[8,4,7,8,128]{4,3,2,1,0:T(8,128)S(1)}, u32[]{:S(2)}, u32[]{:S(2)}) async-start(f32[8,4,7,8,128]{4,3,2,1,0:T(8,128)} %shard_map.68), calls=%async_computation | async-start | bytes 1835008 | tf_op jit(solution)/shard_map/all_to_all | solution.py:235
  21.9 0.0 collective-permute-done.refs_1_
  21.9 0.7 collective-permute-done.1.refs_2_
  22.6 7.1 %collective-permute-done.2.refs_3_ = f32[8,6,8,128]{3,2,1,0:T(8,128)S(1)} collective-permute-done((f32[8,6,8,128]{3,2,1,0:T(8,128)S(1)}, f32[8,6,8,128]{3,2,1,0:T(8,128)S(1)}, u32[]{:S(2)}, u32[]{:S(2)}) %collective-permute-start.2) | collective-permute-done | bytes 196640 | tf_op jit(solution)/shard_map/ppermute | solution.py:238
  29.7 0.9 %shard_map.70.refs_1_ = f32[8,4,6,8,128]{4,3,2,1,0:T(8,128)} custom-call(f32[8,6,8,128]{3,2,1,0:T(8,128)S(1)} %get-tuple-element.10.refs_0_, f32[8,6,8,128]{3,2,1,0:T(8,128)S(1)} %collective-permute-done.refs_1_, f32[8,6,8,128]{3,2,1,0:T(8,128)S(1)} %collective-permute-done.1.refs_2_, f32[8,6,8,128]{3,2,1,0:T(8,128)S(1)} %collective-permute-done.2.refs_3_), custom_call_target="tpu_custom_call" | custom-call | flops 10000000000 | bytes 1572864 | tf_op jit(solution)/shard_map/pallas_call | solution.py:243
  30.7 4.9 %all-to-all-done.refs_0_ = f32[8,4,7,8,128]{4,3,2,1,0:T(8,128)S(1)} async-done(((f32[8,4,7,8,128]{4,3,2,1,0:T(8,128)}), f32[8,4,7,8,128]{4,3,2,1,0:T(8,128)S(1)}, u32[]{:S(2)}, u32[]{:S(2)}) %all-to-all-start) | async-done | bytes 917536 | tf_op jit(solution)/shard_map/all_to_all | solution.py:235
  35.6 0.1 shard_map.71
  35.7 0.1 collective-permute-start.3
  35.8 1.8 %collective-permute-start.4 = (f32[96,128]{1,0:T(8,128)S(1)}, f32[96,128]{1,0:T(8,128)S(1)}, u32[]{:S(2)}, u32[]{:S(2)}) collective-permute-start(f32[96,128]{1,0:T(8,128)S(1)} %get-tuple-element.15.refs_2_), channel_id=1, source_target_pairs={{0,128},{64,192},{128,0},{192,64},{1,129},{65,193},{129,1},{193,65... | collective-permute-start | bytes 147464 | tf_op jit(solution)/shard_map/ppermute | solution.py:238
  37.6 2.5 %collective-permute-start.5 = (f32[96,128]{1,0:T(8,128)S(1)}, f32[96,128]{1,0:T(8,128)S(1)}, u32[]{:S(2)}, u32[]{:S(2)}) collective-permute-start(f32[96,128]{1,0:T(8,128)S(1)} %get-tuple-element.15.refs_2_), channel_id=1, source_target_pairs={{0,192},{64,0},{128,64},{192,128},{1,193},{65,1},{129,65},{193,129... | collective-permute-start | bytes 147464 | tf_op jit(solution)/shard_map/ppermute | solution.py:238
  40.1 5.2 %all-to-all-start.2 = ((f32[8,4,6,8,128]{4,3,2,1,0:T(8,128)}), f32[8,4,6,8,128]{4,3,2,1,0:T(8,128)S(1)}, u32[]{:S(2)}, u32[]{:S(2)}) async-start(f32[8,4,6,8,128]{4,3,2,1,0:T(8,128)} %shard_map.70.refs_1_), calls=%async_computation.2 | async-start | bytes 1572864 | tf_op jit(solution)/shard_map/all_to_all | solution.py:235
  45.2 0.0 collective-permute-done.4.refs_3_
  45.2 1.2 %collective-permute-done.5.refs_4_ = f32[96,128]{1,0:T(8,128)S(1)} collective-permute-done((f32[96,128]{1,0:T(8,128)S(1)}, f32[96,128]{1,0:T(8,128)S(1)}, u32[]{:S(2)}, u32[]{:S(2)}) %collective-permute-start.5) | collective-permute-done | bytes 49184 | tf_op jit(solution)/shard_map/ppermute | solution.py:238
  46.4 4.4 %collective-permute-done.3.refs_1_ = f32[480,128]{1,0:T(8,128)S(1)} collective-permute-done((f32[480,128]{1,0:T(8,128)S(1)}, f32[480,128]{1,0:T(8,128)S(1)}, u32[]{:S(2)}, u32[]{:S(2)}) %collective-permute-start.3) | collective-permute-done | bytes 245792 | tf_op jit(solution)/shard_map/ppermute | solution.py:238
  50.8 10.4 %shard_map.72 = f32[1536,128]{1,0:T(8,128)} custom-call(f32[1792,128]{1,0:T(8,128)S(1)} %bitcast.5, f32[480,128]{1,0:T(8,128)S(1)} %collective-permute-done.3.refs_1_, f32[96,128]{1,0:T(8,128)S(1)} %get-tuple-element.15.refs_2_, f32[96,128]{1,0:T(8,128)S(1)} %collective-permute-done.4.refs_3_, f32[96,128]{1,0:T(8,128)S(1)} %collective-permute-done.5.refs_4_), custom_call_target="tpu_custom_call" | custom-call | flops 104689827840 | bytes 1572864 | tf_op jit(solution)/shard_map/pallas_call | solution.py:260
  61.2 0.0 all-to-all-done.2
  61.2 5.3 %all-to-all-start.1 = ((f32[8,4,6,8,128]{4,3,2,1,0:T(8,128)}), f32[8,4,6,8,128]{4,3,2,1,0:T(8,128)S(1)}, u32[]{:S(2)}, u32[]{:S(2)}) async-start(f32[8,4,6,8,128]{4,3,2,1,0:T(8,128)} %bitcast.3), calls=%async_computation.1 | async-start | bytes 1572864 | tf_op jit(solution)/shard_map/all_to_all | solution.py:235
  66.5 5.3 %shard_map.73 = (f32[8,24576]{1,0:T(8,128)}, f32[8,128]{1,0:T(8,128)S(1)}) custom-call(f32[1536,128]{1,0:T(8,128)S(1)} %bitcast.6, f32[480,128]{1,0:T(8,128)S(1)} %collective-permute-done.3.refs_1_, f32[96,128]{1,0:T(8,128)S(1)} %get-tuple-element.15.refs_2_, f32[96,128]{1,0:T(8,128)S(1)} %collective-permute-done.4.refs_3_, ...), custom_call_target="tpu_custom_call" | custom-call | flops 2617245696 | bytes 2359296 | tf_op jit(solution)/shard_map/pallas_call | solution.py:264
  71.8 7.0 %all-to-all-done.1.y_ref = f32[8,4,6,8,128]{4,3,2,1,0:T(8,128)S(1)} async-done(((f32[8,4,6,8,128]{4,3,2,1,0:T(8,128)}), f32[8,4,6,8,128]{4,3,2,1,0:T(8,128)S(1)}, u32[]{:S(2)}, u32[]{:S(2)}) %all-to-all-start.1) | async-done | bytes 786464 | tf_op jit(solution)/shard_map/all_to_all | solution.py:235
  78.8 1.1 %shard_map.74 = f32[768,256]{1,0:T(8,128)} custom-call(f32[8,4,6,8,128]{4,3,2,1,0:T(8,128)S(1)} %all-to-all-done.1.y_ref, f32[8,128]{1,0:T(8,128)S(1)} %get-tuple-element.16.after_ref), custom_call_target="tpu_custom_call" | custom-call | bytes 1572864 | tf_op jit(solution)/shard_map/pallas_call | solution.py:267
Async XLA Ops:
  0.6 1.1 %copy-start = (f32[768,256]{1,0:T(8,128)S(1)}, f32[768,256]{1,0:T(8,128)}, u32[]{:S(2)}) copy-start(f32[768,256]{1,0:T(8,128)} %g_ref.1) | copy-start | bytes 2359300
  2.1 19.8 %collective-permute-start = (f32[8,6,8,128]{3,2,1,0:T(8,128)S(1)}, f32[8,6,8,128]{3,2,1,0:T(8,128)S(1)}, u32[]{:S(2)}, u32[]{:S(2)}) collective-permute-start(f32[8,6,8,128]{3,2,1,0:T(8,128)S(1)} %get-tuple-element.11), channel_id=1, source_target_pairs={{0,64},{64,128},{128,192},{192,0},{1,65},{65,129},{129,193},{193,1... | collective-permute-start | bytes 589832 | tf_op jit(solution)/shard_map/ppermute | solution.py:238
  6.0 16.6 %collective-permute-start.1 = (f32[8,6,8,128]{3,2,1,0:T(8,128)S(1)}, f32[8,6,8,128]{3,2,1,0:T(8,128)S(1)}, u32[]{:S(2)}, u32[]{:S(2)}) collective-permute-start(f32[8,6,8,128]{3,2,1,0:T(8,128)S(1)} %get-tuple-element.12), channel_id=1, source_target_pairs={{0,128},{64,192},{128,0},{192,64},{1,129},{65,193},{129,1},{193,65... | collective-permute-start | bytes 589832 | tf_op jit(solution)/shard_map/ppermute | solution.py:238
  11.1 18.6 %collective-permute-start.2 = (f32[8,6,8,128]{3,2,1,0:T(8,128)S(1)}, f32[8,6,8,128]{3,2,1,0:T(8,128)S(1)}, u32[]{:S(2)}, u32[]{:S(2)}) collective-permute-start(f32[8,6,8,128]{3,2,1,0:T(8,128)S(1)} %get-tuple-element.13), channel_id=1, source_target_pairs={{0,192},{64,0},{128,64},{192,128},{1,193},{65,1},{129,65},{193,129... | collective-permute-start | bytes 589832 | tf_op jit(solution)/shard_map/ppermute | solution.py:238
  15.9 19.7 %all-to-all-start = ((f32[8,4,7,8,128]{4,3,2,1,0:T(8,128)}), f32[8,4,7,8,128]{4,3,2,1,0:T(8,128)S(1)}, u32[]{:S(2)}, u32[]{:S(2)}) async-start(f32[8,4,7,8,128]{4,3,2,1,0:T(8,128)} %shard_map.68), calls=%async_computation | async-start | bytes 1835008 | tf_op jit(solution)/shard_map/all_to_all | solution.py:235
  35.7 15.1 %collective-permute-start.3 = (f32[480,128]{1,0:T(8,128)S(1)}, f32[480,128]{1,0:T(8,128)S(1)}, u32[]{:S(2)}, u32[]{:S(2)}) collective-permute-start(f32[480,128]{1,0:T(8,128)S(1)} %get-tuple-element.14), channel_id=1, source_target_pairs={{0,64},{64,128},{128,192},{192,0},{1,65},{65,129},{129,193},{193,1... | collective-permute-start | bytes 737288 | tf_op jit(solution)/shard_map/ppermute | solution.py:238
  35.8 9.5 %collective-permute-start.4 = (f32[96,128]{1,0:T(8,128)S(1)}, f32[96,128]{1,0:T(8,128)S(1)}, u32[]{:S(2)}, u32[]{:S(2)}) collective-permute-start(f32[96,128]{1,0:T(8,128)S(1)} %get-tuple-element.15.refs_2_), channel_id=1, source_target_pairs={{0,128},{64,192},{128,0},{192,64},{1,129},{65,193},{129,1},{193,65... | collective-permute-start | bytes 147464 | tf_op jit(solution)/shard_map/ppermute | solution.py:238
  37.6 8.9 %collective-permute-start.5 = (f32[96,128]{1,0:T(8,128)S(1)}, f32[96,128]{1,0:T(8,128)S(1)}, u32[]{:S(2)}, u32[]{:S(2)}) collective-permute-start(f32[96,128]{1,0:T(8,128)S(1)} %get-tuple-element.15.refs_2_), channel_id=1, source_target_pairs={{0,192},{64,0},{128,64},{192,128},{1,193},{65,1},{129,65},{193,129... | collective-permute-start | bytes 147464 | tf_op jit(solution)/shard_map/ppermute | solution.py:238
  40.1 21.2 %all-to-all-start.2 = ((f32[8,4,6,8,128]{4,3,2,1,0:T(8,128)}), f32[8,4,6,8,128]{4,3,2,1,0:T(8,128)S(1)}, u32[]{:S(2)}, u32[]{:S(2)}) async-start(f32[8,4,6,8,128]{4,3,2,1,0:T(8,128)} %shard_map.70.refs_1_), calls=%async_computation.2 | async-start | bytes 1572864 | tf_op jit(solution)/shard_map/all_to_all | solution.py:235
  61.2 17.6 %all-to-all-start.1 = ((f32[8,4,6,8,128]{4,3,2,1,0:T(8,128)}), f32[8,4,6,8,128]{4,3,2,1,0:T(8,128)S(1)}, u32[]{:S(2)}, u32[]{:S(2)}) async-start(f32[8,4,6,8,128]{4,3,2,1,0:T(8,128)} %bitcast.3), calls=%async_computation.1 | async-start | bytes 1572864 | tf_op jit(solution)/shard_map/all_to_all | solution.py:235

commit v4 on v1

--- a/solution.py
+++ b/solution.py
@@ -17,18 +17,30 @@
         out_ref[:, z, k, :, :] = part[z * step:(z + 1) * step].reshape(-1, SUBS, LANES)
 
 
-def pack_with_taps(x_ref, taps_ref, gain_ref, band_ref, out_ref):
+def pack_with_taps(x_ref, taps_ref, gain_ref, band_ref, *refs):
+    outs, held_ref = refs[:-1], refs[-1]
     block_len = x_ref.shape[0]
     tiles = block_len // LANES
     for k in range(tiles):
-        store_parts(out_ref, k, x_ref[k * LANES:(k + 1) * LANES, :].T)
+        store_parts(held_ref, k, x_ref[k * LANES:(k + 1) * LANES, :].T)
     rows, chans = taps_ref.shape
     place = lax.axis_index("far") * NEAR + lax.axis_index("near")
     lag = place * rows + lax.broadcasted_iota(jnp.int32, (rows, chans), 0)
     kept = jnp.where(lag < band_ref[...] * block_len, taps_ref[...], 0.0)
     kept = kept + jnp.where(lag == 0, gain_ref[...], 0.0)
     kept = jnp.concatenate([kept, jnp.zeros((LANES - rows, chans), jnp.float32)], axis=0)
-    store_parts(out_ref, tiles, kept.T)
+    store_parts(held_ref, tiles, kept.T)
+    for bits, out_ref in enumerate(outs):
+        out_ref[...] = held_ref[other(bits)]
+
+
+def other(bits):
+    return lax.axis_index("near") ^ bits
+
+
+def merge(parts, held_ref):
+    for bits, ref in enumerate(parts):
+        held_ref[other(bits)] = ref[...]
 
 
 def pack_plain(x_ref, out_ref):
@@ -37,9 +49,11 @@
         out_ref[:, k, :, :] = part.reshape(-1, SUBS, LANES)
 
 
-def unpack(y_ref, out_ref):
+def unpack(*refs):
+    parts, (out_ref, held_ref) = refs[:-2], refs[-2:]
+    merge(parts, held_ref)
     for k in range(out_ref.shape[0] // LANES):
-        part = jnp.concatenate([y_ref[:, z, k, :, :].reshape(-1, LANES) for z in range(y_ref.shape[1])], axis=0)
+        part = jnp.concatenate([held_ref[:, z, k, :, :].reshape(-1, LANES) for z in range(held_ref.shape[1])], axis=0)
         out_ref[k * LANES:(k + 1) * LANES, :] = part.T
 
 
@@ -48,7 +62,9 @@
     return high, (value - high.astype(jnp.float32)).astype(jnp.bfloat16)
 
 
-def collect(rows, halo_blocks, x_ref, halo_ref, taps_ref):
+def collect(rows, halo_blocks, *refs):
+    parts, (halo_ref, taps_ref, x_ref) = refs[:-3], refs[-3:]
+    merge(parts, x_ref)
     near, far, tiles = x_ref.shape[:3]
     tiles = tiles - 1
     lane = lax.broadcasted_iota(jnp.int32, (far * SUBS, LANES), 1)
@@ -101,11 +117,10 @@
     return jnp.concatenate([row_ref[t, pl.ds(chan, 1), :] for t in range(row_ref.shape[0])], axis=1)
 
 
-def forward(halo_blocks, tiles, x_ref, halo_ref, *refs):
-    others, (y_ref, row_ref, held_ref) = refs[:-3], refs[-3:]
-    far = len(others) + 1
+def forward(halo_blocks, tiles, near, far, *refs):
+    parts, halo_ref, others, outs = refs[:near], refs[near], refs[near + 1:near + far], refs[near + far:-3]
+    y_ref, row_ref, held_ref = refs[-3:]
     chans = far * SUBS
-    near = y_ref.shape[0] // (far * tiles * SUBS)
     chunk = far * (tiles + 1) * SUBS
     halo_rows = halo_blocks * far * tiles * SUBS
     pieces = [(others[0], 0), (halo_ref, halo_rows)] + [(ref, 0) for ref in others[1:]]
@@ -117,7 +132,9 @@
             target = block * chunk + z * (tiles + 1) * SUBS
             value = halo_ref[source:source + tiles * SUBS, :]
             held_ref[target:target + tiles * SUBS, :] = jnp.where(first, 0.0, value)
-    held_ref[halo_blocks * chunk:, :] = x_ref[...]
+    for bits, ref in enumerate(parts):
+        at = pl.multiple_of((halo_blocks + other(bits)) * chunk, SUBS)
+        held_ref[pl.ds(at, chunk), :] = ref[...].reshape(chunk, LANES)
     depth = row_ref.shape[0] - 1
 
     def one(chan, carry):
@@ -148,7 +165,11 @@
             y_ref[pl.ds((z * tiles + k) * SUBS + i, near, stride=far * tiles * SUBS), :] = value
         return carry
 
-    lax.fori_loop(0, chans, one, 0)
+    lax.fori_loop(0, chans, one, 0, unroll=8)
+    share = far * tiles * SUBS
+    for bits, ref in enumerate(outs):
+        at = pl.multiple_of(other(bits) * share, SUBS)
+        ref[...] = y_ref[pl.ds(at, share), :].reshape(ref.shape)
 
 
 def gradient(blocks, tiles, halo_rows, g_ref, halo_ref, *refs):
@@ -185,18 +206,20 @@
             held_ref[pl.ds(k * SUBS + chan, blocks, stride=chunk), :] = value
         return carry
 
-    lax.fori_loop(0, SUBS, one, 0)
+    lax.fori_loop(0, SUBS, one, 0, unroll=2)
     for tile in range(blocks * tiles):
         out_ref[:, tile * LANES:(tile + 1) * LANES] = held_ref[tile * SUBS:(tile + 1) * SUBS, :]
 
 
-def call(body, shapes, scratch=(), flops=0, moved=0):
+def call(body, shapes, scratch=(), flops=0, moved=0, operands=0, after=0, room=40):
+    specs = [pl.BlockSpec(memory_space=pltpu.VMEM)] * operands + [pl.BlockSpec(memory_space=pl.ANY)] * after
     shapes = [jax.ShapeDtypeStruct(shape, jnp.float32) for shape in shapes]
     return pl.pallas_call(
         body,
         out_shape=shapes if len(shapes) > 1 else shapes[0],
+        **({"in_specs": specs} if specs else {}),
         scratch_shapes=list(scratch),
-        compiler_params=pltpu.CompilerParams(vmem_limit_bytes=40 * 1024 * 1024),
+        compiler_params=pltpu.CompilerParams(vmem_limit_bytes=room * 1024 * 1024),
         cost_estimate=pl.CostEstimate(flops=flops, bytes_accessed=moved, transcendentals=0),
     )
 
@@ -212,38 +235,39 @@
     halo_blocks = rows * count // block_len
     size = block_len * chans * 4
 
-    def exchanged(value, axes):
-        return lax.all_to_all(value, axes, split_axis=0, concat_axis=0, tiled=True)
-
     def ahead(value, steps):
         return lax.ppermute(value, "far", [(z, (z + steps) % far) for z in range(far)])
 
-    sent_x = call(pack_with_taps, [(near, far, tiles + 1, SUBS, LANES)], moved=2 * size)(
-        inputs, filter_rows, skip_gain[None, :], band_blocks[None, :])
-    got_x = exchanged(sent_x, "near")
+    def swapped(parts):
+        pairs = [[(n, n ^ bits) for n in range(near)] for bits in range(near)]
+        return [lax.ppermute(part, "near", pairs[bits]) if bits else part for bits, part in enumerate(parts)]
+
+    share = (far, tiles + 1, SUBS, LANES)
+    got_x = swapped(call(pack_with_taps, [share] * near, [pltpu.VMEM((near, *share), jnp.float32)], moved=2 * size, room=60)(
+        inputs, filter_rows, skip_gain[None, :], band_blocks[None, :]))
     halo_rows = halo_blocks * far * tiles * SUBS
     own_taps = lag_tiles // far * far * SUBS
-    halo, taps = call(lambda *refs: collect(rows, halo_blocks, *refs),
-                      [(halo_rows + own_taps, LANES), (own_taps, LANES)], moved=size)(got_x)
+    halo, taps = call(lambda *refs: collect(rows, halo_blocks, *refs), [(halo_rows + own_taps, LANES), (own_taps, LANES)],
+                      [pltpu.VMEM((near, *share), jnp.float32)], moved=size)(*got_x)
     got_halo = ahead(halo, 1)
     pieces = [taps] + [ahead(taps, steps) for steps in range(2, far)]
+
     sent_g = call(pack_plain, [(count, tiles, SUBS, LANES)], moved=2 * size)(cotangent)
-    got_g = exchanged(sent_g, ("far", "near")).reshape(-1, LANES)
+    got_g = lax.all_to_all(sent_g, ("far", "near"), split_axis=0, concat_axis=0, tiled=True).reshape(-1, LANES)
 
     def row(height):
         return pltpu.VMEM((lag_tiles + 2, height, LANES), jnp.float32)
 
-    got_x = got_x.reshape(-1, LANES)
+    all_rows = pltpu.VMEM((count * tiles * SUBS, LANES), jnp.float32)
     held_rows = (near + halo_blocks) * far * (tiles + 1) * SUBS
     flops = 2 * far * SUBS * 2 * near * tiles * (lag_tiles + 1) * LANES * 2 * LANES
-    sent_y = call(lambda *refs: forward(halo_blocks, tiles, *refs), [(count * tiles * SUBS, LANES)],
-                  [row(far * SUBS), pltpu.VMEM((held_rows, LANES), jnp.float32)], 4 * flops, 2 * size)(
-        got_x, got_halo, *pieces)
-    got_y = exchanged(sent_y.reshape(near, far, tiles, SUBS, LANES), "near")
+    share = (far, tiles, SUBS, LANES)
+    got_y = swapped(call(lambda *refs: forward(halo_blocks, tiles, near, far, *refs), [share] * near,
+                         [all_rows, row(far * SUBS), pltpu.VMEM((held_rows, LANES), jnp.float32)], 40 * flops, 2 * size)(
+        *got_x, got_halo, *pieces))
     input_grad = call(lambda *refs: gradient(count, tiles, halo_rows, *refs), [(SUBS, count * block_len)],
-                      [row(SUBS), pltpu.VMEM((count * tiles * SUBS, LANES), jnp.float32)], flops, 3 * size)(
-        got_g, got_halo, *pieces)
-    outputs = call(unpack, [(block_len, chans)], moved=2 * size)(got_y)
+                      [row(SUBS), all_rows], flops, 3 * size)(got_g, got_halo, *pieces)
+    outputs = call(unpack, [(block_len, chans)], [pltpu.VMEM((near, *share), jnp.float32)], moved=2 * size)(*got_y)
     return outputs, input_grad
 
 

time: 105 us -> 78.4 us (0.75)
  waiting for transfers between devices: 39.3 us -> 20.2 us
  Pallas kernels: 27.2 us -> 19.8 us
  local copies, waits for them, and re-layouts: 2.61 us -> 0.91 us
  starting transfers between devices: 35.1 us -> 36.5 us
    ppermute x0 -> x14, starting transfers between devices: none -> 22.4 us  [swapped(): lax.ppermute(part, 'near', pairs[bits])]
    all_to_all x3 -> x1, starting transfers between devices: 26.2 us -> 4.91 us  [local(): lax.all_to_all(sent_g, ('far', 'near'), split_axis=0, concat_axis=0, tile...]
    ppermute x3, waiting for transfers between devices: 21.1 us -> 0.61 us  [ahead(): lax.ppermute(value, 'far', [(z, (z + steps) % far) for z in range(far)])]
    ppermute x0 -> x14, waiting for transfers between devices: none -> 19.5 us  [swapped(): lax.ppermute(part, 'near', pairs[bits])]
    all_to_all x3 -> x1, waiting for transfers between devices: 18.2 us -> 0.01 us  [local(): lax.all_to_all(sent_g, ('far', 'near'), split_axis=0, concat_axis=0, tile...]
    pallas_call x3, Pallas kernels: 19.3 us -> 13.3 us  [the longest x1 9.61 us: local(): call(lambda *refs: forward(halo_blocks, tiles, near, far, *refs), [share]...]
    unnamed x10 -> x6, local copies, waits for them, and re-layouts: 2.61 us -> 0.91 us
    pallas_call x1, Pallas kernels: 6.63 us -> 5.23 us  [local(): call(lambda *refs: gradient(count, tiles, halo_rows, *refs), [(SUBS, coun...]
  transfers between devices with their start and end apart: 6 -> 18, of which waited for: 3 -> 11; matrix products, arithmetic and copies ran while one was open for 0% -> 0% of each run, Pallas kernels for 24% -> 15%
where the time goes in v4:
time: 78.4 us; the launch traced here: 78.1 us
  starting transfers between devices  36.5 us (47%)
  waiting for transfers between devices  20.2 us (26%)
  Pallas kernels  19.8 us (25%)
  local copies, waits for them, and re-layouts  0.91 us (1%)
    ppermute x14, starting transfers between devices, swapped(): lax.ppermute(part, 'near', pairs[bits])  22.4 us
    ppermute x14, waiting for transfers between devices, swapped(): lax.ppermute(part, 'near', pairs[bits])  19.5 us
    pallas_call x1, Pallas kernels, local(): call(lambda *refs: forward(halo_blocks, tiles, near, far, *refs), [share]...  9.61 us
    ppermute x3, starting transfers between devices, ahead(): lax.ppermute(value, 'far', [(z, (z + steps) % far) for z in range(far)])  9.22 us
    pallas_call x1, Pallas kernels, local(): call(lambda *refs: gradient(count, tiles, halo_rows, *refs), [(SUBS, coun...  5.23 us
    all_to_all x1, starting transfers between devices, local(): lax.all_to_all(sent_g, ('far', 'near'), split_axis=0, concat_axis=0, tile...  4.91 us
    pallas_call x1, Pallas kernels, local(): call(pack_with_taps, [share] * near, [pltpu.VMEM((near, *share), jnp.floa...  2.47 us
  transfers between devices with their start and end apart: 18, of which 11 were waited for; matrix products, arithmetic and copies ran while one was open for 0% of the time, Pallas kernels for 15%

profile of v4, /device:TPU:1, one launch (start us, length us, event | category | flops | bytes accessed | tf_op | source)
XLA Modules:
  0.0 78.1 jit_solution(9483613968887598945)
XLA Ops:
  0.6 0.0 copy-start
  0.6 2.5 %shard_map.68 = (f32[4,7,8,128]{3,2,1,0:T(8,128)}, f32[4,7,8,128]{3,2,1,0:T(8,128)}, f32[4,7,8,128]{3,2,1,0:T(8,128)}, f32[4,7,8,128]{3,2,1,0:T(8,128)}, f32[4,7...) custom-call(f32[768,256]{1,0:T(8,128)} %x_ref.2, ...), custom_call_target="tpu_custom_call" | custom-call | bytes 1572864 | tf_op jit(solution)/shard_map/pallas_call | solution.py:246
  3.1 3.2 %collective-permute-start = (f32[4,7,8,128]{3,2,1,0:T(8,128)}, f32[4,7,8,128]{3,2,1,0:T(8,128)S(1)}, u32[]{:S(2)}, u32[]{:S(2)}) collective-permute-start(f32[4,7,8,128]{3,2,1,0:T(8,128)} %get-tuple-element.21), channel_id=1, source_target_pairs={{0,8},{8,0},{16,24},{24,16},{32,40},{40,32},{48,56},{56,48},{1,9},... | collective-permute-start | bytes 344072 | tf_op jit(solution)/shard_map/ppermute | solution.py:243
  6.4 0.0 collective-permute-start.1
  6.4 1.7 %collective-permute-start.2 = (f32[4,7,8,128]{3,2,1,0:T(8,128)}, f32[4,7,8,128]{3,2,1,0:T(8,128)S(1)}, u32[]{:S(2)}, u32[]{:S(2)}) collective-permute-start(f32[4,7,8,128]{3,2,1,0:T(8,128)} %get-tuple-element.23), channel_id=1, source_target_pairs={{0,24},{8,16},{16,8},{24,0},{32,56},{40,48},{48,40},{56,32},{1,25}... | collective-permute-start | bytes 344072 | tf_op jit(solution)/shard_map/ppermute | solution.py:243
  8.0 1.2 %collective-permute-start.3 = (f32[4,7,8,128]{3,2,1,0:T(8,128)}, f32[4,7,8,128]{3,2,1,0:T(8,128)S(1)}, u32[]{:S(2)}, u32[]{:S(2)}) collective-permute-start(f32[4,7,8,128]{3,2,1,0:T(8,128)} %get-tuple-element.24), channel_id=1, source_target_pairs={{0,32},{8,40},{16,48},{24,56},{32,0},{40,8},{48,16},{56,24},{1,33}... | collective-permute-start | bytes 344072 | tf_op jit(solution)/shard_map/ppermute | solution.py:243
  9.2 2.1 %collective-permute-start.4 = (f32[4,7,8,128]{3,2,1,0:T(8,128)}, f32[4,7,8,128]{3,2,1,0:T(8,128)S(1)}, u32[]{:S(2)}, u32[]{:S(2)}) collective-permute-start(f32[4,7,8,128]{3,2,1,0:T(8,128)} %get-tuple-element.25), channel_id=1, source_target_pairs={{0,40},{8,32},{16,56},{24,48},{32,8},{40,0},{48,24},{56,16},{1,41}... | collective-permute-start | bytes 344072 | tf_op jit(solution)/shard_map/ppermute | solution.py:243
  11.4 0.0 collective-permute-done.refs_1_
  11.4 1.0 %collective-permute-start.5 = (f32[4,7,8,128]{3,2,1,0:T(8,128)}, f32[4,7,8,128]{3,2,1,0:T(8,128)S(1)}, u32[]{:S(2)}, u32[]{:S(2)}) collective-permute-start(f32[4,7,8,128]{3,2,1,0:T(8,128)} %get-tuple-element.26), channel_id=1, source_target_pairs={{0,48},{8,56},{16,32},{24,40},{32,16},{40,24},{48,0},{56,8},{1,49}... | collective-permute-start | bytes 344072 | tf_op jit(solution)/shard_map/ppermute | solution.py:243
  12.4 0.0 collective-permute-done.1.refs_2_
  12.4 1.9 %collective-permute-start.6 = (f32[4,7,8,128]{3,2,1,0:T(8,128)}, f32[4,7,8,128]{3,2,1,0:T(8,128)S(1)}, u32[]{:S(2)}, u32[]{:S(2)}) collective-permute-start(f32[4,7,8,128]{3,2,1,0:T(8,128)} %get-tuple-element.27), channel_id=1, source_target_pairs={{0,56},{8,48},{16,40},{24,32},{32,24},{40,16},{48,8},{56,0},{1,57}... | collective-permute-start | bytes 344072 | tf_op jit(solution)/shard_map/ppermute | solution.py:243
  14.3 0.1 collective-permute-done.2.refs_3_
  14.3 2.6 %collective-permute-done.3.refs_4_ = f32[4,7,8,128]{3,2,1,0:T(8,128)S(1)} collective-permute-done((f32[4,7,8,128]{3,2,1,0:T(8,128)}, f32[4,7,8,128]{3,2,1,0:T(8,128)S(1)}, u32[]{:S(2)}, u32[]{:S(2)}) %collective-permute-start.3) | collective-permute-done | bytes 114720 | tf_op jit(solution)/shard_map/ppermute | solution.py:243
  16.9 2.7 %collective-permute-done.4.refs_5_ = f32[4,7,8,128]{3,2,1,0:T(8,128)S(1)} collective-permute-done((f32[4,7,8,128]{3,2,1,0:T(8,128)}, f32[4,7,8,128]{3,2,1,0:T(8,128)S(1)}, u32[]{:S(2)}, u32[]{:S(2)}) %collective-permute-start.4) | collective-permute-done | bytes 114720 | tf_op jit(solution)/shard_map/ppermute | solution.py:243
  19.6 2.6 %collective-permute-done.5.refs_6_ = f32[4,7,8,128]{3,2,1,0:T(8,128)S(1)} collective-permute-done((f32[4,7,8,128]{3,2,1,0:T(8,128)}, f32[4,7,8,128]{3,2,1,0:T(8,128)S(1)}, u32[]{:S(2)}, u32[]{:S(2)}) %collective-permute-start.5) | collective-permute-done | bytes 114720 | tf_op jit(solution)/shard_map/ppermute | solution.py:243
  22.2 2.5 %collective-permute-done.6.refs_7_ = f32[4,7,8,128]{3,2,1,0:T(8,128)S(1)} collective-permute-done((f32[4,7,8,128]{3,2,1,0:T(8,128)}, f32[4,7,8,128]{3,2,1,0:T(8,128)S(1)}, u32[]{:S(2)}, u32[]{:S(2)}) %collective-permute-start.6) | collective-permute-done | bytes 114720 | tf_op jit(solution)/shard_map/ppermute | solution.py:243
  24.7 0.0 copy-start.1
  24.7 0.9 %copy-done.1 = f32[4,7,8,128]{3,2,1,0:T(8,128)S(1)} copy-done((f32[4,7,8,128]{3,2,1,0:T(8,128)S(1)}, f32[4,7,8,128]{3,2,1,0:T(8,128)}, u32[]{:S(2)}) %copy-start.1) | copy-done | bytes 114712
  25.6 0.2 shard_map.69
  25.8 1.7 %collective-permute-start.7 = (f32[480,128]{1,0:T(8,128)S(1)}, f32[480,128]{1,0:T(8,128)S(1)}, u32[]{:S(2)}, u32[]{:S(2)}) collective-permute-start(f32[480,128]{1,0:T(8,128)S(1)} %get-tuple-element.28), channel_id=1, source_target_pairs={{0,64},{64,128},{128,192},{192,0},{1,65},{65,129},{129,193},{193,1... | collective-permute-start | bytes 737288 | tf_op jit(solution)/shard_map/ppermute | solution.py:239
  27.5 5.1 %collective-permute-start.8 = (f32[96,128]{1,0:T(8,128)S(1)}, f32[96,128]{1,0:T(8,128)S(1)}, u32[]{:S(2)}, u32[]{:S(2)}) collective-permute-start(f32[96,128]{1,0:T(8,128)S(1)} %get-tuple-element.29.refs_9_.refs_2_), channel_id=1, source_target_pairs={{0,128},{64,192},{128,0},{192,64},{1,129},{65,193},{129,1},{193,65... | collective-permute-start | bytes 147464 | tf_op jit(solution)/shard_map/ppermute | solution.py:239
  32.6 2.4 %collective-permute-start.9 = (f32[96,128]{1,0:T(8,128)S(1)}, f32[96,128]{1,0:T(8,128)S(1)}, u32[]{:S(2)}, u32[]{:S(2)}) collective-permute-start(f32[96,128]{1,0:T(8,128)S(1)} %get-tuple-element.29.refs_9_.refs_2_), channel_id=1, source_target_pairs={{0,192},{64,0},{128,64},{192,128},{1,193},{65,1},{129,65},{193,129... | collective-permute-start | bytes 147464 | tf_op jit(solution)/shard_map/ppermute | solution.py:239
  35.0 0.0 copy-done
  35.0 1.1 %shard_map.72 = f32[32,6,8,128]{3,2,1,0:T(8,128)} custom-call(f32[768,256]{1,0:T(8,128)S(1)} %copy-done), custom_call_target="tpu_custom_call" | custom-call | bytes 1572864 | tf_op jit(solution)/shard_map/pallas_call | solution.py:255
  36.1 0.0 copy-start.2
  36.1 4.9 %all-to-all-start = ((f32[32,6,8,128]{3,2,1,0:T(8,128)}), f32[32,6,8,128]{3,2,1,0:T(8,128)S(1)}, u32[]{:S(2)}, u32[]{:S(2)}) async-start(f32[32,6,8,128]{3,2,1,0:T(8,128)} %shard_map.72), calls=%async_computation | async-start | bytes 1572864 | tf_op jit(solution)/shard_map/all_to_all | solution.py:256
  41.1 0.6 collective-permute-done.8.refs_10_.refs_3_
  41.7 0.0 collective-permute-done.9.refs_11_.refs_4_
  41.7 0.0 collective-permute-done.7.refs_8_.refs_1_
  41.7 0.0 copy-done.2
  41.7 9.6 %shard_map.70 = (f32[4,6,8,128]{3,2,1,0:T(8,128)S(1)}, f32[4,6,8,128]{3,2,1,0:T(8,128)S(1)}, f32[4,6,8,128]{3,2,1,0:T(8,128)S(1)}, f32[4,6,8,128]{3,2,1,0:T(8,12...) custom-call(f32[4,7,8,128]{3,2,1,0:T(8,128)S(1)} %copy-done.2, ...), custom_call_target="tpu_custom_call" | custom-call | flops 104689827840 | bytes 1572864 | tf_op jit(solution)/shard_map/pallas_call | solution.py:265
  51.3 3.2 %collective-permute-start.10 = (f32[4,6,8,128]{3,2,1,0:T(8,128)S(1)}, f32[4,6,8,128]{3,2,1,0:T(8,128)S(1)}, u32[]{:S(2)}, u32[]{:S(2)}) collective-permute-start(f32[4,6,8,128]{3,2,1,0:T(8,128)S(1)} %get-tuple-element.31), channel_id=1, source_target_pairs={{0,8},{8,0},{16,24},{24,16},{32,40},{40,32},{48,56},{56,48},{1,9},... | collective-permute-start | bytes 294920 | tf_op jit(solution)/shard_map/ppermute | solution.py:243
  54.5 0.0 collective-permute-start.11
  54.5 1.7 %collective-permute-start.12 = (f32[4,6,8,128]{3,2,1,0:T(8,128)S(1)}, f32[4,6,8,128]{3,2,1,0:T(8,128)S(1)}, u32[]{:S(2)}, u32[]{:S(2)}) collective-permute-start(f32[4,6,8,128]{3,2,1,0:T(8,128)S(1)} %get-tuple-element.33), channel_id=1, source_target_pairs={{0,24},{8,16},{16,8},{24,0},{32,56},{40,48},{48,40},{56,32},{1,25}... | collective-permute-start | bytes 294920 | tf_op jit(solution)/shard_map/ppermute | solution.py:243
  56.2 1.2 %collective-permute-start.13 = (f32[4,6,8,128]{3,2,1,0:T(8,128)S(1)}, f32[4,6,8,128]{3,2,1,0:T(8,128)S(1)}, u32[]{:S(2)}, u32[]{:S(2)}) collective-permute-start(f32[4,6,8,128]{3,2,1,0:T(8,128)S(1)} %get-tuple-element.34), channel_id=1, source_target_pairs={{0,32},{8,40},{16,48},{24,56},{32,0},{40,8},{48,16},{56,24},{1,33}... | collective-permute-start | bytes 294920 | tf_op jit(solution)/shard_map/ppermute | solution.py:243
  57.4 2.1 %collective-permute-start.14 = (f32[4,6,8,128]{3,2,1,0:T(8,128)S(1)}, f32[4,6,8,128]{3,2,1,0:T(8,128)S(1)}, u32[]{:S(2)}, u32[]{:S(2)}) collective-permute-start(f32[4,6,8,128]{3,2,1,0:T(8,128)S(1)} %get-tuple-element.35), channel_id=1, source_target_pairs={{0,40},{8,32},{16,56},{24,48},{32,8},{40,0},{48,24},{56,16},{1,41}... | collective-permute-start | bytes 294920 | tf_op jit(solution)/shard_map/ppermute | solution.py:243
  59.5 0.0 collective-permute-done.10.refs_1_
  59.5 1.1 %collective-permute-start.15 = (f32[4,6,8,128]{3,2,1,0:T(8,128)S(1)}, f32[4,6,8,128]{3,2,1,0:T(8,128)S(1)}, u32[]{:S(2)}, u32[]{:S(2)}) collective-permute-start(f32[4,6,8,128]{3,2,1,0:T(8,128)S(1)} %get-tuple-element.36), channel_id=1, source_target_pairs={{0,48},{8,56},{16,32},{24,40},{32,16},{40,24},{48,0},{56,8},{1,49}... | collective-permute-start | bytes 294920 | tf_op jit(solution)/shard_map/ppermute | solution.py:243
  60.6 0.0 collective-permute-done.11.refs_2_
  60.6 2.0 %collective-permute-start.16 = (f32[4,6,8,128]{3,2,1,0:T(8,128)S(1)}, f32[4,6,8,128]{3,2,1,0:T(8,128)S(1)}, u32[]{:S(2)}, u32[]{:S(2)}) collective-permute-start(f32[4,6,8,128]{3,2,1,0:T(8,128)S(1)} %get-tuple-element.37), channel_id=1, source_target_pairs={{0,56},{8,48},{16,40},{24,32},{32,24},{40,16},{48,8},{56,0},{1,57}... | collective-permute-start | bytes 294920 | tf_op jit(solution)/shard_map/ppermute | solution.py:243
  62.6 1.1 %collective-permute-done.12.refs_3_ = f32[4,6,8,128]{3,2,1,0:T(8,128)S(1)} collective-permute-done((f32[4,6,8,128]{3,2,1,0:T(8,128)S(1)}, f32[4,6,8,128]{3,2,1,0:T(8,128)S(1)}, u32[]{:S(2)}, u32[]{:S(2)}) %collective-permute-start.12) | collective-permute-done | bytes 98336 | tf_op jit(solution)/shard_map/ppermute | solution.py:243
  63.7 2.6 %collective-permute-done.13.refs_4_ = f32[4,6,8,128]{3,2,1,0:T(8,128)S(1)} collective-permute-done((f32[4,6,8,128]{3,2,1,0:T(8,128)S(1)}, f32[4,6,8,128]{3,2,1,0:T(8,128)S(1)}, u32[]{:S(2)}, u32[]{:S(2)}) %collective-permute-start.13) | collective-permute-done | bytes 98336 | tf_op jit(solution)/shard_map/ppermute | solution.py:243
  66.3 2.3 %collective-permute-done.14.refs_5_ = f32[4,6,8,128]{3,2,1,0:T(8,128)S(1)} collective-permute-done((f32[4,6,8,128]{3,2,1,0:T(8,128)S(1)}, f32[4,6,8,128]{3,2,1,0:T(8,128)S(1)}, u32[]{:S(2)}, u32[]{:S(2)}) %collective-permute-start.14) | collective-permute-done | bytes 98336 | tf_op jit(solution)/shard_map/ppermute | solution.py:243
  68.7 0.9 %collective-permute-done.15.refs_6_ = f32[4,6,8,128]{3,2,1,0:T(8,128)S(1)} collective-permute-done((f32[4,6,8,128]{3,2,1,0:T(8,128)S(1)}, f32[4,6,8,128]{3,2,1,0:T(8,128)S(1)}, u32[]{:S(2)}, u32[]{:S(2)}) %collective-permute-start.15) | collective-permute-done | bytes 98336 | tf_op jit(solution)/shard_map/ppermute | solution.py:243
  69.5 2.1 %collective-permute-done.16.refs_7_ = f32[4,6,8,128]{3,2,1,0:T(8,128)S(1)} collective-permute-done((f32[4,6,8,128]{3,2,1,0:T(8,128)S(1)}, f32[4,6,8,128]{3,2,1,0:T(8,128)S(1)}, u32[]{:S(2)}, u32[]{:S(2)}) %collective-permute-start.16) | collective-permute-done | bytes 98336 | tf_op jit(solution)/shard_map/ppermute | solution.py:243
  71.7 1.2 %shard_map.71 = f32[768,256]{1,0:T(8,128)} custom-call(f32[4,6,8,128]{3,2,1,0:T(8,128)S(1)} %get-tuple-element.30.refs_0_, f32[4,6,8,128]{3,2,1,0:T(8,128)S(1)} %collective-permute-done.10.refs_1_, f32[4,6,8,128]{3,2,1,0:T(8,128)S(1)} %collective-permute-done.11.refs_2_, f32[4,6,8,128]{3,2,1,0:T(8,128)S(1)} %collective-permute-done.12.refs_3_, ...), custom_call_target="tpu_custom_call" | custom-call | bytes 1572864 | tf_op jit(solution)/shard_map/pallas_call | solution.py:270
  72.9 0.0 all-to-all-done
  72.9 5.2 %shard_map.73 = f32[8,24576]{1,0:T(8,128)} custom-call(f32[1536,128]{1,0:T(8,128)S(1)} %bitcast.3, f32[480,128]{1,0:T(8,128)S(1)} %collective-permute-done.7.refs_8_.refs_1_, f32[96,128]{1,0:T(8,128)S(1)} %get-tuple-element.29.refs_9_.refs_2_, f32[96,128]{1,0:T(8,128)S(1)} %collective-permute-done.8.refs_10_.refs_3_, ...), custom_call_target="tpu_custom_call" | custom-call | flops 2617245696 | bytes 2359296 | tf_op jit(solution)/shard_map/pallas_call | solution.py:268
Async XLA Ops:
  0.6 34.4 %copy-start = (f32[768,256]{1,0:T(8,128)S(1)}, f32[768,256]{1,0:T(8,128)}, u32[]{:S(2)}) copy-start(f32[768,256]{1,0:T(8,128)} %x_ref.3) | copy-start | bytes 2359300
  3.1 8.2 %collective-permute-start = (f32[4,7,8,128]{3,2,1,0:T(8,128)}, f32[4,7,8,128]{3,2,1,0:T(8,128)S(1)}, u32[]{:S(2)}, u32[]{:S(2)}) collective-permute-start(f32[4,7,8,128]{3,2,1,0:T(8,128)} %get-tuple-element.21), channel_id=1, source_target_pairs={{0,8},{8,0},{16,24},{24,16},{32,40},{40,32},{48,56},{56,48},{1,9},... | collective-permute-start | bytes 344072 | tf_op jit(solution)/shard_map/ppermute | solution.py:243
  6.4 6.0 %collective-permute-start.1 = (f32[4,7,8,128]{3,2,1,0:T(8,128)}, f32[4,7,8,128]{3,2,1,0:T(8,128)S(1)}, u32[]{:S(2)}, u32[]{:S(2)}) collective-permute-start(f32[4,7,8,128]{3,2,1,0:T(8,128)} %get-tuple-element.22), channel_id=1, source_target_pairs={{0,16},{8,24},{16,0},{24,8},{32,48},{40,56},{48,32},{56,40},{1,17}... | collective-permute-start | bytes 344072 | tf_op jit(solution)/shard_map/ppermute | solution.py:243
  6.4 8.0 %collective-permute-start.2 = (f32[4,7,8,128]{3,2,1,0:T(8,128)}, f32[4,7,8,128]{3,2,1,0:T(8,128)S(1)}, u32[]{:S(2)}, u32[]{:S(2)}) collective-permute-start(f32[4,7,8,128]{3,2,1,0:T(8,128)} %get-tuple-element.23), channel_id=1, source_target_pairs={{0,24},{8,16},{16,8},{24,0},{32,56},{40,48},{48,40},{56,32},{1,25}... | collective-permute-start | bytes 344072 | tf_op jit(solution)/shard_map/ppermute | solution.py:243
  8.0 8.9 %collective-permute-start.3 = (f32[4,7,8,128]{3,2,1,0:T(8,128)}, f32[4,7,8,128]{3,2,1,0:T(8,128)S(1)}, u32[]{:S(2)}, u32[]{:S(2)}) collective-permute-start(f32[4,7,8,128]{3,2,1,0:T(8,128)} %get-tuple-element.24), channel_id=1, source_target_pairs={{0,32},{8,40},{16,48},{24,56},{32,0},{40,8},{48,16},{56,24},{1,33}... | collective-permute-start | bytes 344072 | tf_op jit(solution)/shard_map/ppermute | solution.py:243
  9.2 10.4 %collective-permute-start.4 = (f32[4,7,8,128]{3,2,1,0:T(8,128)}, f32[4,7,8,128]{3,2,1,0:T(8,128)S(1)}, u32[]{:S(2)}, u32[]{:S(2)}) collective-permute-start(f32[4,7,8,128]{3,2,1,0:T(8,128)} %get-tuple-element.25), channel_id=1, source_target_pairs={{0,40},{8,32},{16,56},{24,48},{32,8},{40,0},{48,24},{56,16},{1,41}... | collective-permute-start | bytes 344072 | tf_op jit(solution)/shard_map/ppermute | solution.py:243
  11.4 10.9 %collective-permute-start.5 = (f32[4,7,8,128]{3,2,1,0:T(8,128)}, f32[4,7,8,128]{3,2,1,0:T(8,128)S(1)}, u32[]{:S(2)}, u32[]{:S(2)}) collective-permute-start(f32[4,7,8,128]{3,2,1,0:T(8,128)} %get-tuple-element.26), channel_id=1, source_target_pairs={{0,48},{8,56},{16,32},{24,40},{32,16},{40,24},{48,0},{56,8},{1,49}... | collective-permute-start | bytes 344072 | tf_op jit(solution)/shard_map/ppermute | solution.py:243
  12.4 12.3 %collective-permute-start.6 = (f32[4,7,8,128]{3,2,1,0:T(8,128)}, f32[4,7,8,128]{3,2,1,0:T(8,128)S(1)}, u32[]{:S(2)}, u32[]{:S(2)}) collective-permute-start(f32[4,7,8,128]{3,2,1,0:T(8,128)} %get-tuple-element.27), channel_id=1, source_target_pairs={{0,56},{8,48},{16,40},{24,32},{32,24},{40,16},{48,8},{56,0},{1,57}... | collective-permute-start | bytes 344072 | tf_op jit(solution)/shard_map/ppermute | solution.py:243
  24.7 0.9 %copy-start.1 = (f32[4,7,8,128]{3,2,1,0:T(8,128)S(1)}, f32[4,7,8,128]{3,2,1,0:T(8,128)}, u32[]{:S(2)}) copy-start(f32[4,7,8,128]{3,2,1,0:T(8,128)} %get-tuple-element.20.refs_0_) | copy-start | bytes 344068
  25.8 15.9 %collective-permute-start.7 = (f32[480,128]{1,0:T(8,128)S(1)}, f32[480,128]{1,0:T(8,128)S(1)}, u32[]{:S(2)}, u32[]{:S(2)}) collective-permute-start(f32[480,128]{1,0:T(8,128)S(1)} %get-tuple-element.28), channel_id=1, source_target_pairs={{0,64},{64,128},{128,192},{192,0},{1,65},{65,129},{129,193},{193,1... | collective-permute-start | bytes 737288 | tf_op jit(solution)/shard_map/ppermute | solution.py:239
  27.5 14.2 %collective-permute-start.8 = (f32[96,128]{1,0:T(8,128)S(1)}, f32[96,128]{1,0:T(8,128)S(1)}, u32[]{:S(2)}, u32[]{:S(2)}) collective-permute-start(f32[96,128]{1,0:T(8,128)S(1)} %get-tuple-element.29.refs_9_.refs_2_), channel_id=1, source_target_pairs={{0,128},{64,192},{128,0},{192,64},{1,129},{65,193},{129,1},{193,65... | collective-permute-start | bytes 147464 | tf_op jit(solution)/shard_map/ppermute | solution.py:239
  32.6 9.1 %collective-permute-start.9 = (f32[96,128]{1,0:T(8,128)S(1)}, f32[96,128]{1,0:T(8,128)S(1)}, u32[]{:S(2)}, u32[]{:S(2)}) collective-permute-start(f32[96,128]{1,0:T(8,128)S(1)} %get-tuple-element.29.refs_9_.refs_2_), channel_id=1, source_target_pairs={{0,192},{64,0},{128,64},{192,128},{1,193},{65,1},{129,65},{193,129... | collective-permute-start | bytes 147464 | tf_op jit(solution)/shard_map/ppermute | solution.py:239
  36.1 5.5 %copy-start.2 = (f32[4,7,8,128]{3,2,1,0:T(8,128)S(1)}, f32[4,7,8,128]{3,2,1,0:T(8,128)}, u32[]{:S(2)}) copy-start(f32[4,7,8,128]{3,2,1,0:T(8,128)} %get-tuple-element.20.refs_0_) | copy-start | bytes 344068
  36.1 36.8 %all-to-all-start = ((f32[32,6,8,128]{3,2,1,0:T(8,128)}), f32[32,6,8,128]{3,2,1,0:T(8,128)S(1)}, u32[]{:S(2)}, u32[]{:S(2)}) async-start(f32[32,6,8,128]{3,2,1,0:T(8,128)} %shard_map.72), calls=%async_computation | async-start | bytes 1572864 | tf_op jit(solution)/shard_map/all_to_all | solution.py:256
  51.3 8.2 %collective-permute-start.10 = (f32[4,6,8,128]{3,2,1,0:T(8,128)S(1)}, f32[4,6,8,128]{3,2,1,0:T(8,128)S(1)}, u32[]{:S(2)}, u32[]{:S(2)}) collective-permute-start(f32[4,6,8,128]{3,2,1,0:T(8,128)S(1)} %get-tuple-element.31), channel_id=1, source_target_pairs={{0,8},{8,0},{16,24},{24,16},{32,40},{40,32},{48,56},{56,48},{1,9},... | collective-permute-start | bytes 294920 | tf_op jit(solution)/shard_map/ppermute | solution.py:243
  54.5 6.1 %collective-permute-start.11 = (f32[4,6,8,128]{3,2,1,0:T(8,128)S(1)}, f32[4,6,8,128]{3,2,1,0:T(8,128)S(1)}, u32[]{:S(2)}, u32[]{:S(2)}) collective-permute-start(f32[4,6,8,128]{3,2,1,0:T(8,128)S(1)} %get-tuple-element.32), channel_id=1, source_target_pairs={{0,16},{8,24},{16,0},{24,8},{32,48},{40,56},{48,32},{56,40},{1,17}... | collective-permute-start | bytes 294920 | tf_op jit(solution)/shard_map/ppermute | solution.py:243
  54.5 9.2 %collective-permute-start.12 = (f32[4,6,8,128]{3,2,1,0:T(8,128)S(1)}, f32[4,6,8,128]{3,2,1,0:T(8,128)S(1)}, u32[]{:S(2)}, u32[]{:S(2)}) collective-permute-start(f32[4,6,8,128]{3,2,1,0:T(8,128)S(1)} %get-tuple-element.33), channel_id=1, source_target_pairs={{0,24},{8,16},{16,8},{24,0},{32,56},{40,48},{48,40},{56,32},{1,25}... | collective-permute-start | bytes 294920 | tf_op jit(solution)/shard_map/ppermute | solution.py:243
  56.2 10.1 %collective-permute-start.13 = (f32[4,6,8,128]{3,2,1,0:T(8,128)S(1)}, f32[4,6,8,128]{3,2,1,0:T(8,128)S(1)}, u32[]{:S(2)}, u32[]{:S(2)}) collective-permute-start(f32[4,6,8,128]{3,2,1,0:T(8,128)S(1)} %get-tuple-element.34), channel_id=1, source_target_pairs={{0,32},{8,40},{16,48},{24,56},{32,0},{40,8},{48,16},{56,24},{1,33}... | collective-permute-start | bytes 294920 | tf_op jit(solution)/shard_map/ppermute | solution.py:243
  57.4 11.3 %collective-permute-start.14 = (f32[4,6,8,128]{3,2,1,0:T(8,128)S(1)}, f32[4,6,8,128]{3,2,1,0:T(8,128)S(1)}, u32[]{:S(2)}, u32[]{:S(2)}) collective-permute-start(f32[4,6,8,128]{3,2,1,0:T(8,128)S(1)} %get-tuple-element.35), channel_id=1, source_target_pairs={{0,40},{8,32},{16,56},{24,48},{32,8},{40,0},{48,24},{56,16},{1,41}... | collective-permute-start | bytes 294920 | tf_op jit(solution)/shard_map/ppermute | solution.py:243
  59.5 10.0 %collective-permute-start.15 = (f32[4,6,8,128]{3,2,1,0:T(8,128)S(1)}, f32[4,6,8,128]{3,2,1,0:T(8,128)S(1)}, u32[]{:S(2)}, u32[]{:S(2)}) collective-permute-start(f32[4,6,8,128]{3,2,1,0:T(8,128)S(1)} %get-tuple-element.36), channel_id=1, source_target_pairs={{0,48},{8,56},{16,32},{24,40},{32,16},{40,24},{48,0},{56,8},{1,49}... | collective-permute-start | bytes 294920 | tf_op jit(solution)/shard_map/ppermute | solution.py:243
  60.6 11.1 %collective-permute-start.16 = (f32[4,6,8,128]{3,2,1,0:T(8,128)S(1)}, f32[4,6,8,128]{3,2,1,0:T(8,128)S(1)}, u32[]{:S(2)}, u32[]{:S(2)}) collective-permute-start(f32[4,6,8,128]{3,2,1,0:T(8,128)S(1)} %get-tuple-element.37), channel_id=1, source_target_pairs={{0,56},{8,48},{16,40},{24,32},{32,24},{40,16},{48,8},{56,0},{1,57}... | collective-permute-start | bytes 294920 | tf_op jit(solution)/shard_map/ppermute | solution.py:243

commit v5 on v4

--- a/solution.py
+++ b/solution.py
@@ -8,29 +8,30 @@
 LANES = 128
 SUBS = 8
 NEAR = 8
-
-
-def store_parts(out_ref, k, part):
-    far = out_ref.shape[1]
-    step = part.shape[0] // far
-    for z in range(far):
-        out_ref[:, z, k, :, :] = part[z * step:(z + 1) * step].reshape(-1, SUBS, LANES)
+ORDER = (0, 4, 5, 2, 6, 3, 7, 1)
 
 
 def pack_with_taps(x_ref, taps_ref, gain_ref, band_ref, *refs):
     outs, held_ref = refs[:-1], refs[-1]
-    block_len = x_ref.shape[0]
+    block_len, chans = x_ref.shape
     tiles = block_len // LANES
+    far = chans // (NEAR * SUBS)
+    step = NEAR * SUBS
     for k in range(tiles):
-        store_parts(held_ref, k, x_ref[k * LANES:(k + 1) * LANES, :].T)
-    rows, chans = taps_ref.shape
+        part = x_ref[k * LANES:(k + 1) * LANES, :].T
+        for z in range(far):
+            held_ref[:, z * tiles + k, :, :] = part[z * step:(z + 1) * step].reshape(-1, SUBS, LANES)
+    rows = taps_ref.shape[0]
     place = lax.axis_index("far") * NEAR + lax.axis_index("near")
     lag = place * rows + lax.broadcasted_iota(jnp.int32, (rows, chans), 0)
     kept = jnp.where(lag < band_ref[...] * block_len, taps_ref[...], 0.0)
     kept = kept + jnp.where(lag == 0, gain_ref[...], 0.0)
-    kept = jnp.concatenate([kept, jnp.zeros((LANES - rows, chans), jnp.float32)], axis=0)
-    store_parts(held_ref, tiles, kept.T)
-    for bits, out_ref in enumerate(outs):
+    kept = jnp.concatenate([kept, jnp.zeros((LANES - rows, chans), jnp.float32)], axis=0).T
+    for pair in range(far // 2):
+        low, high = (kept[z * step:(z + 1) * step] for z in (2 * pair, 2 * pair + 1))
+        both = low + pltpu.roll(high, LANES // 2, axis=1)
+        held_ref[:, far * tiles + pair, :, :] = both.reshape(-1, SUBS, LANES)
+    for bits, out_ref in zip(ORDER, outs):
         out_ref[...] = held_ref[other(bits)]
 
 
@@ -39,22 +40,24 @@
 
 
 def merge(parts, held_ref):
-    for bits, ref in enumerate(parts):
+    for bits, ref in zip(ORDER, parts):
         held_ref[other(bits)] = ref[...]
 
 
-def pack_plain(x_ref, out_ref):
-    for k in range(x_ref.shape[0] // LANES):
-        part = x_ref[k * LANES:(k + 1) * LANES, :].T
+def pack_plain(g_ref, own_ref, out_ref, same_ref):
+    for k in range(g_ref.shape[0] // LANES):
+        part = g_ref[k * LANES:(k + 1) * LANES, :].T
         out_ref[:, k, :, :] = part.reshape(-1, SUBS, LANES)
+    same_ref[...] = own_ref[...]
 
 
 def unpack(*refs):
-    parts, (out_ref, held_ref) = refs[:-2], refs[-2:]
+    parts, (out_ref, held_ref) = refs[:NEAR], refs[-2:]
     merge(parts, held_ref)
-    for k in range(out_ref.shape[0] // LANES):
-        part = jnp.concatenate([held_ref[:, z, k, :, :].reshape(-1, LANES) for z in range(held_ref.shape[1])], axis=0)
-        out_ref[k * LANES:(k + 1) * LANES, :] = part.T
+    tiles = out_ref.shape[0] // LANES
+    for k in range(tiles):
+        picked = [held_ref[:, at, :, :].reshape(-1, LANES) for at in range(k, held_ref.shape[1], tiles)]
+        out_ref[k * LANES:(k + 1) * LANES, :] = jnp.concatenate(picked, axis=0).T
 
 
 def split(value):
@@ -62,32 +65,34 @@
     return high, (value - high.astype(jnp.float32)).astype(jnp.bfloat16)
 
 
-def collect(rows, halo_blocks, *refs):
+def collect(rows, halo_blocks, tiles, *refs):
     parts, (halo_ref, taps_ref, x_ref) = refs[:-3], refs[-3:]
     merge(parts, x_ref)
-    near, far, tiles = x_ref.shape[:3]
-    tiles = tiles - 1
-    lane = lax.broadcasted_iota(jnp.int32, (far * SUBS, LANES), 1)
+    near = len(parts)
+    x_tiles = x_ref.shape[1] * 2 * tiles // (2 * tiles + 1)
+    far = x_tiles // tiles
+    height = far * SUBS
+    lane = lax.broadcasted_iota(jnp.int32, (height, LANES), 1)
     own_tiles = rows * near // LANES
-    held = [jnp.zeros((far * SUBS, LANES), jnp.float32) for _ in range(own_tiles)]
+    held = [jnp.zeros((height, LANES), jnp.float32) for _ in range(own_tiles)]
     for piece in range(near):
         tile, offset = divmod(rows * piece, LANES)
-        value = x_ref[piece, :, tiles, :, :].reshape(far * SUBS, LANES)
+        values = []
+        for pair in range(far // 2):
+            both = x_ref[piece, x_tiles + pair]
+            values += [both, pltpu.roll(both, LANES // 2, axis=1)]
+        value = jnp.concatenate(values, axis=0)
         turned = pltpu.roll(value, offset, axis=1) if offset else value
-        if offset + rows <= LANES:
-            held[tile] = held[tile] + turned
-        else:
-            held[tile] = held[tile] + jnp.where(lane >= offset, turned, 0.0)
-            held[tile + 1] = held[tile + 1] + jnp.where(lane < offset, turned, 0.0)
-    height = far * SUBS
-    halo_rows = halo_blocks * far * tiles * SUBS
+        held[tile] = held[tile] + jnp.where((lane >= offset) & (lane < offset + rows), turned, 0.0)
+        if offset + rows > LANES:
+            held[tile + 1] = held[tile + 1] + jnp.where(lane < offset + rows - LANES, turned, 0.0)
+    share = x_tiles * SUBS
+    halo_rows = halo_blocks * share
     for tile in range(own_tiles):
         taps_ref[tile * height:(tile + 1) * height, :] = held[tile]
         halo_ref[halo_rows + tile * height:halo_rows + (tile + 1) * height, :] = held[tile]
     for block in range(halo_blocks):
-        for z in range(far):
-            base = (block * far + z) * tiles * SUBS
-            halo_ref[base:base + tiles * SUBS, :] = x_ref[near - halo_blocks + block, z, :tiles, :, :].reshape(-1, LANES)
+        halo_ref[block * share:(block + 1) * share, :] = x_ref[near - halo_blocks + block, :x_tiles].reshape(share, LANES)
 
 
 def toeplitz(row):
@@ -121,18 +126,16 @@
     parts, halo_ref, others, outs = refs[:near], refs[near], refs[near + 1:near + far], refs[near + far:-3]
     y_ref, row_ref, held_ref = refs[-3:]
     chans = far * SUBS
-    chunk = far * (tiles + 1) * SUBS
+    chunk = parts[0].shape[0] * SUBS
     halo_rows = halo_blocks * far * tiles * SUBS
     pieces = [(others[0], 0), (halo_ref, halo_rows)] + [(ref, 0) for ref in others[1:]]
     lay_rows(row_ref, pieces, far, chans, lambda ref, base: ref[base:base + chans, :])
     first = lax.axis_index("far") == 0
+    share = far * tiles * SUBS
     for block in range(halo_blocks):
-        for z in range(far):
-            source = (block * far + z) * tiles * SUBS
-            target = block * chunk + z * (tiles + 1) * SUBS
-            value = halo_ref[source:source + tiles * SUBS, :]
-            held_ref[target:target + tiles * SUBS, :] = jnp.where(first, 0.0, value)
-    for bits, ref in enumerate(parts):
+        value = halo_ref[block * share:(block + 1) * share, :]
+        held_ref[block * chunk:block * chunk + share, :] = jnp.where(first, 0.0, value)
+    for bits, ref in zip(ORDER, parts):
         at = pl.multiple_of((halo_blocks + other(bits)) * chunk, SUBS)
         held_ref[pl.ds(at, chunk), :] = ref[...].reshape(chunk, LANES)
     depth = row_ref.shape[0] - 1
@@ -143,7 +146,7 @@
         moved = {}
         for k in range(tiles):
             for steps in range(halo_blocks + 1):
-                start = (halo_blocks - steps) * chunk + z * (tiles + 1) * SUBS + k * SUBS + i
+                start = (halo_blocks - steps) * chunk + (z * tiles + k) * SUBS + i
                 moved[k, steps] = jnp.concatenate(split(held_ref[pl.ds(start, near, stride=chunk), :]), axis=0)
         columns = []
         for d in range(depth):
@@ -166,14 +169,14 @@
         return carry
 
     lax.fori_loop(0, chans, one, 0, unroll=8)
-    share = far * tiles * SUBS
-    for bits, ref in enumerate(outs):
+    for bits, ref in zip(ORDER, outs):
         at = pl.multiple_of(other(bits) * share, SUBS)
         ref[...] = y_ref[pl.ds(at, share), :].reshape(ref.shape)
 
 
 def gradient(blocks, tiles, halo_rows, g_ref, halo_ref, *refs):
-    others, (out_ref, row_ref, held_ref) = refs[:-3], refs[-3:]
+    others, (out_ref, token_ref, row_ref, held_ref) = refs[:-4], refs[-4:]
+    token_ref[...] = jnp.zeros(token_ref.shape, jnp.float32)
     far = len(others) + 1
     me = lax.axis_index("far")
     pieces = [(others[0], 0), (halo_ref, halo_rows)] + [(ref, 0) for ref in others[1:]]
@@ -206,7 +209,7 @@
             held_ref[pl.ds(k * SUBS + chan, blocks, stride=chunk), :] = value
         return carry
 
-    lax.fori_loop(0, SUBS, one, 0, unroll=2)
+    lax.fori_loop(0, SUBS, one, 0, unroll=4)
     for tile in range(blocks * tiles):
         out_ref[:, tile * LANES:(tile + 1) * LANES] = held_ref[tile * SUBS:(tile + 1) * SUBS, :]
 
@@ -240,34 +243,37 @@
 
     def swapped(parts):
         pairs = [[(n, n ^ bits) for n in range(near)] for bits in range(near)]
-        return [lax.ppermute(part, "near", pairs[bits]) if bits else part for bits, part in enumerate(parts)]
-
-    share = (far, tiles + 1, SUBS, LANES)
-    got_x = swapped(call(pack_with_taps, [share] * near, [pltpu.VMEM((near, *share), jnp.float32)], moved=2 * size, room=60)(
-        inputs, filter_rows, skip_gain[None, :], band_blocks[None, :]))
+        return [lax.ppermute(part, "near", pairs[bits]) if bits else part for bits, part in zip(ORDER, parts)]
+
+    share = (far * tiles + far // 2, SUBS, LANES)
+    sent_x = call(pack_with_taps, [share] * near, [pltpu.VMEM((near, *share), jnp.float32)], moved=2 * size, room=60)(
+        inputs, filter_rows, skip_gain[None, :], band_blocks[None, :])
+    got_x = swapped(sent_x)
+    sent_g, got_x[0] = call(pack_plain, [(count, tiles, SUBS, LANES), share], moved=2 * size)(cotangent, sent_x[0])
     halo_rows = halo_blocks * far * tiles * SUBS
     own_taps = lag_tiles // far * far * SUBS
-    halo, taps = call(lambda *refs: collect(rows, halo_blocks, *refs), [(halo_rows + own_taps, LANES), (own_taps, LANES)],
+    halo, taps = call(lambda *refs: collect(rows, halo_blocks, tiles, *refs),
+                      [(halo_rows + own_taps, LANES), (own_taps, LANES)],
                       [pltpu.VMEM((near, *share), jnp.float32)], moved=size)(*got_x)
     got_halo = ahead(halo, 1)
     pieces = [taps] + [ahead(taps, steps) for steps in range(2, far)]
-
-    sent_g = call(pack_plain, [(count, tiles, SUBS, LANES)], moved=2 * size)(cotangent)
     got_g = lax.all_to_all(sent_g, ("far", "near"), split_axis=0, concat_axis=0, tiled=True).reshape(-1, LANES)
 
     def row(height):
         return pltpu.VMEM((lag_tiles + 2, height, LANES), jnp.float32)
 
     all_rows = pltpu.VMEM((count * tiles * SUBS, LANES), jnp.float32)
-    held_rows = (near + halo_blocks) * far * (tiles + 1) * SUBS
+    held_rows = (near + halo_blocks) * share[0] * SUBS
     flops = 2 * far * SUBS * 2 * near * tiles * (lag_tiles + 1) * LANES * 2 * LANES
-    share = (far, tiles, SUBS, LANES)
+    share = (far * tiles, SUBS, LANES)
     got_y = swapped(call(lambda *refs: forward(halo_blocks, tiles, near, far, *refs), [share] * near,
                          [all_rows, row(far * SUBS), pltpu.VMEM((held_rows, LANES), jnp.float32)], 40 * flops, 2 * size)(
         *got_x, got_halo, *pieces))
-    input_grad = call(lambda *refs: gradient(count, tiles, halo_rows, *refs), [(SUBS, count * block_len)],
-                      [row(SUBS), all_rows], flops, 3 * size)(got_g, got_halo, *pieces)
-    outputs = call(unpack, [(block_len, chans)], [pltpu.VMEM((near, *share), jnp.float32)], moved=2 * size)(*got_y)
+    input_grad, token = call(lambda *refs: gradient(count, tiles, halo_rows, *refs),
+                             [(SUBS, count * block_len), (SUBS, LANES)],
+                             [row(SUBS), all_rows], flops, 3 * size)(got_g, got_halo, *pieces)
+    outputs = call(unpack, [(block_len, chans)], [pltpu.VMEM((near, *share), jnp.float32)], moved=2 * size,
+                   operands=near, after=1)(*got_y, token)
     return outputs, input_grad
 
 

time: 78.4 us -> 67.1 us (0.86)
  the two profiles are of different devices: /device:TPU:1 before, /device:TPU:199 now
where the time goes in v5:
time: 67.1 us; the launch traced here: 66.8 us
  starting transfers between devices  35.2 us (52%)
  Pallas kernels  19.1 us (28%)
  waiting for transfers between devices  10.9 us (16%)
  local copies, waits for them, and re-layouts  0.9 us (1%)
  between operations  0.72 us (1%)
    ppermute x14, starting transfers between devices, swapped(): lax.ppermute(part, 'near', pairs[bits])  22.1 us
    pallas_call x1, Pallas kernels, local(): call(lambda *refs: forward(halo_blocks, tiles, near, far, *refs), [share]...  9.35 us
    all_to_all x1, starting transfers between devices, local(): lax.all_to_all(sent_g, ('far', 'near'), split_axis=0, concat_axis=0, tile...  8.55 us
    ppermute x3, waiting for transfers between devices, ahead(): lax.ppermute(value, 'far', [(z, (z + steps) % far) for z in range(far)])  7.45 us
    pallas_call x1, Pallas kernels, local(): call(lambda *refs: gradient(count, tiles, halo_rows, *refs), [(SUBS, coun...  4.68 us
    ppermute x3, starting transfers between devices, ahead(): lax.ppermute(value, 'far', [(z, (z + steps) % far) for z in range(far)])  4.54 us
    ppermute x14, waiting for transfers between devices, swapped(): lax.ppermute(part, 'near', pairs[bits])  3.41 us
    pallas_call x1, Pallas kernels, local(): call(pack_with_taps, [share] * near, [pltpu.VMEM((near, *share), jnp.floa...  2.51 us
  transfers between devices with their start and end apart: 18, of which 4 were waited for; matrix products, arithmetic and copies ran while one was open for 0% of the time, Pallas kernels for 23%

profile of v5, /device:TPU:199, one launch (start us, length us, event | category | flops | bytes accessed | tf_op | source)
XLA Modules:
  0.0 66.8 jit_solution(18262143826620133015)
XLA Ops:
  0.6 0.0 copy-start
  0.6 2.5 %shard_map.68 = (f32[26,8,128]{2,1,0:T(8,128)}, f32[26,8,128]{2,1,0:T(8,128)}, f32[26,8,128]{2,1,0:T(8,128)}, f32[26,8,128]{2,1,0:T(8,128)}, f32[26,8,128]{2,1,0...) custom-call(f32[768,256]{1,0:T(8,128)} %x_ref.1, f32[48,256]{1,0:T(8,128)} %taps_ref.1, ...), custom_call_target="tpu_custom_call" | custom-call | bytes 1572864 | tf_op jit(solution)/shard_map/pallas_call | solution.py:249
  3.2 2.9 %collective-permute-start = (f32[26,8,128]{2,1,0:T(8,128)}, f32[26,8,128]{2,1,0:T(8,128)S(1)}, u32[]{:S(2)}, u32[]{:S(2)}) collective-permute-start(f32[26,8,128]{2,1,0:T(8,128)} %get-tuple-element.26), channel_id=1, source_target_pairs={{0,32},{8,40},{16,48},{24,56},{32,0},{40,8},{48,16},{56,24},{1,33}... | collective-permute-start | bytes 319496 | tf_op jit(solution)/shard_map/ppermute | solution.py:246
  6.1 0.9 %collective-permute-start.1 = (f32[26,8,128]{2,1,0:T(8,128)}, f32[26,8,128]{2,1,0:T(8,128)S(1)}, u32[]{:S(2)}, u32[]{:S(2)}) collective-permute-start(f32[26,8,128]{2,1,0:T(8,128)} %get-tuple-element.27), channel_id=1, source_target_pairs={{0,40},{8,32},{16,56},{24,48},{32,8},{40,0},{48,24},{56,16},{1,41}... | collective-permute-start | bytes 319496 | tf_op jit(solution)/shard_map/ppermute | solution.py:246
  7.0 1.3 %collective-permute-start.2 = (f32[26,8,128]{2,1,0:T(8,128)}, f32[26,8,128]{2,1,0:T(8,128)S(1)}, u32[]{:S(2)}, u32[]{:S(2)}) collective-permute-start(f32[26,8,128]{2,1,0:T(8,128)} %get-tuple-element.28), channel_id=1, source_target_pairs={{0,16},{8,24},{16,0},{24,8},{32,48},{40,56},{48,32},{56,40},{1,17}... | collective-permute-start | bytes 319496 | tf_op jit(solution)/shard_map/ppermute | solution.py:246
  8.3 1.9 %collective-permute-start.3 = (f32[26,8,128]{2,1,0:T(8,128)}, f32[26,8,128]{2,1,0:T(8,128)S(1)}, u32[]{:S(2)}, u32[]{:S(2)}) collective-permute-start(f32[26,8,128]{2,1,0:T(8,128)} %get-tuple-element.29), channel_id=1, source_target_pairs={{0,48},{8,56},{16,32},{24,40},{32,16},{40,24},{48,0},{56,8},{1,49}... | collective-permute-start | bytes 319496 | tf_op jit(solution)/shard_map/ppermute | solution.py:246
  10.2 0.4 collective-permute-start.4
  10.6 0.0 collective-permute-done.refs_1_
  10.6 2.8 %collective-permute-start.5 = (f32[26,8,128]{2,1,0:T(8,128)}, f32[26,8,128]{2,1,0:T(8,128)S(1)}, u32[]{:S(2)}, u32[]{:S(2)}) collective-permute-start(f32[26,8,128]{2,1,0:T(8,128)} %get-tuple-element.31), channel_id=1, source_target_pairs={{0,56},{8,48},{16,40},{24,32},{32,24},{40,16},{48,8},{56,0},{1,57}... | collective-permute-start | bytes 319496 | tf_op jit(solution)/shard_map/ppermute | solution.py:246
  13.4 0.0 collective-permute-done.1.refs_2_
  13.4 0.6 collective-permute-start.6
  14.0 0.0 copy-done
  14.0 0.0 copy-start.1
  14.0 0.9 %copy-done.1 = f32[26,8,128]{2,1,0:T(8,128)S(1)} copy-done((f32[26,8,128]{2,1,0:T(8,128)S(1)}, f32[26,8,128]{2,1,0:T(8,128)}, u32[]{:S(2)}) %copy-start.1) | copy-done | bytes 106520
  14.9 1.1 %shard_map.69 = (f32[32,6,8,128]{3,2,1,0:T(8,128)}, f32[26,8,128]{2,1,0:T(8,128)S(1)}) custom-call(f32[768,256]{1,0:T(8,128)S(1)} %copy-done, f32[26,8,128]{2,1,0:T(8,128)S(1)} %copy-done.1), custom_call_target="tpu_custom_call" | custom-call | bytes 1572864 | tf_op jit(solution)/shard_map/pallas_call | solution.py:252
  16.1 0.0 collective-permute-done.2.refs_3_
  16.1 0.0 collective-permute-done.3.refs_4_
  16.1 1.0 %collective-permute-done.4.refs_5_ = f32[26,8,128]{2,1,0:T(8,128)S(1)} collective-permute-done((f32[26,8,128]{2,1,0:T(8,128)}, f32[26,8,128]{2,1,0:T(8,128)S(1)}, u32[]{:S(2)}, u32[]{:S(2)}) %collective-permute-start.4) | collective-permute-done | bytes 106528 | tf_op jit(solution)/shard_map/ppermute | solution.py:246
  17.0 0.8 %collective-permute-done.5.refs_6_ = f32[26,8,128]{2,1,0:T(8,128)S(1)} collective-permute-done((f32[26,8,128]{2,1,0:T(8,128)}, f32[26,8,128]{2,1,0:T(8,128)S(1)}, u32[]{:S(2)}, u32[]{:S(2)}) %collective-permute-start.5) | collective-permute-done | bytes 106528 | tf_op jit(solution)/shard_map/ppermute | solution.py:246
  17.9 0.0 collective-permute-done.6.refs_7_
  17.9 0.2 shard_map.70
  18.1 0.1 collective-permute-start.7
  18.2 2.4 %collective-permute-start.9 = (f32[96,128]{1,0:T(8,128)S(1)}, f32[96,128]{1,0:T(8,128)S(1)}, u32[]{:S(2)}, u32[]{:S(2)}) collective-permute-start(f32[96,128]{1,0:T(8,128)S(1)} %get-tuple-element.34.refs_9_.refs_2_), channel_id=1, source_target_pairs={{0,192},{64,0},{128,64},{192,128},{1,193},{65,1},{129,65},{193,129... | collective-permute-start | bytes 147464 | tf_op jit(solution)/shard_map/ppermute | solution.py:242
  20.6 2.1 %collective-permute-start.8 = (f32[96,128]{1,0:T(8,128)S(1)}, f32[96,128]{1,0:T(8,128)S(1)}, u32[]{:S(2)}, u32[]{:S(2)}) collective-permute-start(f32[96,128]{1,0:T(8,128)S(1)} %get-tuple-element.34.refs_9_.refs_2_), channel_id=1, source_target_pairs={{0,128},{64,192},{128,0},{192,64},{1,129},{65,193},{129,1},{193,65... | collective-permute-start | bytes 147464 | tf_op jit(solution)/shard_map/ppermute | solution.py:242
  22.7 8.6 %all-to-all-start = ((f32[32,6,8,128]{3,2,1,0:T(8,128)}), f32[32,6,8,128]{3,2,1,0:T(8,128)S(1)}, u32[]{:S(2)}, u32[]{:S(2)}) async-start(f32[32,6,8,128]{3,2,1,0:T(8,128)} %get-tuple-element.43), calls=%async_computation | async-start | bytes 1572864 | tf_op jit(solution)/shard_map/all_to_all | solution.py:260
  31.2 0.0 collective-permute-done.9.refs_11_.refs_4_
  31.2 7.4 %collective-permute-done.8.refs_10_.refs_3_ = f32[96,128]{1,0:T(8,128)S(1)} collective-permute-done((f32[96,128]{1,0:T(8,128)S(1)}, f32[96,128]{1,0:T(8,128)S(1)}, u32[]{:S(2)}, u32[]{:S(2)}) %collective-permute-start.8) | collective-permute-done | bytes 49184 | tf_op jit(solution)/shard_map/ppermute | solution.py:242
  38.7 0.0 collective-permute-done.7.refs_8_.refs_1_
  38.7 9.4 %shard_map.71 = (f32[24,8,128]{2,1,0:T(8,128)S(1)}, f32[24,8,128]{2,1,0:T(8,128)S(1)}, f32[24,8,128]{2,1,0:T(8,128)S(1)}, f32[24,8,128]{2,1,0:T(8,128)S(1)}, f32...) custom-call(f32[26,8,128]{2,1,0:T(8,128)S(1)} %get-tuple-element.25.r, ...), custom_call_target="tpu_custom_call" | custom-call | flops 104689827840 | bytes 1572864 | tf_op jit(solution)/shard_map/pallas_call | solution.py:269
  48.1 0.5 collective-permute-start.10
  48.5 7.0 %collective-permute-start.11 = (f32[24,8,128]{2,1,0:T(8,128)S(1)}, f32[24,8,128]{2,1,0:T(8,128)S(1)}, u32[]{:S(2)}, u32[]{:S(2)}) collective-permute-start(f32[24,8,128]{2,1,0:T(8,128)S(1)} %get-tuple-element.37), channel_id=1, source_target_pairs={{0,40},{8,32},{16,56},{24,48},{32,8},{40,0},{48,24},{56,16},{1,41}... | collective-permute-start | bytes 294920 | tf_op jit(solution)/shard_map/ppermute | solution.py:246
  55.5 0.0 collective-permute-start.12
  55.5 0.1 collective-permute-start.13
  55.6 0.0 collective-permute-start.14
  55.6 0.0 collective-permute-done.10.refs_1_
  55.6 3.7 %collective-permute-start.15 = (f32[24,8,128]{2,1,0:T(8,128)S(1)}, f32[24,8,128]{2,1,0:T(8,128)S(1)}, u32[]{:S(2)}, u32[]{:S(2)}) collective-permute-start(f32[24,8,128]{2,1,0:T(8,128)S(1)} %get-tuple-element.41), channel_id=1, source_target_pairs={{0,56},{8,48},{16,40},{24,32},{32,24},{40,16},{48,8},{56,0},{1,57}... | collective-permute-start | bytes 294920 | tf_op jit(solution)/shard_map/ppermute | solution.py:246
  59.3 1.6 %collective-permute-done.11.refs_2_ = f32[24,8,128]{2,1,0:T(8,128)S(1)} collective-permute-done((f32[24,8,128]{2,1,0:T(8,128)S(1)}, f32[24,8,128]{2,1,0:T(8,128)S(1)}, u32[]{:S(2)}, u32[]{:S(2)}) %collective-permute-start.11) | collective-permute-done | bytes 98336 | tf_op jit(solution)/shard_map/ppermute | solution.py:246
  60.9 0.0 collective-permute-start.16
  60.9 0.0 all-to-all-done
  60.9 4.7 %shard_map.72 = (f32[8,24576]{1,0:T(8,128)}, f32[8,128]{1,0:T(8,128)S(1)}) custom-call(f32[1536,128]{1,0:T(8,128)S(1)} %bitcast.3, f32[480,128]{1,0:T(8,128)S(1)} %collective-permute-done.7.refs_8_.refs_1_, f32[96,128]{1,0:T(8,128)S(1)} %get-tuple-element.34.refs_9_.refs_2_, f32[96,128]{1,0:T(8,128)S(1)} %collective-permute-done.8.refs_10_.refs_3_, ...), custom_call_target="tpu_custom_call" | custom-call | flops 2617245696 | bytes 2359296 | tf_op jit(solution)/shard_map/pallas_call | solution.py:272
  65.6 0.0 collective-permute-done.12.refs_3_
  65.6 0.0 collective-permute-done.13.refs_4_
  65.6 0.0 collective-permute-done.14.refs_5_
  65.6 0.0 collective-permute-done.15.refs_6_
  65.6 0.0 collective-permute-done.16.refs_7_
  65.6 1.2 %shard_map.73 = f32[768,256]{1,0:T(8,128)} custom-call(f32[24,8,128]{2,1,0:T(8,128)S(1)} %get-tuple-element.35.refs_0_, f32[24,8,128]{2,1,0:T(8,128)S(1)} %collective-permute-done.10.refs_1_, f32[24,8,128]{2,1,0:T(8,128)S(1)} %collective-permute-done.11.refs_2_, f32[24,8,128]{2,1,0:T(8,128)S(1)} %collective-permute-done.12.refs_3_, ...), custom_call_target="tpu_custom_call" | custom-call | bytes 1572864 | tf_op jit(solution)/shard_map/pallas_call | solution.py:275
Async XLA Ops:
  0.6 13.4 %copy-start = (f32[768,256]{1,0:T(8,128)S(1)}, f32[768,256]{1,0:T(8,128)}, u32[]{:S(2)}) copy-start(f32[768,256]{1,0:T(8,128)} %g_ref.1) | copy-start | bytes 2359300
  3.2 7.4 %collective-permute-start = (f32[26,8,128]{2,1,0:T(8,128)}, f32[26,8,128]{2,1,0:T(8,128)S(1)}, u32[]{:S(2)}, u32[]{:S(2)}) collective-permute-start(f32[26,8,128]{2,1,0:T(8,128)} %get-tuple-element.26), channel_id=1, source_target_pairs={{0,32},{8,40},{16,48},{24,56},{32,0},{40,8},{48,16},{56,24},{1,33}... | collective-permute-start | bytes 319496 | tf_op jit(solution)/shard_map/ppermute | solution.py:246
  6.1 7.3 %collective-permute-start.1 = (f32[26,8,128]{2,1,0:T(8,128)}, f32[26,8,128]{2,1,0:T(8,128)S(1)}, u32[]{:S(2)}, u32[]{:S(2)}) collective-permute-start(f32[26,8,128]{2,1,0:T(8,128)} %get-tuple-element.27), channel_id=1, source_target_pairs={{0,40},{8,32},{16,56},{24,48},{32,8},{40,0},{48,24},{56,16},{1,41}... | collective-permute-start | bytes 319496 | tf_op jit(solution)/shard_map/ppermute | solution.py:246
  7.0 9.1 %collective-permute-start.2 = (f32[26,8,128]{2,1,0:T(8,128)}, f32[26,8,128]{2,1,0:T(8,128)S(1)}, u32[]{:S(2)}, u32[]{:S(2)}) collective-permute-start(f32[26,8,128]{2,1,0:T(8,128)} %get-tuple-element.28), channel_id=1, source_target_pairs={{0,16},{8,24},{16,0},{24,8},{32,48},{40,56},{48,32},{56,40},{1,17}... | collective-permute-start | bytes 319496 | tf_op jit(solution)/shard_map/ppermute | solution.py:246
  8.3 7.8 %collective-permute-start.3 = (f32[26,8,128]{2,1,0:T(8,128)}, f32[26,8,128]{2,1,0:T(8,128)S(1)}, u32[]{:S(2)}, u32[]{:S(2)}) collective-permute-start(f32[26,8,128]{2,1,0:T(8,128)} %get-tuple-element.29), channel_id=1, source_target_pairs={{0,48},{8,56},{16,32},{24,40},{32,16},{40,24},{48,0},{56,8},{1,49}... | collective-permute-start | bytes 319496 | tf_op jit(solution)/shard_map/ppermute | solution.py:246
  10.2 6.9 %collective-permute-start.4 = (f32[26,8,128]{2,1,0:T(8,128)}, f32[26,8,128]{2,1,0:T(8,128)S(1)}, u32[]{:S(2)}, u32[]{:S(2)}) collective-permute-start(f32[26,8,128]{2,1,0:T(8,128)} %get-tuple-element.30), channel_id=1, source_target_pairs={{0,24},{8,16},{16,8},{24,0},{32,56},{40,48},{48,40},{56,32},{1,25}... | collective-permute-start | bytes 319496 | tf_op jit(solution)/shard_map/ppermute | solution.py:246
  10.6 7.3 %collective-permute-start.5 = (f32[26,8,128]{2,1,0:T(8,128)}, f32[26,8,128]{2,1,0:T(8,128)S(1)}, u32[]{:S(2)}, u32[]{:S(2)}) collective-permute-start(f32[26,8,128]{2,1,0:T(8,128)} %get-tuple-element.31), channel_id=1, source_target_pairs={{0,56},{8,48},{16,40},{24,32},{32,24},{40,16},{48,8},{56,0},{1,57}... | collective-permute-start | bytes 319496 | tf_op jit(solution)/shard_map/ppermute | solution.py:246
  13.4 4.5 %collective-permute-start.6 = (f32[26,8,128]{2,1,0:T(8,128)}, f32[26,8,128]{2,1,0:T(8,128)S(1)}, u32[]{:S(2)}, u32[]{:S(2)}) collective-permute-start(f32[26,8,128]{2,1,0:T(8,128)} %get-tuple-element.32), channel_id=1, source_target_pairs={{0,8},{8,0},{16,24},{24,16},{32,40},{40,32},{48,56},{56,48},{1,9},... | collective-permute-start | bytes 319496 | tf_op jit(solution)/shard_map/ppermute | solution.py:246
  14.0 0.9 %copy-start.1 = (f32[26,8,128]{2,1,0:T(8,128)S(1)}, f32[26,8,128]{2,1,0:T(8,128)}, u32[]{:S(2)}) copy-start(f32[26,8,128]{2,1,0:T(8,128)} %get-tuple-element.24.own_ref) | copy-start | bytes 319492
  18.1 20.6 %collective-permute-start.7 = (f32[480,128]{1,0:T(8,128)S(1)}, f32[480,128]{1,0:T(8,128)S(1)}, u32[]{:S(2)}, u32[]{:S(2)}) collective-permute-start(f32[480,128]{1,0:T(8,128)S(1)} %get-tuple-element.33), channel_id=1, source_target_pairs={{0,64},{64,128},{128,192},{192,0},{1,65},{65,129},{129,193},{193,1... | collective-permute-start | bytes 737288 | tf_op jit(solution)/shard_map/ppermute | solution.py:242
  18.2 13.0 %collective-permute-start.9 = (f32[96,128]{1,0:T(8,128)S(1)}, f32[96,128]{1,0:T(8,128)S(1)}, u32[]{:S(2)}, u32[]{:S(2)}) collective-permute-start(f32[96,128]{1,0:T(8,128)S(1)} %get-tuple-element.34.refs_9_.refs_2_), channel_id=1, source_target_pairs={{0,192},{64,0},{128,64},{192,128},{1,193},{65,1},{129,65},{193,129... | collective-permute-start | bytes 147464 | tf_op jit(solution)/shard_map/ppermute | solution.py:242
  20.6 18.1 %collective-permute-start.8 = (f32[96,128]{1,0:T(8,128)S(1)}, f32[96,128]{1,0:T(8,128)S(1)}, u32[]{:S(2)}, u32[]{:S(2)}) collective-permute-start(f32[96,128]{1,0:T(8,128)S(1)} %get-tuple-element.34.refs_9_.refs_2_), channel_id=1, source_target_pairs={{0,128},{64,192},{128,0},{192,64},{1,129},{65,193},{129,1},{193,65... | collective-permute-start | bytes 147464 | tf_op jit(solution)/shard_map/ppermute | solution.py:242
  22.7 38.2 %all-to-all-start = ((f32[32,6,8,128]{3,2,1,0:T(8,128)}), f32[32,6,8,128]{3,2,1,0:T(8,128)S(1)}, u32[]{:S(2)}, u32[]{:S(2)}) async-start(f32[32,6,8,128]{3,2,1,0:T(8,128)} %get-tuple-element.43), calls=%async_computation | async-start | bytes 1572864 | tf_op jit(solution)/shard_map/all_to_all | solution.py:260
  48.1 7.6 %collective-permute-start.10 = (f32[24,8,128]{2,1,0:T(8,128)S(1)}, f32[24,8,128]{2,1,0:T(8,128)S(1)}, u32[]{:S(2)}, u32[]{:S(2)}) collective-permute-start(f32[24,8,128]{2,1,0:T(8,128)S(1)} %get-tuple-element.36), channel_id=1, source_target_pairs={{0,32},{8,40},{16,48},{24,56},{32,0},{40,8},{48,16},{56,24},{1,33}... | collective-permute-start | bytes 294920 | tf_op jit(solution)/shard_map/ppermute | solution.py:246
  48.5 12.4 %collective-permute-start.11 = (f32[24,8,128]{2,1,0:T(8,128)S(1)}, f32[24,8,128]{2,1,0:T(8,128)S(1)}, u32[]{:S(2)}, u32[]{:S(2)}) collective-permute-start(f32[24,8,128]{2,1,0:T(8,128)S(1)} %get-tuple-element.37), channel_id=1, source_target_pairs={{0,40},{8,32},{16,56},{24,48},{32,8},{40,0},{48,24},{56,16},{1,41}... | collective-permute-start | bytes 294920 | tf_op jit(solution)/shard_map/ppermute | solution.py:246
  55.5 10.1 %collective-permute-start.12 = (f32[24,8,128]{2,1,0:T(8,128)S(1)}, f32[24,8,128]{2,1,0:T(8,128)S(1)}, u32[]{:S(2)}, u32[]{:S(2)}) collective-permute-start(f32[24,8,128]{2,1,0:T(8,128)S(1)} %get-tuple-element.38), channel_id=1, source_target_pairs={{0,16},{8,24},{16,0},{24,8},{32,48},{40,56},{48,32},{56,40},{1,17}... | collective-permute-start | bytes 294920 | tf_op jit(solution)/shard_map/ppermute | solution.py:246
  55.5 10.1 %collective-permute-start.13 = (f32[24,8,128]{2,1,0:T(8,128)S(1)}, f32[24,8,128]{2,1,0:T(8,128)S(1)}, u32[]{:S(2)}, u32[]{:S(2)}) collective-permute-start(f32[24,8,128]{2,1,0:T(8,128)S(1)} %get-tuple-element.39), channel_id=1, source_target_pairs={{0,48},{8,56},{16,32},{24,40},{32,16},{40,24},{48,0},{56,8},{1,49}... | collective-permute-start | bytes 294920 | tf_op jit(solution)/shard_map/ppermute | solution.py:246
  55.6 10.0 %collective-permute-start.14 = (f32[24,8,128]{2,1,0:T(8,128)S(1)}, f32[24,8,128]{2,1,0:T(8,128)S(1)}, u32[]{:S(2)}, u32[]{:S(2)}) collective-permute-start(f32[24,8,128]{2,1,0:T(8,128)S(1)} %get-tuple-element.40), channel_id=1, source_target_pairs={{0,24},{8,16},{16,8},{24,0},{32,56},{40,48},{48,40},{56,32},{1,25}... | collective-permute-start | bytes 294920 | tf_op jit(solution)/shard_map/ppermute | solution.py:246
  55.6 10.0 %collective-permute-start.15 = (f32[24,8,128]{2,1,0:T(8,128)S(1)}, f32[24,8,128]{2,1,0:T(8,128)S(1)}, u32[]{:S(2)}, u32[]{:S(2)}) collective-permute-start(f32[24,8,128]{2,1,0:T(8,128)S(1)} %get-tuple-element.41), channel_id=1, source_target_pairs={{0,56},{8,48},{16,40},{24,32},{32,24},{40,16},{48,8},{56,0},{1,57}... | collective-permute-start | bytes 294920 | tf_op jit(solution)/shard_map/ppermute | solution.py:246
  60.9 4.7 %collective-permute-start.16 = (f32[24,8,128]{2,1,0:T(8,128)S(1)}, f32[24,8,128]{2,1,0:T(8,128)S(1)}, u32[]{:S(2)}, u32[]{:S(2)}) collective-permute-start(f32[24,8,128]{2,1,0:T(8,128)S(1)} %get-tuple-element.42), channel_id=1, source_target_pairs={{0,8},{8,0},{16,24},{24,16},{32,40},{40,32},{48,56},{56,48},{1,9},... | collective-permute-start | bytes 294920 | tf_op jit(solution)/shard_map/ppermute | solution.py:246

commit v6 on v5

--- a/solution.py
+++ b/solution.py
@@ -8,7 +8,8 @@
 LANES = 128
 SUBS = 8
 NEAR = 8
-ORDER = (0, 4, 5, 2, 6, 3, 7, 1)
+IN_ORDER = (0, 4, 5, 2, 6, 3, 7, 1)
+OUT_ORDER = (0, 1, 4, 2, 6, 5, 3, 7)
 
 
 def pack_with_taps(x_ref, taps_ref, gain_ref, band_ref, *refs):
@@ -31,7 +32,7 @@
         low, high = (kept[z * step:(z + 1) * step] for z in (2 * pair, 2 * pair + 1))
         both = low + pltpu.roll(high, LANES // 2, axis=1)
         held_ref[:, far * tiles + pair, :, :] = both.reshape(-1, SUBS, LANES)
-    for bits, out_ref in zip(ORDER, outs):
+    for bits, out_ref in zip(IN_ORDER, outs):
         out_ref[...] = held_ref[other(bits)]
 
 
@@ -39,8 +40,8 @@
     return lax.axis_index("near") ^ bits
 
 
-def merge(parts, held_ref):
-    for bits, ref in zip(ORDER, parts):
+def merge(order, parts, held_ref):
+    for bits, ref in zip(order, parts):
         held_ref[other(bits)] = ref[...]
 
 
@@ -53,7 +54,7 @@
 
 def unpack(*refs):
     parts, (out_ref, held_ref) = refs[:NEAR], refs[-2:]
-    merge(parts, held_ref)
+    merge(OUT_ORDER, parts, held_ref)
     tiles = out_ref.shape[0] // LANES
     for k in range(tiles):
         picked = [held_ref[:, at, :, :].reshape(-1, LANES) for at in range(k, held_ref.shape[1], tiles)]
@@ -67,7 +68,7 @@
 
 def collect(rows, halo_blocks, tiles, *refs):
     parts, (halo_ref, taps_ref, x_ref) = refs[:-3], refs[-3:]
-    merge(parts, x_ref)
+    merge(IN_ORDER, parts, x_ref)
     near = len(parts)
     x_tiles = x_ref.shape[1] * 2 * tiles // (2 * tiles + 1)
     far = x_tiles // tiles
@@ -135,7 +136,7 @@
     for block in range(halo_blocks):
         value = halo_ref[block * share:(block + 1) * share, :]
         held_ref[block * chunk:block * chunk + share, :] = jnp.where(first, 0.0, value)
-    for bits, ref in zip(ORDER, parts):
+    for bits, ref in zip(IN_ORDER, parts):
         at = pl.multiple_of((halo_blocks + other(bits)) * chunk, SUBS)
         held_ref[pl.ds(at, chunk), :] = ref[...].reshape(chunk, LANES)
     depth = row_ref.shape[0] - 1
@@ -168,8 +169,8 @@
             y_ref[pl.ds((z * tiles + k) * SUBS + i, near, stride=far * tiles * SUBS), :] = value
         return carry
 
-    lax.fori_loop(0, chans, one, 0, unroll=8)
-    for bits, ref in zip(ORDER, outs):
+    lax.fori_loop(0, chans, one, 0, unroll=16)
+    for bits, ref in zip(OUT_ORDER, outs):
         at = pl.multiple_of(other(bits) * share, SUBS)
         ref[...] = y_ref[pl.ds(at, share), :].reshape(ref.shape)
 
@@ -209,7 +210,7 @@
             held_ref[pl.ds(k * SUBS + chan, blocks, stride=chunk), :] = value
         return carry
 
-    lax.fori_loop(0, SUBS, one, 0, unroll=4)
+    lax.fori_loop(0, SUBS, one, 0, unroll=8)
     for tile in range(blocks * tiles):
         out_ref[:, tile * LANES:(tile + 1) * LANES] = held_ref[tile * SUBS:(tile + 1) * SUBS, :]
 
@@ -241,14 +242,14 @@
     def ahead(value, steps):
         return lax.ppermute(value, "far", [(z, (z + steps) % far) for z in range(far)])
 
-    def swapped(parts):
+    def swapped(parts, order):
         pairs = [[(n, n ^ bits) for n in range(near)] for bits in range(near)]
-        return [lax.ppermute(part, "near", pairs[bits]) if bits else part for bits, part in zip(ORDER, parts)]
+        return [lax.ppermute(part, "near", pairs[bits]) if bits else part for bits, part in zip(order, parts)]
 
     share = (far * tiles + far // 2, SUBS, LANES)
     sent_x = call(pack_with_taps, [share] * near, [pltpu.VMEM((near, *share), jnp.float32)], moved=2 * size, room=60)(
         inputs, filter_rows, skip_gain[None, :], band_blocks[None, :])
-    got_x = swapped(sent_x)
+    got_x = swapped(sent_x, IN_ORDER)
     sent_g, got_x[0] = call(pack_plain, [(count, tiles, SUBS, LANES), share], moved=2 * size)(cotangent, sent_x[0])
     halo_rows = halo_blocks * far * tiles * SUBS
     own_taps = lag_tiles // far * far * SUBS
@@ -268,7 +269,7 @@
     share = (far * tiles, SUBS, LANES)
     got_y = swapped(call(lambda *refs: forward(halo_blocks, tiles, near, far, *refs), [share] * near,
                          [all_rows, row(far * SUBS), pltpu.VMEM((held_rows, LANES), jnp.float32)], 40 * flops, 2 * size)(
-        *got_x, got_halo, *pieces))
+        *got_x, got_halo, *pieces), OUT_ORDER)
     input_grad, token = call(lambda *refs: gradient(count, tiles, halo_rows, *refs),
                              [(SUBS, count * block_len), (SUBS, LANES)],
                              [row(SUBS), all_rows], flops, 3 * size)(got_g, got_halo, *pieces)

time: 67.1 us -> 65.6 us (0.978)
  the two profiles are of different devices: /device:TPU:199 before, /device:TPU:1 now
where the time goes in v6:
time: 65.6 us; the launch traced here: 64.4 us
  starting transfers between devices  38.7 us (59%)
  Pallas kernels  18.3 us (28%)
  waiting for transfers between devices  5.91 us (9%)
  local copies, waits for them, and re-layouts  0.9 us (1%)
  between operations  0.7 us (1%)
    ppermute x14, starting transfers between devices, swapped(): lax.ppermute(part, 'near', pairs[bits])  23.5 us
    ppermute x3, starting transfers between devices, ahead(): lax.ppermute(value, 'far', [(z, (z + steps) % far) for z in range(far)])  10.2 us
    pallas_call x1, Pallas kernels, local(): call(lambda *refs: forward(halo_blocks, tiles, near, far, *refs), [share]...  8.76 us
    all_to_all x1, starting transfers between devices, local(): lax.all_to_all(sent_g, ('far', 'near'), split_axis=0, concat_axis=0, tile...  5.01 us
    pallas_call x1, Pallas kernels, local(): call(lambda *refs: gradient(count, tiles, halo_rows, *refs), [(SUBS, coun...  4.38 us
    ppermute x14, waiting for transfers between devices, swapped(): lax.ppermute(part, 'near', pairs[bits])  3.5 us
    pallas_call x1, Pallas kernels, local(): call(pack_with_taps, [share] * near, [pltpu.VMEM((near, *share), jnp.floa...  2.51 us
    ppermute x3, waiting for transfers between devices, ahead(): lax.ppermute(value, 'far', [(z, (z + steps) % far) for z in range(far)])  1.99 us
  transfers between devices with their start and end apart: 18, of which 7 were waited for; matrix products, arithmetic and copies ran while one was open for 0% of the time, Pallas kernels for 22%

profile of v6, /device:TPU:1, one launch (start us, length us, event | category | flops | bytes accessed | tf_op | source)
XLA Modules:
  0.0 64.4 jit_solution(9835393893359806118)
XLA Ops:
  0.6 0.0 copy-start
  0.6 2.5 %shard_map.68 = (f32[26,8,128]{2,1,0:T(8,128)}, f32[26,8,128]{2,1,0:T(8,128)}, f32[26,8,128]{2,1,0:T(8,128)}, f32[26,8,128]{2,1,0:T(8,128)}, f32[26,8,128]{2,1,0...) custom-call(f32[768,256]{1,0:T(8,128)} %x_ref.1, f32[48,256]{1,0:T(8,128)} %taps_ref.1, ...), custom_call_target="tpu_custom_call" | custom-call | bytes 1572864 | tf_op jit(solution)/shard_map/pallas_call | solution.py:250
  3.2 3.7 %collective-permute-start = (f32[26,8,128]{2,1,0:T(8,128)}, f32[26,8,128]{2,1,0:T(8,128)S(1)}, u32[]{:S(2)}, u32[]{:S(2)}) collective-permute-start(f32[26,8,128]{2,1,0:T(8,128)} %get-tuple-element.26), channel_id=1, source_target_pairs={{0,32},{8,40},{16,48},{24,56},{32,0},{40,8},{48,16},{56,24},{1,33}... | collective-permute-start | bytes 319496 | tf_op jit(solution)/shard_map/ppermute | solution.py:247
  6.9 2.6 %collective-permute-start.1 = (f32[26,8,128]{2,1,0:T(8,128)}, f32[26,8,128]{2,1,0:T(8,128)S(1)}, u32[]{:S(2)}, u32[]{:S(2)}) collective-permute-start(f32[26,8,128]{2,1,0:T(8,128)} %get-tuple-element.27), channel_id=1, source_target_pairs={{0,40},{8,32},{16,56},{24,48},{32,8},{40,0},{48,24},{56,16},{1,41}... | collective-permute-start | bytes 319496 | tf_op jit(solution)/shard_map/ppermute | solution.py:247
  9.5 0.0 collective-permute-start.2
  9.5 1.5 %collective-permute-start.3 = (f32[26,8,128]{2,1,0:T(8,128)}, f32[26,8,128]{2,1,0:T(8,128)S(1)}, u32[]{:S(2)}, u32[]{:S(2)}) collective-permute-start(f32[26,8,128]{2,1,0:T(8,128)} %get-tuple-element.29), channel_id=1, source_target_pairs={{0,48},{8,56},{16,32},{24,40},{32,16},{40,24},{48,0},{56,8},{1,49}... | collective-permute-start | bytes 319496 | tf_op jit(solution)/shard_map/ppermute | solution.py:247
  11.0 0.4 collective-permute-start.4
  11.4 0.0 collective-permute-done.refs_1_
  11.4 2.8 %collective-permute-start.5 = (f32[26,8,128]{2,1,0:T(8,128)}, f32[26,8,128]{2,1,0:T(8,128)S(1)}, u32[]{:S(2)}, u32[]{:S(2)}) collective-permute-start(f32[26,8,128]{2,1,0:T(8,128)} %get-tuple-element.31), channel_id=1, source_target_pairs={{0,56},{8,48},{16,40},{24,32},{32,24},{40,16},{48,8},{56,0},{1,57}... | collective-permute-start | bytes 319496 | tf_op jit(solution)/shard_map/ppermute | solution.py:247
  14.2 0.4 collective-permute-done.1.refs_2_
  14.7 0.2 collective-permute-start.6
  14.9 0.0 copy-done
  14.9 0.0 copy-start.1
  14.9 0.9 %copy-done.1 = f32[26,8,128]{2,1,0:T(8,128)S(1)} copy-done((f32[26,8,128]{2,1,0:T(8,128)S(1)}, f32[26,8,128]{2,1,0:T(8,128)}, u32[]{:S(2)}) %copy-start.1) | copy-done | bytes 106520
  15.8 1.1 %shard_map.69 = (f32[32,6,8,128]{3,2,1,0:T(8,128)}, f32[26,8,128]{2,1,0:T(8,128)S(1)}) custom-call(f32[768,256]{1,0:T(8,128)S(1)} %copy-done, f32[26,8,128]{2,1,0:T(8,128)S(1)} %copy-done.1), custom_call_target="tpu_custom_call" | custom-call | bytes 1572864 | tf_op jit(solution)/shard_map/pallas_call | solution.py:253
  17.0 0.0 collective-permute-done.2.refs_3_
  17.0 0.0 collective-permute-done.3.refs_4_
  17.0 0.9 %collective-permute-done.4.refs_5_ = f32[26,8,128]{2,1,0:T(8,128)S(1)} collective-permute-done((f32[26,8,128]{2,1,0:T(8,128)}, f32[26,8,128]{2,1,0:T(8,128)S(1)}, u32[]{:S(2)}, u32[]{:S(2)}) %collective-permute-start.4) | collective-permute-done | bytes 106528 | tf_op jit(solution)/shard_map/ppermute | solution.py:247
  17.9 1.2 %collective-permute-done.5.refs_6_ = f32[26,8,128]{2,1,0:T(8,128)S(1)} collective-permute-done((f32[26,8,128]{2,1,0:T(8,128)}, f32[26,8,128]{2,1,0:T(8,128)S(1)}, u32[]{:S(2)}, u32[]{:S(2)}) %collective-permute-start.5) | collective-permute-done | bytes 106528 | tf_op jit(solution)/shard_map/ppermute | solution.py:247
  19.1 0.0 collective-permute-done.6.refs_7_
  19.1 0.2 shard_map.70
  19.3 2.7 %collective-permute-start.7 = (f32[480,128]{1,0:T(8,128)S(1)}, f32[480,128]{1,0:T(8,128)S(1)}, u32[]{:S(2)}, u32[]{:S(2)}) collective-permute-start(f32[480,128]{1,0:T(8,128)S(1)} %get-tuple-element.33), channel_id=1, source_target_pairs={{0,64},{64,128},{128,192},{192,0},{1,65},{65,129},{129,193},{193,1... | collective-permute-start | bytes 737288 | tf_op jit(solution)/shard_map/ppermute | solution.py:243
  22.0 3.1 %collective-permute-start.9 = (f32[96,128]{1,0:T(8,128)S(1)}, f32[96,128]{1,0:T(8,128)S(1)}, u32[]{:S(2)}, u32[]{:S(2)}) collective-permute-start(f32[96,128]{1,0:T(8,128)S(1)} %get-tuple-element.34.refs_9_.refs_2_), channel_id=1, source_target_pairs={{0,192},{64,0},{128,64},{192,128},{1,193},{65,1},{129,65},{193,129... | collective-permute-start | bytes 147464 | tf_op jit(solution)/shard_map/ppermute | solution.py:243
  25.1 4.4 %collective-permute-start.8 = (f32[96,128]{1,0:T(8,128)S(1)}, f32[96,128]{1,0:T(8,128)S(1)}, u32[]{:S(2)}, u32[]{:S(2)}) collective-permute-start(f32[96,128]{1,0:T(8,128)S(1)} %get-tuple-element.34.refs_9_.refs_2_), channel_id=1, source_target_pairs={{0,128},{64,192},{128,0},{192,64},{1,129},{65,193},{129,1},{193,65... | collective-permute-start | bytes 147464 | tf_op jit(solution)/shard_map/ppermute | solution.py:243
  29.5 5.0 %all-to-all-start = ((f32[32,6,8,128]{3,2,1,0:T(8,128)}), f32[32,6,8,128]{3,2,1,0:T(8,128)S(1)}, u32[]{:S(2)}, u32[]{:S(2)}) async-start(f32[32,6,8,128]{3,2,1,0:T(8,128)} %get-tuple-element.43), calls=%async_computation | async-start | bytes 1572864 | tf_op jit(solution)/shard_map/all_to_all | solution.py:261
  34.5 0.0 collective-permute-done.9.refs_11_.refs_4_
  34.6 2.0 %collective-permute-done.8.refs_10_.refs_3_ = f32[96,128]{1,0:T(8,128)S(1)} collective-permute-done((f32[96,128]{1,0:T(8,128)S(1)}, f32[96,128]{1,0:T(8,128)S(1)}, u32[]{:S(2)}, u32[]{:S(2)}) %collective-permute-start.8) | collective-permute-done | bytes 49184 | tf_op jit(solution)/shard_map/ppermute | solution.py:243
  36.5 0.0 collective-permute-done.7.refs_8_.refs_1_
  36.5 8.8 %shard_map.71 = (f32[24,8,128]{2,1,0:T(8,128)S(1)}, f32[24,8,128]{2,1,0:T(8,128)S(1)}, f32[24,8,128]{2,1,0:T(8,128)S(1)}, f32[24,8,128]{2,1,0:T(8,128)S(1)}, f32...) custom-call(f32[26,8,128]{2,1,0:T(8,128)S(1)} %get-tuple-element.25.r, ...), custom_call_target="tpu_custom_call" | custom-call | flops 104689827840 | bytes 1572864 | tf_op jit(solution)/shard_map/pallas_call | solution.py:270
  45.3 2.5 %collective-permute-start.10 = (f32[24,8,128]{2,1,0:T(8,128)S(1)}, f32[24,8,128]{2,1,0:T(8,128)S(1)}, u32[]{:S(2)}, u32[]{:S(2)}) collective-permute-start(f32[24,8,128]{2,1,0:T(8,128)S(1)} %get-tuple-element.36), channel_id=1, source_target_pairs={{0,8},{8,0},{16,24},{24,16},{32,40},{40,32},{48,56},{56,48},{1,9},... | collective-permute-start | bytes 294920 | tf_op jit(solution)/shard_map/ppermute | solution.py:247
  47.9 1.7 %collective-permute-start.11 = (f32[24,8,128]{2,1,0:T(8,128)S(1)}, f32[24,8,128]{2,1,0:T(8,128)S(1)}, u32[]{:S(2)}, u32[]{:S(2)}) collective-permute-start(f32[24,8,128]{2,1,0:T(8,128)S(1)} %get-tuple-element.37), channel_id=1, source_target_pairs={{0,32},{8,40},{16,48},{24,56},{32,0},{40,8},{48,16},{56,24},{1,33}... | collective-permute-start | bytes 294920 | tf_op jit(solution)/shard_map/ppermute | solution.py:247
  49.5 0.1 collective-permute-start.12
  49.6 1.5 %collective-permute-start.13 = (f32[24,8,128]{2,1,0:T(8,128)S(1)}, f32[24,8,128]{2,1,0:T(8,128)S(1)}, u32[]{:S(2)}, u32[]{:S(2)}) collective-permute-start(f32[24,8,128]{2,1,0:T(8,128)S(1)} %get-tuple-element.39), channel_id=1, source_target_pairs={{0,48},{8,56},{16,32},{24,40},{32,16},{40,24},{48,0},{56,8},{1,49}... | collective-permute-start | bytes 294920 | tf_op jit(solution)/shard_map/ppermute | solution.py:247
  51.1 2.7 %collective-permute-start.14 = (f32[24,8,128]{2,1,0:T(8,128)S(1)}, f32[24,8,128]{2,1,0:T(8,128)S(1)}, u32[]{:S(2)}, u32[]{:S(2)}) collective-permute-start(f32[24,8,128]{2,1,0:T(8,128)S(1)} %get-tuple-element.40), channel_id=1, source_target_pairs={{0,40},{8,32},{16,56},{24,48},{32,8},{40,0},{48,24},{56,16},{1,41}... | collective-permute-start | bytes 294920 | tf_op jit(solution)/shard_map/ppermute | solution.py:247
  53.8 0.0 collective-permute-done.10.refs_1_
  53.8 0.0 collective-permute-start.15
  53.8 0.7 %collective-permute-done.11.refs_2_ = f32[24,8,128]{2,1,0:T(8,128)S(1)} collective-permute-done((f32[24,8,128]{2,1,0:T(8,128)S(1)}, f32[24,8,128]{2,1,0:T(8,128)S(1)}, u32[]{:S(2)}, u32[]{:S(2)}) %collective-permute-start.11) | collective-permute-done | bytes 98336 | tf_op jit(solution)/shard_map/ppermute | solution.py:247
  54.5 3.7 %collective-permute-start.16 = (f32[24,8,128]{2,1,0:T(8,128)S(1)}, f32[24,8,128]{2,1,0:T(8,128)S(1)}, u32[]{:S(2)}, u32[]{:S(2)}) collective-permute-start(f32[24,8,128]{2,1,0:T(8,128)S(1)} %get-tuple-element.42), channel_id=1, source_target_pairs={{0,56},{8,48},{16,40},{24,32},{32,24},{40,16},{48,8},{56,0},{1,57}... | collective-permute-start | bytes 294920 | tf_op jit(solution)/shard_map/ppermute | solution.py:247
  58.2 0.4 all-to-all-done
  58.6 4.4 %shard_map.72 = (f32[8,24576]{1,0:T(8,128)}, f32[8,128]{1,0:T(8,128)S(1)}) custom-call(f32[1536,128]{1,0:T(8,128)S(1)} %bitcast.3, f32[480,128]{1,0:T(8,128)S(1)} %collective-permute-done.7.refs_8_.refs_1_, f32[96,128]{1,0:T(8,128)S(1)} %get-tuple-element.34.refs_9_.refs_2_, f32[96,128]{1,0:T(8,128)S(1)} %collective-permute-done.8.refs_10_.refs_3_, ...), custom_call_target="tpu_custom_call" | custom-call | flops 2617245696 | bytes 2359296 | tf_op jit(solution)/shard_map/pallas_call | solution.py:273
  63.0 0.0 collective-permute-done.12.refs_3_
  63.0 0.0 collective-permute-done.13.refs_4_
  63.0 0.0 collective-permute-done.14.refs_5_
  63.0 0.0 collective-permute-done.15.refs_6_
  63.0 0.2 collective-permute-done.16.refs_7_
  63.2 1.2 %shard_map.73 = f32[768,256]{1,0:T(8,128)} custom-call(f32[24,8,128]{2,1,0:T(8,128)S(1)} %get-tuple-element.35.refs_0_, f32[24,8,128]{2,1,0:T(8,128)S(1)} %collective-permute-done.10.refs_1_, f32[24,8,128]{2,1,0:T(8,128)S(1)} %collective-permute-done.11.refs_2_, f32[24,8,128]{2,1,0:T(8,128)S(1)} %collective-permute-done.12.refs_3_, ...), custom_call_target="tpu_custom_call" | custom-call | bytes 1572864 | tf_op jit(solution)/shard_map/pallas_call | solution.py:276
Async XLA Ops:
  0.6 14.3 %copy-start = (f32[768,256]{1,0:T(8,128)S(1)}, f32[768,256]{1,0:T(8,128)}, u32[]{:S(2)}) copy-start(f32[768,256]{1,0:T(8,128)} %g_ref.1) | copy-start | bytes 2359300
  3.2 8.2 %collective-permute-start = (f32[26,8,128]{2,1,0:T(8,128)}, f32[26,8,128]{2,1,0:T(8,128)S(1)}, u32[]{:S(2)}, u32[]{:S(2)}) collective-permute-start(f32[26,8,128]{2,1,0:T(8,128)} %get-tuple-element.26), channel_id=1, source_target_pairs={{0,32},{8,40},{16,48},{24,56},{32,0},{40,8},{48,16},{56,24},{1,33}... | collective-permute-start | bytes 319496 | tf_op jit(solution)/shard_map/ppermute | solution.py:247
  6.9 7.8 %collective-permute-start.1 = (f32[26,8,128]{2,1,0:T(8,128)}, f32[26,8,128]{2,1,0:T(8,128)S(1)}, u32[]{:S(2)}, u32[]{:S(2)}) collective-permute-start(f32[26,8,128]{2,1,0:T(8,128)} %get-tuple-element.27), channel_id=1, source_target_pairs={{0,40},{8,32},{16,56},{24,48},{32,8},{40,0},{48,24},{56,16},{1,41}... | collective-permute-start | bytes 319496 | tf_op jit(solution)/shard_map/ppermute | solution.py:247
  9.5 7.4 %collective-permute-start.2 = (f32[26,8,128]{2,1,0:T(8,128)}, f32[26,8,128]{2,1,0:T(8,128)S(1)}, u32[]{:S(2)}, u32[]{:S(2)}) collective-permute-start(f32[26,8,128]{2,1,0:T(8,128)} %get-tuple-element.28), channel_id=1, source_target_pairs={{0,16},{8,24},{16,0},{24,8},{32,48},{40,56},{48,32},{56,40},{1,17}... | collective-permute-start | bytes 319496 | tf_op jit(solution)/shard_map/ppermute | solution.py:247
  9.5 7.4 %collective-permute-start.3 = (f32[26,8,128]{2,1,0:T(8,128)}, f32[26,8,128]{2,1,0:T(8,128)S(1)}, u32[]{:S(2)}, u32[]{:S(2)}) collective-permute-start(f32[26,8,128]{2,1,0:T(8,128)} %get-tuple-element.29), channel_id=1, source_target_pairs={{0,48},{8,56},{16,32},{24,40},{32,16},{40,24},{48,0},{56,8},{1,49}... | collective-permute-start | bytes 319496 | tf_op jit(solution)/shard_map/ppermute | solution.py:247
  11.0 6.9 %collective-permute-start.4 = (f32[26,8,128]{2,1,0:T(8,128)}, f32[26,8,128]{2,1,0:T(8,128)S(1)}, u32[]{:S(2)}, u32[]{:S(2)}) collective-permute-start(f32[26,8,128]{2,1,0:T(8,128)} %get-tuple-element.30), channel_id=1, source_target_pairs={{0,24},{8,16},{16,8},{24,0},{32,56},{40,48},{48,40},{56,32},{1,25}... | collective-permute-start | bytes 319496 | tf_op jit(solution)/shard_map/ppermute | solution.py:247
  11.4 7.7 %collective-permute-start.5 = (f32[26,8,128]{2,1,0:T(8,128)}, f32[26,8,128]{2,1,0:T(8,128)S(1)}, u32[]{:S(2)}, u32[]{:S(2)}) collective-permute-start(f32[26,8,128]{2,1,0:T(8,128)} %get-tuple-element.31), channel_id=1, source_target_pairs={{0,56},{8,48},{16,40},{24,32},{32,24},{40,16},{48,8},{56,0},{1,57}... | collective-permute-start | bytes 319496 | tf_op jit(solution)/shard_map/ppermute | solution.py:247
  14.7 4.4 %collective-permute-start.6 = (f32[26,8,128]{2,1,0:T(8,128)}, f32[26,8,128]{2,1,0:T(8,128)S(1)}, u32[]{:S(2)}, u32[]{:S(2)}) collective-permute-start(f32[26,8,128]{2,1,0:T(8,128)} %get-tuple-element.32), channel_id=1, source_target_pairs={{0,8},{8,0},{16,24},{24,16},{32,40},{40,32},{48,56},{56,48},{1,9},... | collective-permute-start | bytes 319496 | tf_op jit(solution)/shard_map/ppermute | solution.py:247
  14.9 0.9 %copy-start.1 = (f32[26,8,128]{2,1,0:T(8,128)S(1)}, f32[26,8,128]{2,1,0:T(8,128)}, u32[]{:S(2)}) copy-start(f32[26,8,128]{2,1,0:T(8,128)} %get-tuple-element.24.own_ref) | copy-start | bytes 319492
  19.3 17.2 %collective-permute-start.7 = (f32[480,128]{1,0:T(8,128)S(1)}, f32[480,128]{1,0:T(8,128)S(1)}, u32[]{:S(2)}, u32[]{:S(2)}) collective-permute-start(f32[480,128]{1,0:T(8,128)S(1)} %get-tuple-element.33), channel_id=1, source_target_pairs={{0,64},{64,128},{128,192},{192,0},{1,65},{65,129},{129,193},{193,1... | collective-permute-start | bytes 737288 | tf_op jit(solution)/shard_map/ppermute | solution.py:243
  22.0 12.5 %collective-permute-start.9 = (f32[96,128]{1,0:T(8,128)S(1)}, f32[96,128]{1,0:T(8,128)S(1)}, u32[]{:S(2)}, u32[]{:S(2)}) collective-permute-start(f32[96,128]{1,0:T(8,128)S(1)} %get-tuple-element.34.refs_9_.refs_2_), channel_id=1, source_target_pairs={{0,192},{64,0},{128,64},{192,128},{1,193},{65,1},{129,65},{193,129... | collective-permute-start | bytes 147464 | tf_op jit(solution)/shard_map/ppermute | solution.py:243
  25.1 11.4 %collective-permute-start.8 = (f32[96,128]{1,0:T(8,128)S(1)}, f32[96,128]{1,0:T(8,128)S(1)}, u32[]{:S(2)}, u32[]{:S(2)}) collective-permute-start(f32[96,128]{1,0:T(8,128)S(1)} %get-tuple-element.34.refs_9_.refs_2_), channel_id=1, source_target_pairs={{0,128},{64,192},{128,0},{192,64},{1,129},{65,193},{129,1},{193,65... | collective-permute-start | bytes 147464 | tf_op jit(solution)/shard_map/ppermute | solution.py:243
  29.5 29.1 %all-to-all-start = ((f32[32,6,8,128]{3,2,1,0:T(8,128)}), f32[32,6,8,128]{3,2,1,0:T(8,128)S(1)}, u32[]{:S(2)}, u32[]{:S(2)}) async-start(f32[32,6,8,128]{3,2,1,0:T(8,128)} %get-tuple-element.43), calls=%async_computation | async-start | bytes 1572864 | tf_op jit(solution)/shard_map/all_to_all | solution.py:261
  45.3 8.5 %collective-permute-start.10 = (f32[24,8,128]{2,1,0:T(8,128)S(1)}, f32[24,8,128]{2,1,0:T(8,128)S(1)}, u32[]{:S(2)}, u32[]{:S(2)}) collective-permute-start(f32[24,8,128]{2,1,0:T(8,128)S(1)} %get-tuple-element.36), channel_id=1, source_target_pairs={{0,8},{8,0},{16,24},{24,16},{32,40},{40,32},{48,56},{56,48},{1,9},... | collective-permute-start | bytes 294920 | tf_op jit(solution)/shard_map/ppermute | solution.py:247
  47.9 6.7 %collective-permute-start.11 = (f32[24,8,128]{2,1,0:T(8,128)S(1)}, f32[24,8,128]{2,1,0:T(8,128)S(1)}, u32[]{:S(2)}, u32[]{:S(2)}) collective-permute-start(f32[24,8,128]{2,1,0:T(8,128)S(1)} %get-tuple-element.37), channel_id=1, source_target_pairs={{0,32},{8,40},{16,48},{24,56},{32,0},{40,8},{48,16},{56,24},{1,33}... | collective-permute-start | bytes 294920 | tf_op jit(solution)/shard_map/ppermute | solution.py:247
  49.5 13.5 %collective-permute-start.12 = (f32[24,8,128]{2,1,0:T(8,128)S(1)}, f32[24,8,128]{2,1,0:T(8,128)S(1)}, u32[]{:S(2)}, u32[]{:S(2)}) collective-permute-start(f32[24,8,128]{2,1,0:T(8,128)S(1)} %get-tuple-element.38), channel_id=1, source_target_pairs={{0,16},{8,24},{16,0},{24,8},{32,48},{40,56},{48,32},{56,40},{1,17}... | collective-permute-start | bytes 294920 | tf_op jit(solution)/shard_map/ppermute | solution.py:247
  49.6 13.4 %collective-permute-start.13 = (f32[24,8,128]{2,1,0:T(8,128)S(1)}, f32[24,8,128]{2,1,0:T(8,128)S(1)}, u32[]{:S(2)}, u32[]{:S(2)}) collective-permute-start(f32[24,8,128]{2,1,0:T(8,128)S(1)} %get-tuple-element.39), channel_id=1, source_target_pairs={{0,48},{8,56},{16,32},{24,40},{32,16},{40,24},{48,0},{56,8},{1,49}... | collective-permute-start | bytes 294920 | tf_op jit(solution)/shard_map/ppermute | solution.py:247
  51.1 11.9 %collective-permute-start.14 = (f32[24,8,128]{2,1,0:T(8,128)S(1)}, f32[24,8,128]{2,1,0:T(8,128)S(1)}, u32[]{:S(2)}, u32[]{:S(2)}) collective-permute-start(f32[24,8,128]{2,1,0:T(8,128)S(1)} %get-tuple-element.40), channel_id=1, source_target_pairs={{0,40},{8,32},{16,56},{24,48},{32,8},{40,0},{48,24},{56,16},{1,41}... | collective-permute-start | bytes 294920 | tf_op jit(solution)/shard_map/ppermute | solution.py:247
  53.8 9.2 %collective-permute-start.15 = (f32[24,8,128]{2,1,0:T(8,128)S(1)}, f32[24,8,128]{2,1,0:T(8,128)S(1)}, u32[]{:S(2)}, u32[]{:S(2)}) collective-permute-start(f32[24,8,128]{2,1,0:T(8,128)S(1)} %get-tuple-element.41), channel_id=1, source_target_pairs={{0,24},{8,16},{16,8},{24,0},{32,56},{40,48},{48,40},{56,32},{1,25}... | collective-permute-start | bytes 294920 | tf_op jit(solution)/shard_map/ppermute | solution.py:247
  54.5 8.7 %collective-permute-start.16 = (f32[24,8,128]{2,1,0:T(8,128)S(1)}, f32[24,8,128]{2,1,0:T(8,128)S(1)}, u32[]{:S(2)}, u32[]{:S(2)}) collective-permute-start(f32[24,8,128]{2,1,0:T(8,128)S(1)} %get-tuple-element.42), channel_id=1, source_target_pairs={{0,56},{8,48},{16,40},{24,32},{32,24},{40,16},{48,8},{56,0},{1,57}... | collective-permute-start | bytes 294920 | tf_op jit(solution)/shard_map/ppermute | solution.py:247

commit v7 on v6

--- a/solution.py
+++ b/solution.py
@@ -169,7 +169,7 @@
             y_ref[pl.ds((z * tiles + k) * SUBS + i, near, stride=far * tiles * SUBS), :] = value
         return carry
 
-    lax.fori_loop(0, chans, one, 0, unroll=16)
+    lax.fori_loop(0, chans, one, 0, unroll=32)
     for bits, ref in zip(OUT_ORDER, outs):
         at = pl.multiple_of(other(bits) * share, SUBS)
         ref[...] = y_ref[pl.ds(at, share), :].reshape(ref.shape)

time: 65.6 us -> 65.3 us (level)
  transfers between devices with their start and end apart: 18 -> 18, of which waited for: 7 -> 6; matrix products, arithmetic and copies ran while one was open for 0% -> 0% of each run, Pallas kernels for 22% -> 22%
where the time goes in v7:
time: 65.3 us; the launch traced here: 64.3 us
  starting transfers between devices  38.5 us (59%)
  Pallas kernels  17.9 us (27%)
  waiting for transfers between devices  6.26 us (10%)
  local copies, waits for them, and re-layouts  0.9 us (1%)
  between operations  0.71 us (1%)
    ppermute x14, starting transfers between devices, swapped(): lax.ppermute(part, 'near', pairs[bits])  23.3 us
    ppermute x3, starting transfers between devices, ahead(): lax.ppermute(value, 'far', [(z, (z + steps) % far) for z in range(far)])  10.2 us
    pallas_call x1, Pallas kernels, local(): call(lambda *refs: forward(halo_blocks, tiles, near, far, *refs), [share]...  8.42 us
    all_to_all x1, starting transfers between devices, local(): lax.all_to_all(sent_g, ('far', 'near'), split_axis=0, concat_axis=0, tile...  5.02 us
    pallas_call x1, Pallas kernels, local(): call(lambda *refs: gradient(count, tiles, halo_rows, *refs), [(SUBS, coun...  4.38 us
    ppermute x14, waiting for transfers between devices, swapped(): lax.ppermute(part, 'near', pairs[bits])  3.51 us
    pallas_call x1, Pallas kernels, local(): call(pack_with_taps, [share] * near, [pltpu.VMEM((near, *share), jnp.floa...  2.51 us
    ppermute x3, waiting for transfers between devices, ahead(): lax.ppermute(value, 'far', [(z, (z + steps) % far) for z in range(far)])  1.98 us
  transfers between devices with their start and end apart: 18, of which 6 were waited for; matrix products, arithmetic and copies ran while one was open for 0% of the time, Pallas kernels for 22%

profile of v7, /device:TPU:1, one launch (start us, length us, event | category | flops | bytes accessed | tf_op | source)
XLA Modules:
  0.0 64.3 jit_solution(18211673129861844290)
XLA Ops:
  0.6 0.0 copy-start
  0.6 2.5 %shard_map.68 = (f32[26,8,128]{2,1,0:T(8,128)}, f32[26,8,128]{2,1,0:T(8,128)}, f32[26,8,128]{2,1,0:T(8,128)}, f32[26,8,128]{2,1,0:T(8,128)}, f32[26,8,128]{2,1,0...) custom-call(f32[768,256]{1,0:T(8,128)} %x_ref.1, f32[48,256]{1,0:T(8,128)} %taps_ref.1, ...), custom_call_target="tpu_custom_call" | custom-call | bytes 1572864 | tf_op jit(solution)/shard_map/pallas_call | solution.py:250
  3.2 3.7 %collective-permute-start = (f32[26,8,128]{2,1,0:T(8,128)}, f32[26,8,128]{2,1,0:T(8,128)S(1)}, u32[]{:S(2)}, u32[]{:S(2)}) collective-permute-start(f32[26,8,128]{2,1,0:T(8,128)} %get-tuple-element.26), channel_id=1, source_target_pairs={{0,32},{8,40},{16,48},{24,56},{32,0},{40,8},{48,16},{56,24},{1,33}... | collective-permute-start | bytes 319496 | tf_op jit(solution)/shard_map/ppermute | solution.py:247
  6.9 2.6 %collective-permute-start.1 = (f32[26,8,128]{2,1,0:T(8,128)}, f32[26,8,128]{2,1,0:T(8,128)S(1)}, u32[]{:S(2)}, u32[]{:S(2)}) collective-permute-start(f32[26,8,128]{2,1,0:T(8,128)} %get-tuple-element.27), channel_id=1, source_target_pairs={{0,40},{8,32},{16,56},{24,48},{32,8},{40,0},{48,24},{56,16},{1,41}... | collective-permute-start | bytes 319496 | tf_op jit(solution)/shard_map/ppermute | solution.py:247
  9.5 0.0 collective-permute-start.2
  9.5 1.5 %collective-permute-start.3 = (f32[26,8,128]{2,1,0:T(8,128)}, f32[26,8,128]{2,1,0:T(8,128)S(1)}, u32[]{:S(2)}, u32[]{:S(2)}) collective-permute-start(f32[26,8,128]{2,1,0:T(8,128)} %get-tuple-element.29), channel_id=1, source_target_pairs={{0,48},{8,56},{16,32},{24,40},{32,16},{40,24},{48,0},{56,8},{1,49}... | collective-permute-start | bytes 319496 | tf_op jit(solution)/shard_map/ppermute | solution.py:247
  11.0 0.4 collective-permute-start.4
  11.4 0.0 collective-permute-done.refs_1_
  11.4 2.8 %collective-permute-start.5 = (f32[26,8,128]{2,1,0:T(8,128)}, f32[26,8,128]{2,1,0:T(8,128)S(1)}, u32[]{:S(2)}, u32[]{:S(2)}) collective-permute-start(f32[26,8,128]{2,1,0:T(8,128)} %get-tuple-element.31), channel_id=1, source_target_pairs={{0,56},{8,48},{16,40},{24,32},{32,24},{40,16},{48,8},{56,0},{1,57}... | collective-permute-start | bytes 319496 | tf_op jit(solution)/shard_map/ppermute | solution.py:247
  14.2 0.4 collective-permute-done.1.refs_2_
  14.7 0.2 collective-permute-start.6
  14.9 0.0 copy-done
  14.9 0.0 copy-start.1
  14.9 0.9 %copy-done.1 = f32[26,8,128]{2,1,0:T(8,128)S(1)} copy-done((f32[26,8,128]{2,1,0:T(8,128)S(1)}, f32[26,8,128]{2,1,0:T(8,128)}, u32[]{:S(2)}) %copy-start.1) | copy-done | bytes 106520
  15.8 1.1 %shard_map.69 = (f32[32,6,8,128]{3,2,1,0:T(8,128)}, f32[26,8,128]{2,1,0:T(8,128)S(1)}) custom-call(f32[768,256]{1,0:T(8,128)S(1)} %copy-done, f32[26,8,128]{2,1,0:T(8,128)S(1)} %copy-done.1), custom_call_target="tpu_custom_call" | custom-call | bytes 1572864 | tf_op jit(solution)/shard_map/pallas_call | solution.py:253
  17.0 0.0 collective-permute-done.2.refs_3_
  17.0 0.0 collective-permute-done.3.refs_4_
  17.0 0.9 %collective-permute-done.4.refs_5_ = f32[26,8,128]{2,1,0:T(8,128)S(1)} collective-permute-done((f32[26,8,128]{2,1,0:T(8,128)}, f32[26,8,128]{2,1,0:T(8,128)S(1)}, u32[]{:S(2)}, u32[]{:S(2)}) %collective-permute-start.4) | collective-permute-done | bytes 106528 | tf_op jit(solution)/shard_map/ppermute | solution.py:247
  17.9 1.2 %collective-permute-done.5.refs_6_ = f32[26,8,128]{2,1,0:T(8,128)S(1)} collective-permute-done((f32[26,8,128]{2,1,0:T(8,128)}, f32[26,8,128]{2,1,0:T(8,128)S(1)}, u32[]{:S(2)}, u32[]{:S(2)}) %collective-permute-start.5) | collective-permute-done | bytes 106528 | tf_op jit(solution)/shard_map/ppermute | solution.py:247
  19.1 0.0 collective-permute-done.6.refs_7_
  19.1 0.2 shard_map.70
  19.3 2.7 %collective-permute-start.7 = (f32[480,128]{1,0:T(8,128)S(1)}, f32[480,128]{1,0:T(8,128)S(1)}, u32[]{:S(2)}, u32[]{:S(2)}) collective-permute-start(f32[480,128]{1,0:T(8,128)S(1)} %get-tuple-element.33), channel_id=1, source_target_pairs={{0,64},{64,128},{128,192},{192,0},{1,65},{65,129},{129,193},{193,1... | collective-permute-start | bytes 737288 | tf_op jit(solution)/shard_map/ppermute | solution.py:243
  22.0 3.1 %collective-permute-start.9 = (f32[96,128]{1,0:T(8,128)S(1)}, f32[96,128]{1,0:T(8,128)S(1)}, u32[]{:S(2)}, u32[]{:S(2)}) collective-permute-start(f32[96,128]{1,0:T(8,128)S(1)} %get-tuple-element.34.refs_9_.refs_2_), channel_id=1, source_target_pairs={{0,192},{64,0},{128,64},{192,128},{1,193},{65,1},{129,65},{193,129... | collective-permute-start | bytes 147464 | tf_op jit(solution)/shard_map/ppermute | solution.py:243
  25.1 4.4 %collective-permute-start.8 = (f32[96,128]{1,0:T(8,128)S(1)}, f32[96,128]{1,0:T(8,128)S(1)}, u32[]{:S(2)}, u32[]{:S(2)}) collective-permute-start(f32[96,128]{1,0:T(8,128)S(1)} %get-tuple-element.34.refs_9_.refs_2_), channel_id=1, source_target_pairs={{0,128},{64,192},{128,0},{192,64},{1,129},{65,193},{129,1},{193,65... | collective-permute-start | bytes 147464 | tf_op jit(solution)/shard_map/ppermute | solution.py:243
  29.5 5.0 %all-to-all-start = ((f32[32,6,8,128]{3,2,1,0:T(8,128)}), f32[32,6,8,128]{3,2,1,0:T(8,128)S(1)}, u32[]{:S(2)}, u32[]{:S(2)}) async-start(f32[32,6,8,128]{3,2,1,0:T(8,128)} %get-tuple-element.43), calls=%async_computation | async-start | bytes 1572864 | tf_op jit(solution)/shard_map/all_to_all | solution.py:261
  34.6 0.0 collective-permute-done.9.refs_11_.refs_4_
  34.6 2.0 %collective-permute-done.8.refs_10_.refs_3_ = f32[96,128]{1,0:T(8,128)S(1)} collective-permute-done((f32[96,128]{1,0:T(8,128)S(1)}, f32[96,128]{1,0:T(8,128)S(1)}, u32[]{:S(2)}, u32[]{:S(2)}) %collective-permute-start.8) | collective-permute-done | bytes 49184 | tf_op jit(solution)/shard_map/ppermute | solution.py:243
  36.5 0.0 collective-permute-done.7.refs_8_.refs_1_
  36.5 8.4 %shard_map.71 = (f32[24,8,128]{2,1,0:T(8,128)S(1)}, f32[24,8,128]{2,1,0:T(8,128)S(1)}, f32[24,8,128]{2,1,0:T(8,128)S(1)}, f32[24,8,128]{2,1,0:T(8,128)S(1)}, f32...) custom-call(f32[26,8,128]{2,1,0:T(8,128)S(1)} %get-tuple-element.25.r, ...), custom_call_target="tpu_custom_call" | custom-call | flops 104689827840 | bytes 1572864 | tf_op jit(solution)/shard_map/pallas_call | solution.py:270
  45.0 2.5 %collective-permute-start.10 = (f32[24,8,128]{2,1,0:T(8,128)S(1)}, f32[24,8,128]{2,1,0:T(8,128)S(1)}, u32[]{:S(2)}, u32[]{:S(2)}) collective-permute-start(f32[24,8,128]{2,1,0:T(8,128)S(1)} %get-tuple-element.36), channel_id=1, source_target_pairs={{0,8},{8,0},{16,24},{24,16},{32,40},{40,32},{48,56},{56,48},{1,9},... | collective-permute-start | bytes 294920 | tf_op jit(solution)/shard_map/ppermute | solution.py:247
  47.5 1.7 %collective-permute-start.11 = (f32[24,8,128]{2,1,0:T(8,128)S(1)}, f32[24,8,128]{2,1,0:T(8,128)S(1)}, u32[]{:S(2)}, u32[]{:S(2)}) collective-permute-start(f32[24,8,128]{2,1,0:T(8,128)S(1)} %get-tuple-element.37), channel_id=1, source_target_pairs={{0,32},{8,40},{16,48},{24,56},{32,0},{40,8},{48,16},{56,24},{1,33}... | collective-permute-start | bytes 294920 | tf_op jit(solution)/shard_map/ppermute | solution.py:247
  49.2 0.1 collective-permute-start.12
  49.3 1.5 %collective-permute-start.13 = (f32[24,8,128]{2,1,0:T(8,128)S(1)}, f32[24,8,128]{2,1,0:T(8,128)S(1)}, u32[]{:S(2)}, u32[]{:S(2)}) collective-permute-start(f32[24,8,128]{2,1,0:T(8,128)S(1)} %get-tuple-element.39), channel_id=1, source_target_pairs={{0,48},{8,56},{16,32},{24,40},{32,16},{40,24},{48,0},{56,8},{1,49}... | collective-permute-start | bytes 294920 | tf_op jit(solution)/shard_map/ppermute | solution.py:247
  50.8 2.5 %collective-permute-start.14 = (f32[24,8,128]{2,1,0:T(8,128)S(1)}, f32[24,8,128]{2,1,0:T(8,128)S(1)}, u32[]{:S(2)}, u32[]{:S(2)}) collective-permute-start(f32[24,8,128]{2,1,0:T(8,128)S(1)} %get-tuple-element.40), channel_id=1, source_target_pairs={{0,40},{8,32},{16,56},{24,48},{32,8},{40,0},{48,24},{56,16},{1,41}... | collective-permute-start | bytes 294920 | tf_op jit(solution)/shard_map/ppermute | solution.py:247
  53.3 0.0 collective-permute-done.10.refs_1_
  53.3 0.0 collective-permute-start.15
  53.3 0.9 %collective-permute-done.11.refs_2_ = f32[24,8,128]{2,1,0:T(8,128)S(1)} collective-permute-done((f32[24,8,128]{2,1,0:T(8,128)S(1)}, f32[24,8,128]{2,1,0:T(8,128)S(1)}, u32[]{:S(2)}, u32[]{:S(2)}) %collective-permute-start.11) | collective-permute-done | bytes 98336 | tf_op jit(solution)/shard_map/ppermute | solution.py:247
  54.2 3.7 %collective-permute-start.16 = (f32[24,8,128]{2,1,0:T(8,128)S(1)}, f32[24,8,128]{2,1,0:T(8,128)S(1)}, u32[]{:S(2)}, u32[]{:S(2)}) collective-permute-start(f32[24,8,128]{2,1,0:T(8,128)S(1)} %get-tuple-element.42), channel_id=1, source_target_pairs={{0,56},{8,48},{16,40},{24,32},{32,24},{40,16},{48,8},{56,0},{1,57}... | collective-permute-start | bytes 294920 | tf_op jit(solution)/shard_map/ppermute | solution.py:247
  57.9 0.8 %all-to-all-done = f32[32,6,8,128]{3,2,1,0:T(8,128)S(1)} async-done(((f32[32,6,8,128]{3,2,1,0:T(8,128)}), f32[32,6,8,128]{3,2,1,0:T(8,128)S(1)}, u32[]{:S(2)}, u32[]{:S(2)}) %all-to-all-start) | async-done | bytes 786464 | tf_op jit(solution)/shard_map/all_to_all | solution.py:261
  58.6 4.4 %shard_map.72 = (f32[8,24576]{1,0:T(8,128)}, f32[8,128]{1,0:T(8,128)S(1)}) custom-call(f32[1536,128]{1,0:T(8,128)S(1)} %bitcast.3, f32[480,128]{1,0:T(8,128)S(1)} %collective-permute-done.7.refs_8_.refs_1_, f32[96,128]{1,0:T(8,128)S(1)} %get-tuple-element.34.refs_9_.refs_2_, f32[96,128]{1,0:T(8,128)S(1)} %collective-permute-done.8.refs_10_.refs_3_, ...), custom_call_target="tpu_custom_call" | custom-call | flops 2617245696 | bytes 2359296 | tf_op jit(solution)/shard_map/pallas_call | solution.py:273
  63.0 0.0 collective-permute-done.12.refs_3_
  63.0 0.0 collective-permute-done.13.refs_4_
  63.0 0.0 collective-permute-done.14.refs_5_
  63.0 0.0 collective-permute-done.15.refs_6_
  63.0 0.0 collective-permute-done.16.refs_7_
  63.0 1.2 %shard_map.73 = f32[768,256]{1,0:T(8,128)} custom-call(f32[24,8,128]{2,1,0:T(8,128)S(1)} %get-tuple-element.35.refs_0_, f32[24,8,128]{2,1,0:T(8,128)S(1)} %collective-permute-done.10.refs_1_, f32[24,8,128]{2,1,0:T(8,128)S(1)} %collective-permute-done.11.refs_2_, f32[24,8,128]{2,1,0:T(8,128)S(1)} %collective-permute-done.12.refs_3_, ...), custom_call_target="tpu_custom_call" | custom-call | bytes 1572864 | tf_op jit(solution)/shard_map/pallas_call | solution.py:276
Async XLA Ops:
  0.6 14.3 %copy-start = (f32[768,256]{1,0:T(8,128)S(1)}, f32[768,256]{1,0:T(8,128)}, u32[]{:S(2)}) copy-start(f32[768,256]{1,0:T(8,128)} %g_ref.1) | copy-start | bytes 2359300
  3.2 8.2 %collective-permute-start = (f32[26,8,128]{2,1,0:T(8,128)}, f32[26,8,128]{2,1,0:T(8,128)S(1)}, u32[]{:S(2)}, u32[]{:S(2)}) collective-permute-start(f32[26,8,128]{2,1,0:T(8,128)} %get-tuple-element.26), channel_id=1, source_target_pairs={{0,32},{8,40},{16,48},{24,56},{32,0},{40,8},{48,16},{56,24},{1,33}... | collective-permute-start | bytes 319496 | tf_op jit(solution)/shard_map/ppermute | solution.py:247
  6.9 7.8 %collective-permute-start.1 = (f32[26,8,128]{2,1,0:T(8,128)}, f32[26,8,128]{2,1,0:T(8,128)S(1)}, u32[]{:S(2)}, u32[]{:S(2)}) collective-permute-start(f32[26,8,128]{2,1,0:T(8,128)} %get-tuple-element.27), channel_id=1, source_target_pairs={{0,40},{8,32},{16,56},{24,48},{32,8},{40,0},{48,24},{56,16},{1,41}... | collective-permute-start | bytes 319496 | tf_op jit(solution)/shard_map/ppermute | solution.py:247
  9.5 7.4 %collective-permute-start.2 = (f32[26,8,128]{2,1,0:T(8,128)}, f32[26,8,128]{2,1,0:T(8,128)S(1)}, u32[]{:S(2)}, u32[]{:S(2)}) collective-permute-start(f32[26,8,128]{2,1,0:T(8,128)} %get-tuple-element.28), channel_id=1, source_target_pairs={{0,16},{8,24},{16,0},{24,8},{32,48},{40,56},{48,32},{56,40},{1,17}... | collective-permute-start | bytes 319496 | tf_op jit(solution)/shard_map/ppermute | solution.py:247
  9.5 7.4 %collective-permute-start.3 = (f32[26,8,128]{2,1,0:T(8,128)}, f32[26,8,128]{2,1,0:T(8,128)S(1)}, u32[]{:S(2)}, u32[]{:S(2)}) collective-permute-start(f32[26,8,128]{2,1,0:T(8,128)} %get-tuple-element.29), channel_id=1, source_target_pairs={{0,48},{8,56},{16,32},{24,40},{32,16},{40,24},{48,0},{56,8},{1,49}... | collective-permute-start | bytes 319496 | tf_op jit(solution)/shard_map/ppermute | solution.py:247
  11.0 6.9 %collective-permute-start.4 = (f32[26,8,128]{2,1,0:T(8,128)}, f32[26,8,128]{2,1,0:T(8,128)S(1)}, u32[]{:S(2)}, u32[]{:S(2)}) collective-permute-start(f32[26,8,128]{2,1,0:T(8,128)} %get-tuple-element.30), channel_id=1, source_target_pairs={{0,24},{8,16},{16,8},{24,0},{32,56},{40,48},{48,40},{56,32},{1,25}... | collective-permute-start | bytes 319496 | tf_op jit(solution)/shard_map/ppermute | solution.py:247
  11.4 7.7 %collective-permute-start.5 = (f32[26,8,128]{2,1,0:T(8,128)}, f32[26,8,128]{2,1,0:T(8,128)S(1)}, u32[]{:S(2)}, u32[]{:S(2)}) collective-permute-start(f32[26,8,128]{2,1,0:T(8,128)} %get-tuple-element.31), channel_id=1, source_target_pairs={{0,56},{8,48},{16,40},{24,32},{32,24},{40,16},{48,8},{56,0},{1,57}... | collective-permute-start | bytes 319496 | tf_op jit(solution)/shard_map/ppermute | solution.py:247
  14.7 4.4 %collective-permute-start.6 = (f32[26,8,128]{2,1,0:T(8,128)}, f32[26,8,128]{2,1,0:T(8,128)S(1)}, u32[]{:S(2)}, u32[]{:S(2)}) collective-permute-start(f32[26,8,128]{2,1,0:T(8,128)} %get-tuple-element.32), channel_id=1, source_target_pairs={{0,8},{8,0},{16,24},{24,16},{32,40},{40,32},{48,56},{56,48},{1,9},... | collective-permute-start | bytes 319496 | tf_op jit(solution)/shard_map/ppermute | solution.py:247
  14.9 0.9 %copy-start.1 = (f32[26,8,128]{2,1,0:T(8,128)S(1)}, f32[26,8,128]{2,1,0:T(8,128)}, u32[]{:S(2)}) copy-start(f32[26,8,128]{2,1,0:T(8,128)} %get-tuple-element.24.own_ref) | copy-start | bytes 319492
  19.3 17.2 %collective-permute-start.7 = (f32[480,128]{1,0:T(8,128)S(1)}, f32[480,128]{1,0:T(8,128)S(1)}, u32[]{:S(2)}, u32[]{:S(2)}) collective-permute-start(f32[480,128]{1,0:T(8,128)S(1)} %get-tuple-element.33), channel_id=1, source_target_pairs={{0,64},{64,128},{128,192},{192,0},{1,65},{65,129},{129,193},{193,1... | collective-permute-start | bytes 737288 | tf_op jit(solution)/shard_map/ppermute | solution.py:243
  22.0 12.5 %collective-permute-start.9 = (f32[96,128]{1,0:T(8,128)S(1)}, f32[96,128]{1,0:T(8,128)S(1)}, u32[]{:S(2)}, u32[]{:S(2)}) collective-permute-start(f32[96,128]{1,0:T(8,128)S(1)} %get-tuple-element.34.refs_9_.refs_2_), channel_id=1, source_target_pairs={{0,192},{64,0},{128,64},{192,128},{1,193},{65,1},{129,65},{193,129... | collective-permute-start | bytes 147464 | tf_op jit(solution)/shard_map/ppermute | solution.py:243
  25.1 11.4 %collective-permute-start.8 = (f32[96,128]{1,0:T(8,128)S(1)}, f32[96,128]{1,0:T(8,128)S(1)}, u32[]{:S(2)}, u32[]{:S(2)}) collective-permute-start(f32[96,128]{1,0:T(8,128)S(1)} %get-tuple-element.34.refs_9_.refs_2_), channel_id=1, source_target_pairs={{0,128},{64,192},{128,0},{192,64},{1,129},{65,193},{129,1},{193,65... | collective-permute-start | bytes 147464 | tf_op jit(solution)/shard_map/ppermute | solution.py:243
  29.5 29.1 %all-to-all-start = ((f32[32,6,8,128]{3,2,1,0:T(8,128)}), f32[32,6,8,128]{3,2,1,0:T(8,128)S(1)}, u32[]{:S(2)}, u32[]{:S(2)}) async-start(f32[32,6,8,128]{3,2,1,0:T(8,128)} %get-tuple-element.43), calls=%async_computation | async-start | bytes 1572864 | tf_op jit(solution)/shard_map/all_to_all | solution.py:261
  45.0 8.3 %collective-permute-start.10 = (f32[24,8,128]{2,1,0:T(8,128)S(1)}, f32[24,8,128]{2,1,0:T(8,128)S(1)}, u32[]{:S(2)}, u32[]{:S(2)}) collective-permute-start(f32[24,8,128]{2,1,0:T(8,128)S(1)} %get-tuple-element.36), channel_id=1, source_target_pairs={{0,8},{8,0},{16,24},{24,16},{32,40},{40,32},{48,56},{56,48},{1,9},... | collective-permute-start | bytes 294920 | tf_op jit(solution)/shard_map/ppermute | solution.py:247
  47.5 6.7 %collective-permute-start.11 = (f32[24,8,128]{2,1,0:T(8,128)S(1)}, f32[24,8,128]{2,1,0:T(8,128)S(1)}, u32[]{:S(2)}, u32[]{:S(2)}) collective-permute-start(f32[24,8,128]{2,1,0:T(8,128)S(1)} %get-tuple-element.37), channel_id=1, source_target_pairs={{0,32},{8,40},{16,48},{24,56},{32,0},{40,8},{48,16},{56,24},{1,33}... | collective-permute-start | bytes 294920 | tf_op jit(solution)/shard_map/ppermute | solution.py:247
  49.2 13.8 %collective-permute-start.12 = (f32[24,8,128]{2,1,0:T(8,128)S(1)}, f32[24,8,128]{2,1,0:T(8,128)S(1)}, u32[]{:S(2)}, u32[]{:S(2)}) collective-permute-start(f32[24,8,128]{2,1,0:T(8,128)S(1)} %get-tuple-element.38), channel_id=1, source_target_pairs={{0,16},{8,24},{16,0},{24,8},{32,48},{40,56},{48,32},{56,40},{1,17}... | collective-permute-start | bytes 294920 | tf_op jit(solution)/shard_map/ppermute | solution.py:247
  49.3 13.7 %collective-permute-start.13 = (f32[24,8,128]{2,1,0:T(8,128)S(1)}, f32[24,8,128]{2,1,0:T(8,128)S(1)}, u32[]{:S(2)}, u32[]{:S(2)}) collective-permute-start(f32[24,8,128]{2,1,0:T(8,128)S(1)} %get-tuple-element.39), channel_id=1, source_target_pairs={{0,48},{8,56},{16,32},{24,40},{32,16},{40,24},{48,0},{56,8},{1,49}... | collective-permute-start | bytes 294920 | tf_op jit(solution)/shard_map/ppermute | solution.py:247
  50.8 12.2 %collective-permute-start.14 = (f32[24,8,128]{2,1,0:T(8,128)S(1)}, f32[24,8,128]{2,1,0:T(8,128)S(1)}, u32[]{:S(2)}, u32[]{:S(2)}) collective-permute-start(f32[24,8,128]{2,1,0:T(8,128)S(1)} %get-tuple-element.40), channel_id=1, source_target_pairs={{0,40},{8,32},{16,56},{24,48},{32,8},{40,0},{48,24},{56,16},{1,41}... | collective-permute-start | bytes 294920 | tf_op jit(solution)/shard_map/ppermute | solution.py:247
  53.3 9.8 %collective-permute-start.15 = (f32[24,8,128]{2,1,0:T(8,128)S(1)}, f32[24,8,128]{2,1,0:T(8,128)S(1)}, u32[]{:S(2)}, u32[]{:S(2)}) collective-permute-start(f32[24,8,128]{2,1,0:T(8,128)S(1)} %get-tuple-element.41), channel_id=1, source_target_pairs={{0,24},{8,16},{16,8},{24,0},{32,56},{40,48},{48,40},{56,32},{1,25}... | collective-permute-start | bytes 294920 | tf_op jit(solution)/shard_map/ppermute | solution.py:247
  54.2 8.8 %collective-permute-start.16 = (f32[24,8,128]{2,1,0:T(8,128)S(1)}, f32[24,8,128]{2,1,0:T(8,128)S(1)}, u32[]{:S(2)}, u32[]{:S(2)}) collective-permute-start(f32[24,8,128]{2,1,0:T(8,128)S(1)} %get-tuple-element.42), channel_id=1, source_target_pairs={{0,56},{8,48},{16,40},{24,32},{32,24},{40,16},{48,8},{56,0},{1,57}... | collective-permute-start | bytes 294920 | tf_op jit(solution)/shard_map/ppermute | solution.py:247

commit v8 on v7

--- a/solution.py
+++ b/solution.py
@@ -9,7 +9,7 @@
 SUBS = 8
 NEAR = 8
 IN_ORDER = (0, 4, 5, 2, 6, 3, 7, 1)
-OUT_ORDER = (0, 1, 4, 2, 6, 5, 3, 7)
+OUT_ORDER = (0, 1, 2, 4, 6, 5, 3, 7)
 
 
 def pack_with_taps(x_ref, taps_ref, gain_ref, band_ref, *refs):

time: 65.3 us -> 65.7 us (level)
  waiting for transfers between devices: 6.26 us -> 8.5 us
  starting transfers between devices: 38.5 us -> 37.3 us
    all_to_all x1, waiting for transfers between devices: 0.77 us -> 2.93 us  [local(): lax.all_to_all(sent_g, ('far', 'near'), split_axis=0, concat_axis=0, tile...]
    ppermute x14, starting transfers between devices: 23.3 us -> 22.1 us  [swapped(): lax.ppermute(part, 'near', pairs[bits])]
  transfers between devices with their start and end apart: 18 -> 18, of which waited for: 6 -> 6; matrix products, arithmetic and copies ran while one was open for 0% -> 0% of each run, Pallas kernels for 22% -> 21%
where the time goes in v8:
time: 65.7 us; the launch traced here: 65.3 us
  starting transfers between devices  37.3 us (57%)
  Pallas kernels  17.9 us (27%)
  waiting for transfers between devices  8.5 us (13%)
  local copies, waits for them, and re-layouts  0.9 us (1%)
  between operations  0.7 us (1%)
    ppermute x14, starting transfers between devices, swapped(): lax.ppermute(part, 'near', pairs[bits])  22.1 us
    ppermute x3, starting transfers between devices, ahead(): lax.ppermute(value, 'far', [(z, (z + steps) % far) for z in range(far)])  10.2 us
    pallas_call x1, Pallas kernels, local(): call(lambda *refs: forward(halo_blocks, tiles, near, far, *refs), [share]...  8.42 us
    all_to_all x1, starting transfers between devices, local(): lax.all_to_all(sent_g, ('far', 'near'), split_axis=0, concat_axis=0, tile...  5.02 us
    pallas_call x1, Pallas kernels, local(): call(lambda *refs: gradient(count, tiles, halo_rows, *refs), [(SUBS, coun...  4.38 us
    ppermute x14, waiting for transfers between devices, swapped(): lax.ppermute(part, 'near', pairs[bits])  3.59 us
    all_to_all x1, waiting for transfers between devices, local(): lax.all_to_all(sent_g, ('far', 'near'), split_axis=0, concat_axis=0, tile...  2.93 us
    pallas_call x1, Pallas kernels, local(): call(pack_with_taps, [share] * near, [pltpu.VMEM((near, *share), jnp.floa...  2.51 us
  transfers between devices with their start and end apart: 18, of which 6 were waited for; matrix products, arithmetic and copies ran while one was open for 0% of the time, Pallas kernels for 21%

profile of v8, /device:TPU:1, one launch (start us, length us, event | category | flops | bytes accessed | tf_op | source)
XLA Modules:
  0.0 65.3 jit_solution(6166931244809780374)
XLA Ops:
  0.6 0.0 copy-start
  0.6 2.5 %shard_map.68 = (f32[26,8,128]{2,1,0:T(8,128)}, f32[26,8,128]{2,1,0:T(8,128)}, f32[26,8,128]{2,1,0:T(8,128)}, f32[26,8,128]{2,1,0:T(8,128)}, f32[26,8,128]{2,1,0...) custom-call(f32[768,256]{1,0:T(8,128)} %x_ref.1, f32[48,256]{1,0:T(8,128)} %taps_ref.1, ...), custom_call_target="tpu_custom_call" | custom-call | bytes 1572864 | tf_op jit(solution)/shard_map/pallas_call | solution.py:250
  3.2 3.7 %collective-permute-start = (f32[26,8,128]{2,1,0:T(8,128)}, f32[26,8,128]{2,1,0:T(8,128)S(1)}, u32[]{:S(2)}, u32[]{:S(2)}) collective-permute-start(f32[26,8,128]{2,1,0:T(8,128)} %get-tuple-element.26), channel_id=1, source_target_pairs={{0,32},{8,40},{16,48},{24,56},{32,0},{40,8},{48,16},{56,24},{1,33}... | collective-permute-start | bytes 319496 | tf_op jit(solution)/shard_map/ppermute | solution.py:247
  6.9 2.6 %collective-permute-start.1 = (f32[26,8,128]{2,1,0:T(8,128)}, f32[26,8,128]{2,1,0:T(8,128)S(1)}, u32[]{:S(2)}, u32[]{:S(2)}) collective-permute-start(f32[26,8,128]{2,1,0:T(8,128)} %get-tuple-element.27), channel_id=1, source_target_pairs={{0,40},{8,32},{16,56},{24,48},{32,8},{40,0},{48,24},{56,16},{1,41}... | collective-permute-start | bytes 319496 | tf_op jit(solution)/shard_map/ppermute | solution.py:247
  9.5 0.0 collective-permute-start.2
  9.5 1.5 %collective-permute-start.3 = (f32[26,8,128]{2,1,0:T(8,128)}, f32[26,8,128]{2,1,0:T(8,128)S(1)}, u32[]{:S(2)}, u32[]{:S(2)}) collective-permute-start(f32[26,8,128]{2,1,0:T(8,128)} %get-tuple-element.29), channel_id=1, source_target_pairs={{0,48},{8,56},{16,32},{24,40},{32,16},{40,24},{48,0},{56,8},{1,49}... | collective-permute-start | bytes 319496 | tf_op jit(solution)/shard_map/ppermute | solution.py:247
  11.0 0.4 collective-permute-start.4
  11.4 0.0 collective-permute-done.refs_1_
  11.4 2.8 %collective-permute-start.5 = (f32[26,8,128]{2,1,0:T(8,128)}, f32[26,8,128]{2,1,0:T(8,128)S(1)}, u32[]{:S(2)}, u32[]{:S(2)}) collective-permute-start(f32[26,8,128]{2,1,0:T(8,128)} %get-tuple-element.31), channel_id=1, source_target_pairs={{0,56},{8,48},{16,40},{24,32},{32,24},{40,16},{48,8},{56,0},{1,57}... | collective-permute-start | bytes 319496 | tf_op jit(solution)/shard_map/ppermute | solution.py:247
  14.2 0.4 collective-permute-done.1.refs_2_
  14.7 0.2 collective-permute-start.6
  14.9 0.0 copy-done
  14.9 0.0 copy-start.1
  14.9 0.9 %copy-done.1 = f32[26,8,128]{2,1,0:T(8,128)S(1)} copy-done((f32[26,8,128]{2,1,0:T(8,128)S(1)}, f32[26,8,128]{2,1,0:T(8,128)}, u32[]{:S(2)}) %copy-start.1) | copy-done | bytes 106520
  15.8 1.1 %shard_map.69 = (f32[32,6,8,128]{3,2,1,0:T(8,128)}, f32[26,8,128]{2,1,0:T(8,128)S(1)}) custom-call(f32[768,256]{1,0:T(8,128)S(1)} %copy-done, f32[26,8,128]{2,1,0:T(8,128)S(1)} %copy-done.1), custom_call_target="tpu_custom_call" | custom-call | bytes 1572864 | tf_op jit(solution)/shard_map/pallas_call | solution.py:253
  17.0 0.0 collective-permute-done.2.refs_3_
  17.0 0.0 collective-permute-done.3.refs_4_
  17.0 0.9 %collective-permute-done.4.refs_5_ = f32[26,8,128]{2,1,0:T(8,128)S(1)} collective-permute-done((f32[26,8,128]{2,1,0:T(8,128)}, f32[26,8,128]{2,1,0:T(8,128)S(1)}, u32[]{:S(2)}, u32[]{:S(2)}) %collective-permute-start.4) | collective-permute-done | bytes 106528 | tf_op jit(solution)/shard_map/ppermute | solution.py:247
  17.9 1.2 %collective-permute-done.5.refs_6_ = f32[26,8,128]{2,1,0:T(8,128)S(1)} collective-permute-done((f32[26,8,128]{2,1,0:T(8,128)}, f32[26,8,128]{2,1,0:T(8,128)S(1)}, u32[]{:S(2)}, u32[]{:S(2)}) %collective-permute-start.5) | collective-permute-done | bytes 106528 | tf_op jit(solution)/shard_map/ppermute | solution.py:247
  19.1 0.0 collective-permute-done.6.refs_7_
  19.1 0.2 shard_map.70
  19.3 2.7 %collective-permute-start.7 = (f32[480,128]{1,0:T(8,128)S(1)}, f32[480,128]{1,0:T(8,128)S(1)}, u32[]{:S(2)}, u32[]{:S(2)}) collective-permute-start(f32[480,128]{1,0:T(8,128)S(1)} %get-tuple-element.33), channel_id=1, source_target_pairs={{0,64},{64,128},{128,192},{192,0},{1,65},{65,129},{129,193},{193,1... | collective-permute-start | bytes 737288 | tf_op jit(solution)/shard_map/ppermute | solution.py:243
  22.0 3.1 %collective-permute-start.9 = (f32[96,128]{1,0:T(8,128)S(1)}, f32[96,128]{1,0:T(8,128)S(1)}, u32[]{:S(2)}, u32[]{:S(2)}) collective-permute-start(f32[96,128]{1,0:T(8,128)S(1)} %get-tuple-element.34.refs_9_.refs_2_), channel_id=1, source_target_pairs={{0,192},{64,0},{128,64},{192,128},{1,193},{65,1},{129,65},{193,129... | collective-permute-start | bytes 147464 | tf_op jit(solution)/shard_map/ppermute | solution.py:243
  25.1 4.4 %collective-permute-start.8 = (f32[96,128]{1,0:T(8,128)S(1)}, f32[96,128]{1,0:T(8,128)S(1)}, u32[]{:S(2)}, u32[]{:S(2)}) collective-permute-start(f32[96,128]{1,0:T(8,128)S(1)} %get-tuple-element.34.refs_9_.refs_2_), channel_id=1, source_target_pairs={{0,128},{64,192},{128,0},{192,64},{1,129},{65,193},{129,1},{193,65... | collective-permute-start | bytes 147464 | tf_op jit(solution)/shard_map/ppermute | solution.py:243
  29.5 5.0 %all-to-all-start = ((f32[32,6,8,128]{3,2,1,0:T(8,128)}), f32[32,6,8,128]{3,2,1,0:T(8,128)S(1)}, u32[]{:S(2)}, u32[]{:S(2)}) async-start(f32[32,6,8,128]{3,2,1,0:T(8,128)} %get-tuple-element.43), calls=%async_computation | async-start | bytes 1572864 | tf_op jit(solution)/shard_map/all_to_all | solution.py:261
  34.6 0.0 collective-permute-done.9.refs_11_.refs_4_
  34.6 2.0 %collective-permute-done.8.refs_10_.refs_3_ = f32[96,128]{1,0:T(8,128)S(1)} collective-permute-done((f32[96,128]{1,0:T(8,128)S(1)}, f32[96,128]{1,0:T(8,128)S(1)}, u32[]{:S(2)}, u32[]{:S(2)}) %collective-permute-start.8) | collective-permute-done | bytes 49184 | tf_op jit(solution)/shard_map/ppermute | solution.py:243
  36.5 0.0 collective-permute-done.7.refs_8_.refs_1_
  36.5 8.4 %shard_map.71 = (f32[24,8,128]{2,1,0:T(8,128)S(1)}, f32[24,8,128]{2,1,0:T(8,128)S(1)}, f32[24,8,128]{2,1,0:T(8,128)S(1)}, f32[24,8,128]{2,1,0:T(8,128)S(1)}, f32...) custom-call(f32[26,8,128]{2,1,0:T(8,128)S(1)} %get-tuple-element.25.r, ...), custom_call_target="tpu_custom_call" | custom-call | flops 104689827840 | bytes 1572864 | tf_op jit(solution)/shard_map/pallas_call | solution.py:270
  45.0 2.5 %collective-permute-start.10 = (f32[24,8,128]{2,1,0:T(8,128)S(1)}, f32[24,8,128]{2,1,0:T(8,128)S(1)}, u32[]{:S(2)}, u32[]{:S(2)}) collective-permute-start(f32[24,8,128]{2,1,0:T(8,128)S(1)} %get-tuple-element.36), channel_id=1, source_target_pairs={{0,8},{8,0},{16,24},{24,16},{32,40},{40,32},{48,56},{56,48},{1,9},... | collective-permute-start | bytes 294920 | tf_op jit(solution)/shard_map/ppermute | solution.py:247
  47.5 0.4 collective-permute-start.11
  47.9 2.0 %collective-permute-start.12 = (f32[24,8,128]{2,1,0:T(8,128)S(1)}, f32[24,8,128]{2,1,0:T(8,128)S(1)}, u32[]{:S(2)}, u32[]{:S(2)}) collective-permute-start(f32[24,8,128]{2,1,0:T(8,128)S(1)} %get-tuple-element.38), channel_id=1, source_target_pairs={{0,32},{8,40},{16,48},{24,56},{32,0},{40,8},{48,16},{56,24},{1,33}... | collective-permute-start | bytes 294920 | tf_op jit(solution)/shard_map/ppermute | solution.py:247
  49.9 1.5 %collective-permute-start.13 = (f32[24,8,128]{2,1,0:T(8,128)S(1)}, f32[24,8,128]{2,1,0:T(8,128)S(1)}, u32[]{:S(2)}, u32[]{:S(2)}) collective-permute-start(f32[24,8,128]{2,1,0:T(8,128)S(1)} %get-tuple-element.39), channel_id=1, source_target_pairs={{0,48},{8,56},{16,32},{24,40},{32,16},{40,24},{48,0},{56,8},{1,49}... | collective-permute-start | bytes 294920 | tf_op jit(solution)/shard_map/ppermute | solution.py:247
  51.4 1.3 %collective-permute-start.14 = (f32[24,8,128]{2,1,0:T(8,128)S(1)}, f32[24,8,128]{2,1,0:T(8,128)S(1)}, u32[]{:S(2)}, u32[]{:S(2)}) collective-permute-start(f32[24,8,128]{2,1,0:T(8,128)S(1)} %get-tuple-element.40), channel_id=1, source_target_pairs={{0,40},{8,32},{16,56},{24,48},{32,8},{40,0},{48,24},{56,16},{1,41}... | collective-permute-start | bytes 294920 | tf_op jit(solution)/shard_map/ppermute | solution.py:247
  52.7 0.0 collective-permute-done.10.refs_1_
  52.7 0.8 %collective-permute-start.15 = (f32[24,8,128]{2,1,0:T(8,128)S(1)}, f32[24,8,128]{2,1,0:T(8,128)S(1)}, u32[]{:S(2)}, u32[]{:S(2)}) collective-permute-start(f32[24,8,128]{2,1,0:T(8,128)S(1)} %get-tuple-element.41), channel_id=1, source_target_pairs={{0,24},{8,16},{16,8},{24,0},{32,56},{40,48},{48,40},{56,32},{1,25}... | collective-permute-start | bytes 294920 | tf_op jit(solution)/shard_map/ppermute | solution.py:247
  53.5 0.0 collective-permute-done.11.refs_2_
  53.5 2.3 %collective-permute-start.16 = (f32[24,8,128]{2,1,0:T(8,128)S(1)}, f32[24,8,128]{2,1,0:T(8,128)S(1)}, u32[]{:S(2)}, u32[]{:S(2)}) collective-permute-start(f32[24,8,128]{2,1,0:T(8,128)S(1)} %get-tuple-element.42), channel_id=1, source_target_pairs={{0,56},{8,48},{16,40},{24,32},{32,24},{40,16},{48,8},{56,0},{1,57}... | collective-permute-start | bytes 294920 | tf_op jit(solution)/shard_map/ppermute | solution.py:247
  55.7 2.9 %all-to-all-done = f32[32,6,8,128]{3,2,1,0:T(8,128)S(1)} async-done(((f32[32,6,8,128]{3,2,1,0:T(8,128)}), f32[32,6,8,128]{3,2,1,0:T(8,128)S(1)}, u32[]{:S(2)}, u32[]{:S(2)}) %all-to-all-start) | async-done | bytes 786464 | tf_op jit(solution)/shard_map/all_to_all | solution.py:261
  58.7 4.4 %shard_map.72 = (f32[8,24576]{1,0:T(8,128)}, f32[8,128]{1,0:T(8,128)S(1)}) custom-call(f32[1536,128]{1,0:T(8,128)S(1)} %bitcast.3, f32[480,128]{1,0:T(8,128)S(1)} %collective-permute-done.7.refs_8_.refs_1_, f32[96,128]{1,0:T(8,128)S(1)} %get-tuple-element.34.refs_9_.refs_2_, f32[96,128]{1,0:T(8,128)S(1)} %collective-permute-done.8.refs_10_.refs_3_, ...), custom_call_target="tpu_custom_call" | custom-call | flops 2617245696 | bytes 2359296 | tf_op jit(solution)/shard_map/pallas_call | solution.py:273
  63.1 0.0 collective-permute-done.12.refs_3_
  63.1 0.0 collective-permute-done.13.refs_4_
  63.1 0.0 collective-permute-done.14.refs_5_
  63.1 0.0 collective-permute-done.15.refs_6_
  63.1 1.0 %collective-permute-done.16.refs_7_ = f32[24,8,128]{2,1,0:T(8,128)S(1)} collective-permute-done((f32[24,8,128]{2,1,0:T(8,128)S(1)}, f32[24,8,128]{2,1,0:T(8,128)S(1)}, u32[]{:S(2)}, u32[]{:S(2)}) %collective-permute-start.16) | collective-permute-done | bytes 98336 | tf_op jit(solution)/shard_map/ppermute | solution.py:247
  64.1 1.2 %shard_map.73 = f32[768,256]{1,0:T(8,128)} custom-call(f32[24,8,128]{2,1,0:T(8,128)S(1)} %get-tuple-element.35.refs_0_, f32[24,8,128]{2,1,0:T(8,128)S(1)} %collective-permute-done.10.refs_1_, f32[24,8,128]{2,1,0:T(8,128)S(1)} %collective-permute-done.11.refs_2_, f32[24,8,128]{2,1,0:T(8,128)S(1)} %collective-permute-done.12.refs_3_, ...), custom_call_target="tpu_custom_call" | custom-call | bytes 1572864 | tf_op jit(solution)/shard_map/pallas_call | solution.py:276
Async XLA Ops:
  0.6 14.3 %copy-start = (f32[768,256]{1,0:T(8,128)S(1)}, f32[768,256]{1,0:T(8,128)}, u32[]{:S(2)}) copy-start(f32[768,256]{1,0:T(8,128)} %g_ref.1) | copy-start | bytes 2359300
  3.2 8.2 %collective-permute-start = (f32[26,8,128]{2,1,0:T(8,128)}, f32[26,8,128]{2,1,0:T(8,128)S(1)}, u32[]{:S(2)}, u32[]{:S(2)}) collective-permute-start(f32[26,8,128]{2,1,0:T(8,128)} %get-tuple-element.26), channel_id=1, source_target_pairs={{0,32},{8,40},{16,48},{24,56},{32,0},{40,8},{48,16},{56,24},{1,33}... | collective-permute-start | bytes 319496 | tf_op jit(solution)/shard_map/ppermute | solution.py:247
  6.9 7.8 %collective-permute-start.1 = (f32[26,8,128]{2,1,0:T(8,128)}, f32[26,8,128]{2,1,0:T(8,128)S(1)}, u32[]{:S(2)}, u32[]{:S(2)}) collective-permute-start(f32[26,8,128]{2,1,0:T(8,128)} %get-tuple-element.27), channel_id=1, source_target_pairs={{0,40},{8,32},{16,56},{24,48},{32,8},{40,0},{48,24},{56,16},{1,41}... | collective-permute-start | bytes 319496 | tf_op jit(solution)/shard_map/ppermute | solution.py:247
  9.5 7.4 %collective-permute-start.2 = (f32[26,8,128]{2,1,0:T(8,128)}, f32[26,8,128]{2,1,0:T(8,128)S(1)}, u32[]{:S(2)}, u32[]{:S(2)}) collective-permute-start(f32[26,8,128]{2,1,0:T(8,128)} %get-tuple-element.28), channel_id=1, source_target_pairs={{0,16},{8,24},{16,0},{24,8},{32,48},{40,56},{48,32},{56,40},{1,17}... | collective-permute-start | bytes 319496 | tf_op jit(solution)/shard_map/ppermute | solution.py:247
  9.5 7.4 %collective-permute-start.3 = (f32[26,8,128]{2,1,0:T(8,128)}, f32[26,8,128]{2,1,0:T(8,128)S(1)}, u32[]{:S(2)}, u32[]{:S(2)}) collective-permute-start(f32[26,8,128]{2,1,0:T(8,128)} %get-tuple-element.29), channel_id=1, source_target_pairs={{0,48},{8,56},{16,32},{24,40},{32,16},{40,24},{48,0},{56,8},{1,49}... | collective-permute-start | bytes 319496 | tf_op jit(solution)/shard_map/ppermute | solution.py:247
  11.0 6.9 %collective-permute-start.4 = (f32[26,8,128]{2,1,0:T(8,128)}, f32[26,8,128]{2,1,0:T(8,128)S(1)}, u32[]{:S(2)}, u32[]{:S(2)}) collective-permute-start(f32[26,8,128]{2,1,0:T(8,128)} %get-tuple-element.30), channel_id=1, source_target_pairs={{0,24},{8,16},{16,8},{24,0},{32,56},{40,48},{48,40},{56,32},{1,25}... | collective-permute-start | bytes 319496 | tf_op jit(solution)/shard_map/ppermute | solution.py:247
  11.4 7.7 %collective-permute-start.5 = (f32[26,8,128]{2,1,0:T(8,128)}, f32[26,8,128]{2,1,0:T(8,128)S(1)}, u32[]{:S(2)}, u32[]{:S(2)}) collective-permute-start(f32[26,8,128]{2,1,0:T(8,128)} %get-tuple-element.31), channel_id=1, source_target_pairs={{0,56},{8,48},{16,40},{24,32},{32,24},{40,16},{48,8},{56,0},{1,57}... | collective-permute-start | bytes 319496 | tf_op jit(solution)/shard_map/ppermute | solution.py:247
  14.7 4.4 %collective-permute-start.6 = (f32[26,8,128]{2,1,0:T(8,128)}, f32[26,8,128]{2,1,0:T(8,128)S(1)}, u32[]{:S(2)}, u32[]{:S(2)}) collective-permute-start(f32[26,8,128]{2,1,0:T(8,128)} %get-tuple-element.32), channel_id=1, source_target_pairs={{0,8},{8,0},{16,24},{24,16},{32,40},{40,32},{48,56},{56,48},{1,9},... | collective-permute-start | bytes 319496 | tf_op jit(solution)/shard_map/ppermute | solution.py:247
  14.9 0.9 %copy-start.1 = (f32[26,8,128]{2,1,0:T(8,128)S(1)}, f32[26,8,128]{2,1,0:T(8,128)}, u32[]{:S(2)}) copy-start(f32[26,8,128]{2,1,0:T(8,128)} %get-tuple-element.24.own_ref) | copy-start | bytes 319492
  19.3 17.2 %collective-permute-start.7 = (f32[480,128]{1,0:T(8,128)S(1)}, f32[480,128]{1,0:T(8,128)S(1)}, u32[]{:S(2)}, u32[]{:S(2)}) collective-permute-start(f32[480,128]{1,0:T(8,128)S(1)} %get-tuple-element.33), channel_id=1, source_target_pairs={{0,64},{64,128},{128,192},{192,0},{1,65},{65,129},{129,193},{193,1... | collective-permute-start | bytes 737288 | tf_op jit(solution)/shard_map/ppermute | solution.py:243
  22.0 12.5 %collective-permute-start.9 = (f32[96,128]{1,0:T(8,128)S(1)}, f32[96,128]{1,0:T(8,128)S(1)}, u32[]{:S(2)}, u32[]{:S(2)}) collective-permute-start(f32[96,128]{1,0:T(8,128)S(1)} %get-tuple-element.34.refs_9_.refs_2_), channel_id=1, source_target_pairs={{0,192},{64,0},{128,64},{192,128},{1,193},{65,1},{129,65},{193,129... | collective-permute-start | bytes 147464 | tf_op jit(solution)/shard_map/ppermute | solution.py:243
  25.1 11.4 %collective-permute-start.8 = (f32[96,128]{1,0:T(8,128)S(1)}, f32[96,128]{1,0:T(8,128)S(1)}, u32[]{:S(2)}, u32[]{:S(2)}) collective-permute-start(f32[96,128]{1,0:T(8,128)S(1)} %get-tuple-element.34.refs_9_.refs_2_), channel_id=1, source_target_pairs={{0,128},{64,192},{128,0},{192,64},{1,129},{65,193},{129,1},{193,65... | collective-permute-start | bytes 147464 | tf_op jit(solution)/shard_map/ppermute | solution.py:243
  29.5 29.1 %all-to-all-start = ((f32[32,6,8,128]{3,2,1,0:T(8,128)}), f32[32,6,8,128]{3,2,1,0:T(8,128)S(1)}, u32[]{:S(2)}, u32[]{:S(2)}) async-start(f32[32,6,8,128]{3,2,1,0:T(8,128)} %get-tuple-element.43), calls=%async_computation | async-start | bytes 1572864 | tf_op jit(solution)/shard_map/all_to_all | solution.py:261
  45.0 7.7 %collective-permute-start.10 = (f32[24,8,128]{2,1,0:T(8,128)S(1)}, f32[24,8,128]{2,1,0:T(8,128)S(1)}, u32[]{:S(2)}, u32[]{:S(2)}) collective-permute-start(f32[24,8,128]{2,1,0:T(8,128)S(1)} %get-tuple-element.36), channel_id=1, source_target_pairs={{0,8},{8,0},{16,24},{24,16},{32,40},{40,32},{48,56},{56,48},{1,9},... | collective-permute-start | bytes 294920 | tf_op jit(solution)/shard_map/ppermute | solution.py:247
  47.5 5.9 %collective-permute-start.11 = (f32[24,8,128]{2,1,0:T(8,128)S(1)}, f32[24,8,128]{2,1,0:T(8,128)S(1)}, u32[]{:S(2)}, u32[]{:S(2)}) collective-permute-start(f32[24,8,128]{2,1,0:T(8,128)S(1)} %get-tuple-element.37), channel_id=1, source_target_pairs={{0,16},{8,24},{16,0},{24,8},{32,48},{40,56},{48,32},{56,40},{1,17}... | collective-permute-start | bytes 294920 | tf_op jit(solution)/shard_map/ppermute | solution.py:247
  47.9 15.1 %collective-permute-start.12 = (f32[24,8,128]{2,1,0:T(8,128)S(1)}, f32[24,8,128]{2,1,0:T(8,128)S(1)}, u32[]{:S(2)}, u32[]{:S(2)}) collective-permute-start(f32[24,8,128]{2,1,0:T(8,128)S(1)} %get-tuple-element.38), channel_id=1, source_target_pairs={{0,32},{8,40},{16,48},{24,56},{32,0},{40,8},{48,16},{56,24},{1,33}... | collective-permute-start | bytes 294920 | tf_op jit(solution)/shard_map/ppermute | solution.py:247
  49.9 13.1 %collective-permute-start.13 = (f32[24,8,128]{2,1,0:T(8,128)S(1)}, f32[24,8,128]{2,1,0:T(8,128)S(1)}, u32[]{:S(2)}, u32[]{:S(2)}) collective-permute-start(f32[24,8,128]{2,1,0:T(8,128)S(1)} %get-tuple-element.39), channel_id=1, source_target_pairs={{0,48},{8,56},{16,32},{24,40},{32,16},{40,24},{48,0},{56,8},{1,49}... | collective-permute-start | bytes 294920 | tf_op jit(solution)/shard_map/ppermute | solution.py:247
  51.4 11.7 %collective-permute-start.14 = (f32[24,8,128]{2,1,0:T(8,128)S(1)}, f32[24,8,128]{2,1,0:T(8,128)S(1)}, u32[]{:S(2)}, u32[]{:S(2)}) collective-permute-start(f32[24,8,128]{2,1,0:T(8,128)S(1)} %get-tuple-element.40), channel_id=1, source_target_pairs={{0,40},{8,32},{16,56},{24,48},{32,8},{40,0},{48,24},{56,16},{1,41}... | collective-permute-start | bytes 294920 | tf_op jit(solution)/shard_map/ppermute | solution.py:247
  52.7 10.4 %collective-permute-start.15 = (f32[24,8,128]{2,1,0:T(8,128)S(1)}, f32[24,8,128]{2,1,0:T(8,128)S(1)}, u32[]{:S(2)}, u32[]{:S(2)}) collective-permute-start(f32[24,8,128]{2,1,0:T(8,128)S(1)} %get-tuple-element.41), channel_id=1, source_target_pairs={{0,24},{8,16},{16,8},{24,0},{32,56},{40,48},{48,40},{56,32},{1,25}... | collective-permute-start | bytes 294920 | tf_op jit(solution)/shard_map/ppermute | solution.py:247
  53.5 10.6 %collective-permute-start.16 = (f32[24,8,128]{2,1,0:T(8,128)S(1)}, f32[24,8,128]{2,1,0:T(8,128)S(1)}, u32[]{:S(2)}, u32[]{:S(2)}) collective-permute-start(f32[24,8,128]{2,1,0:T(8,128)S(1)} %get-tuple-element.42), channel_id=1, source_target_pairs={{0,56},{8,48},{16,40},{24,32},{32,24},{40,16},{48,8},{56,0},{1,57}... | collective-permute-start | bytes 294920 | tf_op jit(solution)/shard_map/ppermute | solution.py:247
